TPU v7x, 256 devices: a whole 4x4x8 slice. The times are simulated.
256 devices in a mesh: dur: 32 (over y, z), inc: 8 (over x, core).
Axes of the slice: x: 4, y: 4, z: 8, core: 2. Of those that a mesh axis runs over, the one named last changes fastest.
Arguments:
- value_next: float32 [32, 128, 512], P('dur', 'inc'), may hold values from 0.5 to 2
- markov: float32 [128, 128], replicated, may hold values from 0 to 1, as said below
- energy_share: float32 [32, 128, 512], P('dur', 'inc'), may hold values from 0.1 to 0.5
- bwd_bracket: int32 [2, 32, 128, 512], P(None, 'dur', 'inc'), may hold values from 0 to 510
- bwd_weight: float32 [2, 32, 128, 512], P(None, 'dur', 'inc'), may hold values from 0 to 1
- fwd_bracket: int32 [2, 32, 128, 512], P(None, 'dur', 'inc'), may hold values from 0 to 510
- fwd_weight: float32 [2, 32, 128, 512], P(None, 'dur', 'inc'), may hold values from 0 to 1
- dur_step: int32 [2, 32, 128, 512], P(None, 'dur', 'inc'), may hold values from -1 to 0
- dur_weight: float32 [2, 32, 128, 512], P(None, 'dur', 'inc'), may hold values from 0 to 1
- mass_start: float32 [32, 128, 512], P('dur', 'inc'), may hold values from 0.5 to 1.5
- tax: float32 [2], replicated, may hold values from 0 to 0.5
Outputs:
- value_start: float32 [32, 128, 512], P('dur', 'inc')
- mass_end: float32 [32, 128, 512], P('dur', 'inc')
- demand: float32 [2], replicated
Inputs may be any that keep to these rules, and one draw needn't show every extreme that they name: `markov`: entries are positive, each row sums to about one with 0.6 on the diagonal.
All inputs are finite; a program needn't handle non-finite values.
Results may differ from a plain program's by a relative error of at most 0.0001.
Values sent between devices are 32-bit elements; how exact they have to be, the bound alone decides.
No kernel may reach another device: no remote copies, remote signals or barrier semaphores. Data moves between devices by JAX's collectives and lax.ppermute only.
A program may use at most 64 MiB of HBM per device.

v0:
```python
import jax
import jax.numpy as jnp
from jax import lax
from jax.sharding import PartitionSpec as P

discount = 0.985
gross_rate = 1.01
adjust_share = 0.3


def with_halo(block, sides, width):
    for axis, dim in sides:
        count = lax.axis_size(axis)
        forward = [(i, i + 1) for i in range(count - 1)]
        backward = [(target, source) for source, target in forward]
        low = lax.ppermute(
            lax.slice_in_dim(block, block.shape[dim] - width, None, axis=dim), axis, forward
        )
        high = lax.ppermute(lax.slice_in_dim(block, 0, width, axis=dim), axis, backward)
        block = jnp.concatenate([low, block, high], axis=dim)
    return block


def markov_apply(field, matrix):
    groups = field.shape[1]
    own_rows = lax.dynamic_slice_in_dim(matrix, lax.axis_index("inc") * groups, groups, 0)
    return jnp.einsum(
        "ij,dja->dia",
        own_rows,
        lax.all_gather(field, "inc", axis=1, tiled=True),
        precision=lax.Precision.HIGHEST,
    )


def smooth_levels(expect):
    padded = with_halo(expect, (("dur", 0),), 1)
    dur_pos = lax.axis_index("dur")
    low_edge = jnp.where(dur_pos == 0, expect, padded[:1])
    high_edge = jnp.where(dur_pos == lax.axis_size("dur") - 1, expect, padded[-1:])
    lower_side = jnp.concatenate([low_edge, expect[:-1]], 0)
    upper_side = jnp.concatenate([expect[1:], high_edge], 0)
    return (1.0 - adjust_share) * expect + adjust_share * 0.5 * (lower_side + upper_side)


def bracket_read(mixed, bracket, weight):
    asset_count = mixed.shape[2]
    both_index = jnp.concatenate([bracket, bracket + 1], 2)
    both_values = jnp.take_along_axis(mixed, both_index, axis=2)
    return (1.0 - weight) * both_values[:, :, :asset_count] + weight * both_values[
        :, :, asset_count:
    ]


def push_assets(density, bracket, weight):
    asset_count = density.shape[2]
    flat_rows = density.shape[0] * density.shape[1]
    row_base = (jnp.arange(flat_rows, dtype=jnp.int32) * asset_count)[:, None]
    position = (bracket.reshape(flat_rows, asset_count) + row_base).reshape(-1)
    both_position = jnp.concatenate([position, position + 1], 0)
    both_values = jnp.concatenate(
        [((1.0 - weight) * density).reshape(-1), (weight * density).reshape(-1)], 0
    )
    moved = jnp.zeros((flat_rows * asset_count,), jnp.float32).at[both_position].add(both_values)
    return moved.reshape(density.shape)


def push_levels(moved, step_offset, omega, level_index, total_levels):
    lower_level = jnp.clip(level_index + step_offset, 0, total_levels - 2)
    down_flag = (lower_level - level_index == -1).astype(jnp.float32)
    stay_flag = 1.0 - down_flag
    to_minus = moved * (1.0 - omega) * down_flag
    to_self = moved * ((1.0 - omega) * stay_flag + omega * down_flag)
    to_plus = moved * omega * stay_flag
    padded = with_halo(jnp.stack([to_minus, to_plus]), (("dur", 1),), 1)
    return to_self + padded[1, :-2] + padded[0, 2:]


def per_device(
    value_next,
    markov,
    energy_share,
    bwd_bracket,
    bwd_weight,
    fwd_bracket,
    fwd_weight,
    dur_step,
    dur_weight,
    mass_start,
    tax,
):
    levels = value_next.shape[0]
    total_levels = levels * lax.axis_size("dur")
    scale = 1.0 / (total_levels * markov.shape[0] * value_next.shape[2])
    level_index = (
        lax.axis_index("dur") * levels + jnp.arange(levels, dtype=jnp.int32)[:, None, None]
    )
    marginal = value_next
    energies = [None, None]
    for quarter in (1, 0):
        expect = discount * markov_apply(marginal, markov)
        mixed = smooth_levels(expect)
        interp = bracket_read(mixed, bwd_bracket[quarter], bwd_weight[quarter])
        energies[quarter] = energy_share * lax.rsqrt(interp) / (1.0 + tax[quarter])
        marginal = gross_rate * interp * (1.0 + tax[quarter] * energy_share)
    transposed = markov.T
    density = mass_start
    partial_terms = []
    for quarter in (0, 1):
        local_demand = jnp.sum(density * energies[quarter]) * scale
        partial_terms.append(lax.psum(local_demand, ("dur", "inc")))
        moved = push_assets(density, fwd_bracket[quarter], fwd_weight[quarter])
        levels_moved = push_levels(
            moved, dur_step[quarter], dur_weight[quarter], level_index, total_levels
        )
        density = markov_apply(levels_moved, transposed)
    demand = jnp.stack(partial_terms)
    return (marginal, density, demand)


def solution(mesh):
    return jax.shard_map(
        per_device,
        mesh=mesh,
        in_specs=(
            P("dur", "inc", None),
            P(),
            P("dur", "inc", None),
            P(None, "dur", "inc", None),
            P(None, "dur", "inc", None),
            P(None, "dur", "inc", None),
            P(None, "dur", "inc", None),
            P(None, "dur", "inc", None),
            P(None, "dur", "inc", None),
            P("dur", "inc", None),
            P(),
        ),
        out_specs=(P("dur", "inc", None), P("dur", "inc", None), P()),
        check_vma=False,
    )
```

profile of v0, /device:TPU:1, one launch (start us, length us, event | category | flops | bytes accessed | tf_op | source)
XLA Modules:
  0.0 662.2 jit_solution(4900564054730084854)
XLA Ops:
  0.6 0.0 copy-start
  0.7 16.1 %all_gather.12 = f32[1,128,512]{2,1,0:T(8,128)S(1)} all-gather(f32[1,16,512]{2,1,0:T(8,128)} %param.13), channel_id=1, replica_groups=mesh['dur'=32,'inc'=8] {'inc'}, dimensions={1}, use_global_device_ids=true | all-gather | bytes 294912 | tf_op jit(solution)/shard_map/all_gather | solution.py:30
  16.8 0.2 fusion.4
  17.0 2.3 collective-permute-start
  19.3 1.3 collective-permute-start.1
  20.7 0.1 broadcast_bitcast_fusion
  20.9 0.0 copy-start.1
  20.9 0.1 compare_select_fusion
  21.0 113.5 %scatter_custom_fusion = f32[8192]{0:T(1024)S(1)} fusion(s32[16384]{0:T(1024)S(1)} %bitcast.189, f32[16384]{0:T(1024)S(1)} %pad_maximum_fusion, f32[]{:T(128)} %constant.24.clone.1), kind=kCustom, calls=%fused_computation.84 | custom fusion | flops 16384 | bytes 32772 | tf_op jit(solution)/shard_map/scatter-add | solution.py:63
  134.6 4.2 collective-permute-start.4
  138.8 1.3 collective-permute-start.5
  140.2 0.1 compare_select_fusion.1
  140.3 0.6 fusion.36
  140.9 129.5 %gather_fusion = f32[16384]{0:T(1024)S(1)} fusion(f32[16,512]{1,0:T(8,128)S(1)} %fusion.17, s32[16384]{0:T(1024)S(1)} %bitcast.176), kind=kCustom, calls=%fused_computation.clone | custom fusion | bytes 262144 | tf_op jit(solution)/shard_map/jit(take_along_axis)/gather | solution.py:48
  270.5 0.7 copy-done.3
  271.2 0.1 copy-done.5
  271.3 0.7 add_multiply_fusion.1
  271.9 13.5 %all_gather.13 = f32[1,128,512]{2,1,0:T(8,128)S(1)} all-gather(f32[1,16,512]{2,1,0:T(8,128)S(1)} %add_multiply_fusion.1), channel_id=1, replica_groups=mesh['dur'=32,'inc'=8] {'inc'}, dimensions={1}, use_global_device_ids=true | all-gather | bytes 294912 | tf_op jit(solution)/shard_map/all_gather | solution.py:30
  285.4 0.3 fusion.2
  285.7 4.3 collective-permute-start.2
  290.0 1.3 collective-permute-start.3
  292.6 3.2 collective-permute-done.3
  295.8 129.5 %gather_fusion.1 = f32[16384]{0:T(1024)S(1)} fusion(f32[16,512]{1,0:T(8,128)S(1)} %fusion.16, s32[16384]{0:T(1024)S(1)} %bitcast.175), kind=kCustom, calls=%fused_computation.1.clone | custom fusion | bytes 262144 | tf_op jit(solution)/shard_map/jit(take_along_axis)/gather | solution.py:48
  425.4 14.0 %all_gather.14 = f32[1,128,512]{2,1,0:T(8,128)S(1)} all-gather(f32[1,16,512]{2,1,0:T(8,128)S(1)} %fusion.12), channel_id=1, replica_groups=mesh['dur'=32,'inc'=8] {'inc'}, dimensions={1}, use_global_device_ids=true | all-gather | bytes 294912 | tf_op jit(solution)/shard_map/all_gather | solution.py:30
  439.4 2.1 multiply_reduce_fusion.1
  441.6 113.5 %scatter_custom_fusion.1 = f32[8192]{0:T(1024)S(1)} fusion(s32[16384]{0:T(1024)S(1)} %bitcast.188, f32[16384]{0:T(1024)S(1)} %pad_maximum_fusion.2, f32[]{:T(128)} %constant.24.clone.1), kind=kCustom, calls=%fused_computation.82 | custom fusion | flops 16384 | bytes 32772 | tf_op jit(solution)/shard_map/scatter-add | solution.py:63
  555.1 4.9 collective-permute-start.6
  560.0 1.3 collective-permute-start.7
  562.5 83.6 %all-reduce = (f32[1]{0:T(128)}, f32[1]{0:T(128)}) all-reduce(f32[1]{0:T(128)} %bitcast.47, f32[1]{0:T(128)} %bitcast.46), channel_id=1, replica_groups=mesh['dur'=32,'inc'=8] {'dur','inc'}, use_global_device_ids=true, to_apply=%region_5.7 | all-reduce | flops 2 | bytes 16 | tf_op jit(solution)/shard_map/psum | solution.py:110
  646.1 1.8 pad_maximum_fusion.4
  647.9 13.3 %all_gather.15 = f32[1,128,512]{2,1,0:T(8,128)S(1)} all-gather(f32[1,16,512]{2,1,0:T(8,128)S(1)} %fusion.10), channel_id=1, replica_groups=mesh['dur'=32,'inc'=8] {'inc'}, dimensions={1}, use_global_device_ids=true | all-gather | bytes 294912 | tf_op jit(solution)/shard_map/all_gather | solution.py:30
  661.3 1.0 convolution_bitcast_fusion
  (62 shorter events, 0.5 us)
Async XLA Ops:
  0.6 16.2 %copy-start = (f32[128,128]{1,0:T(8,128)S(1)}, f32[128,128]{1,0:T(8,128)}, u32[]{:S(2)}) copy-start(f32[128,128]{1,0:T(8,128)} %param.14) | copy-start | bytes 196612
  16.8 3.9 copy-start.7
  17.0 3.8 copy-start.4
  17.0 3.8 copy-start.8
  17.0 123.8 %collective-permute-start = (f32[1,16,512]{2,1,0:T(8,128)S(1)}, f32[1,16,512]{2,1,0:T(8,128)S(1)}, u32[]{:S(2)}, u32[]{:S(2)}) collective-permute-start(f32[1,16,512]{2,1,0:T(8,128)S(1)} %multiply_bitcast_fusion.1), channel_id=1, source_target_pairs={{0,8},{8,16},{16,24},{24,32},{32,40},{40,48},{48,56},{56,64},{64,7... | collective-permute-start | bytes 98312 | tf_op jit(solution)/shard_map/ppermute | solution.py:16
  19.3 121.5 %collective-permute-start.1 = (f32[1,16,512]{2,1,0:T(8,128)S(1)}, f32[1,16,512]{2,1,0:T(8,128)S(1)}, u32[]{:S(2)}, u32[]{:S(2)}) collective-permute-start(f32[1,16,512]{2,1,0:T(8,128)S(1)} %multiply_bitcast_fusion.1), channel_id=1, source_target_pairs={{8,0},{16,8},{24,16},{32,24},{40,32},{48,40},{56,48},{64,56},{72,6... | collective-permute-start | bytes 98312 | tf_op jit(solution)/shard_map/ppermute | solution.py:19
  20.9 113.7 %copy-start.1 = (f32[2,1,16,512]{3,2,1,0:T(8,128)S(1)}, f32[2,1,16,512]{3,2,1,0:T(8,128)}, u32[]{:S(2)}) copy-start(f32[2,1,16,512]{3,2,1,0:T(8,128)} %param.21) | copy-start | bytes 196612
  20.9 113.7 %copy-start.6 = (s32[2,1,16,512]{3,2,1,0:T(8,128)S(1)}, s32[2,1,16,512]{3,2,1,0:T(8,128)}, u32[]{:S(2)}) copy-start(s32[2,1,16,512]{3,2,1,0:T(8,128)} %param.20) | copy-start | bytes 196612
  21.0 119.1 %copy-start.2 = (s32[2,1,16,512]{3,2,1,0:T(8,128)S(1)}, s32[2,1,16,512]{3,2,1,0:T(8,128)}, u32[]{:S(2)}) copy-start(s32[2,1,16,512]{3,2,1,0:T(8,128)} %param.16) | copy-start | bytes 196612
  134.6 5.7 copy-start.9
  134.6 290.8 %collective-permute-start.4 = (f32[2,1,16,512]{3,2,1,0:T(8,128)S(1)}, f32[2,1,16,512]{3,2,1,0:T(8,128)S(1)}, u32[]{:S(2)}, u32[]{:S(2)}) collective-permute-start(f32[2,1,16,512]{3,2,1,0:T(8,128)S(1)} %pad_maximum_fusion.1), channel_id=1, source_target_pairs={{0,8},{8,16},{16,24},{24,32},{32,40},{40,48},{48,56},{56,64},{64,7... | collective-permute-start | bytes 196616 | tf_op jit(solution)/shard_map/ppermute | solution.py:16
  138.8 286.6 %collective-permute-start.5 = (f32[2,1,16,512]{3,2,1,0:T(8,128)S(1)}, f32[2,1,16,512]{3,2,1,0:T(8,128)S(1)}, u32[]{:S(2)}, u32[]{:S(2)}) collective-permute-start(f32[2,1,16,512]{3,2,1,0:T(8,128)S(1)} %pad_maximum_fusion.1), channel_id=1, source_target_pairs={{8,0},{16,8},{24,16},{32,24},{40,32},{48,40},{56,48},{64,56},{72,6... | collective-permute-start | bytes 196616 | tf_op jit(solution)/shard_map/ppermute | solution.py:19
  270.4 0.8 copy-start.3
  270.4 0.8 copy-start.5
  285.7 6.9 %collective-permute-start.2 = (f32[1,16,512]{2,1,0:T(8,128)S(1)}, f32[1,16,512]{2,1,0:T(8,128)S(1)}, u32[]{:S(2)}, u32[]{:S(2)}) collective-permute-start(f32[1,16,512]{2,1,0:T(8,128)S(1)} %multiply_bitcast_fusion), channel_id=1, source_target_pairs={{0,8},{8,16},{16,24},{24,32},{32,40},{40,48},{48,56},{56,64},{64,7... | collective-permute-start | bytes 98312 | tf_op jit(solution)/shard_map/ppermute | solution.py:16
  290.0 5.9 collective-permute-start.3
  555.1 92.8 %collective-permute-start.6 = (f32[2,1,16,512]{3,2,1,0:T(8,128)S(1)}, f32[2,1,16,512]{3,2,1,0:T(8,128)S(1)}, u32[]{:S(2)}, u32[]{:S(2)}) collective-permute-start(f32[2,1,16,512]{3,2,1,0:T(8,128)S(1)} %pad_maximum_fusion.3), channel_id=1, source_target_pairs={{0,8},{8,16},{16,24},{24,32},{32,40},{40,48},{48,56},{56,64},{64,7... | collective-permute-start | bytes 196616 | tf_op jit(solution)/shard_map/ppermute | solution.py:16
  560.0 87.9 %collective-permute-start.7 = (f32[2,1,16,512]{3,2,1,0:T(8,128)S(1)}, f32[2,1,16,512]{3,2,1,0:T(8,128)S(1)}, u32[]{:S(2)}, u32[]{:S(2)}) collective-permute-start(f32[2,1,16,512]{3,2,1,0:T(8,128)S(1)} %pad_maximum_fusion.3), channel_id=1, source_target_pairs={{8,0},{16,8},{24,16},{32,24},{40,32},{48,40},{56,48},{64,56},{72,6... | collective-permute-start | bytes 196616 | tf_op jit(solution)/shard_map/ppermute | solution.py:19
where the time goes:
time: 663 us; the launch traced here: 662 us
  local copies, waits for them, and re-layouts  261 us (39%)
  other arithmetic  230 us (35%)
  blocking collectives  141 us (21%)
  starting transfers between devices  20.8 us (3%)
    gather x4, local copies, waits for them, and re-layouts, bracket_read(): both_values = jnp.take_along_axis(mixed, both_index, axis=2)  259 us
    scatter-add x2, other arithmetic, push_assets(): jnp.zeros((flat_rows * asset_count,), jnp.float32).at[both_position]  227 us
    psum x1, blocking collectives, per_device(): partial_terms.append(lax.psum(local_demand, ('dur', 'inc')))  83.6 us
    all_gather x4, blocking collectives, markov_apply(): lax.all_gather(field, 'inc', axis=1, tiled=True)  57 us
    ppermute x4, starting transfers between devices, with_halo(): lax.ppermute(lax.slice_in_dim(block, block.shape[dim] - width, None, axis...  15.6 us
  transfers between devices with their start and end apart: 8, of which 1 were waited for; matrix products, arithmetic and copies ran while one was open for 57% of the time, Pallas kernels for 0%

commit v1 on v0

v1 whole, which is shorter than its diff:
```python
import jax
import jax.numpy as jnp
from jax import lax
from jax.experimental import pallas as pl
from jax.experimental.pallas import tpu as pltpu
from jax.sharding import PartitionSpec as P

discount = 0.985
gross_rate = 1.01
adjust_share = 0.3

LANES = 128
F32 = jnp.float32
BF16 = jnp.bfloat16
VMEM = pl.BlockSpec(memory_space=pltpu.VMEM)
SMEM = pl.BlockSpec(memory_space=pltpu.SMEM)


def split_bf16(x):
    high = x.astype(BF16)
    return high, (x - high.astype(F32)).astype(BF16)


def bracket_read(mixed, bracket, weight):
    rows, assets = mixed.shape
    upper = pltpu.roll(mixed, assets - 1, 1)
    chunk_of = bracket >> 7
    lane_of = bracket & (LANES - 1)
    pieces = []
    for out in range(assets // LANES):
        span = slice(out * LANES, (out + 1) * LANES)
        lane, chunk = lane_of[:, span], chunk_of[:, span]
        low = high = None
        for source in range(assets // LANES):
            table = slice(source * LANES, (source + 1) * LANES)
            got_low = jnp.take_along_axis(mixed[:, table], lane, axis=1, mode="promise_in_bounds")
            got_high = jnp.take_along_axis(upper[:, table], lane, axis=1, mode="promise_in_bounds")
            low = got_low if source == 0 else jnp.where(chunk == source, got_low, low)
            high = got_high if source == 0 else jnp.where(chunk == source, got_high, high)
        lam = weight[:, span]
        pieces.append((1.0 - lam) * low + lam * high)
    return jnp.concatenate(pieces, axis=1)


def push_assets(density, bracket, weight, parts_ref, sums_ref):
    rows, assets = density.shape
    chunks = assets // LANES
    chunk_of = bracket >> 7
    lane_of = bracket & (LANES - 1)
    share = weight * density
    stay = density - share
    parts = []
    for value in (stay, share):
        high, low = split_bf16(value)
        parts += [high.astype(F32), low.astype(F32)]
    for k, part in enumerate(parts):
        parts_ref[k] = part
    height = 4 * chunks
    place = lax.broadcasted_iota(jnp.int32, (height, assets), 0)
    lane_iota = lax.broadcasted_iota(jnp.int32, (LANES, assets), 0)
    for r in range(rows):
        picked = jnp.broadcast_to(parts_ref[3, r : r + 1, :], (height, assets))
        for k in (2, 1, 0):
            picked = jnp.where(
                place < (k + 1) * chunks, jnp.broadcast_to(parts_ref[k, r : r + 1, :], (height, assets)), picked
            )
        left = jnp.where((place & (chunks - 1)) == chunk_of[r : r + 1, :], picked, 0.0).astype(BF16)
        right = jnp.where(lane_iota == lane_of[r : r + 1, :], 1.0, 0.0).astype(BF16)
        sums_ref[r * height : (r + 1) * height, :] = lax.dot_general(
            left, right, (((1,), (1,)), ((), ())), preferred_element_type=F32
        )

    def gathered(k, h):
        return sums_ref[pl.ds(k * chunks + h, rows, stride=height), :]

    stayed = jnp.concatenate([gathered(0, h) + gathered(1, h) for h in range(chunks)], axis=1)
    shared = jnp.concatenate([gathered(2, h) + gathered(3, h) for h in range(chunks)], axis=1)
    return stayed + pltpu.roll(shared, 1, 1)


def level_shares(moved, step, omega):
    level = lax.axis_index("dur")
    total = lax.axis_size("dur")
    lower = jnp.clip(level + step, 0, total - 2)
    down = lower - level == -1
    upper_part = moved * omega
    lower_part = moved - upper_part
    to_self = jnp.where(down, upper_part, lower_part)
    to_minus = jnp.where(down, lower_part, 0.0)
    to_plus = jnp.where(down, 0.0, upper_part)
    return to_self, to_plus, to_minus


def weights_kernel(markov_ref, out_ref, flip_ref):
    chip = lax.axis_index("inc") // 2
    wide = out_ref.shape[1] // 2
    flip_ref[...] = markov_ref[...].T
    rows = pl.ds(pl.multiple_of(chip * wide, wide), wide)
    for k, matrix in enumerate((flip_ref[rows, :], discount * markov_ref[rows, :])):
        high, low = split_bf16(matrix)
        out_ref[k, :wide, :] = high
        out_ref[k, wide:, :] = low


def open_kernel(
    value_ref, mass_ref, bracket_ref, weight_ref, step_ref, omega_ref, up_ref, down_ref, self_ref, parts_ref, sums_ref
):
    rows = self_ref.shape[0]
    moved = push_assets(mass_ref[0], bracket_ref[0, 0], weight_ref[0, 0], parts_ref, sums_ref)
    to_self, to_plus, to_minus = level_shares(moved, step_ref[0, 0], omega_ref[0, 0])
    self_ref[...] = to_self
    up_ref[:rows, :] = to_plus
    up_ref[rows:, :] = value_ref[0]
    down_ref[:rows, :] = to_minus
    down_ref[rows:, :] = value_ref[0]


def merge_kernel(self_ref, value_ref, from_low_ref, from_high_ref, out_ref):
    rows = self_ref.shape[0]
    level = lax.axis_index("dur")
    value = value_ref[...].reshape(self_ref.shape)
    low = jnp.where(level == 0, value, from_low_ref[rows:, :])
    high = jnp.where(level == lax.axis_size("dur") - 1, value, from_high_ref[rows:, :])
    out_ref[:rows, :] = self_ref[...] + from_low_ref[:rows, :] + from_high_ref[:rows, :]
    out_ref[rows:, :] = (1.0 - adjust_share) * value + adjust_share * 0.5 * (low + high)


def markov_kernel(own_ref, one_ref, two_ref, three_ref, weights_ref, keep_ref, send_ref, field_ref, total_ref):
    inc = lax.axis_index("inc")
    core = inc % 2
    chip = inc // 2
    chips = lax.axis_size("inc") // 2
    rows = own_ref.shape[0] // 2
    wide = 2 * rows
    for k in range(2):
        field_ref[...] = jnp.zeros_like(field_ref)
        for shift, ref in enumerate((own_ref, one_ref, two_ref, three_ref)):
            source = lax.rem(chip + chips - shift, chips)
            at = pl.ds(pl.multiple_of(source * wide + core * rows, rows), rows)
            field_ref[at, :] = ref[k * rows : (k + 1) * rows, :]
        high, low = split_bf16(field_ref[...])
        both = jnp.dot(weights_ref[k], high, preferred_element_type=F32)
        total_ref[k] = both[:wide] + (
            both[wide:] + jnp.dot(weights_ref[k, :wide, :], low, preferred_element_type=F32)
        )
    for k in range(2):
        part = slice(k * rows, (k + 1) * rows)
        keep_ref[part, :] = total_ref[k, pl.ds(pl.multiple_of(core * rows, rows), rows), :]
        send_ref[part, :] = total_ref[k, pl.ds(pl.multiple_of((1 - core) * rows, rows), rows), :]


def turn_kernel(
    keep_ref, got_ref, bracket_ref, lam_ref, energy_ref, tax_ref, fwd_bracket_ref, fwd_weight_ref, step_ref, omega_ref,
    up_ref, down_ref, self_ref, value_ref, demand_ref, parts_ref, sums_ref,
):
    rows = self_ref.shape[0]
    density = keep_ref[:rows, :] + got_ref[:rows, :]
    mixed = keep_ref[rows:, :] + got_ref[rows:, :]
    interp = bracket_read(mixed, bracket_ref[1, 0], lam_ref[1, 0])
    tax = tax_ref[1]
    share = energy_ref[0]
    demand_ref[0] = jnp.sum(density * (share * lax.rsqrt(interp))) / (1.0 + tax)
    value = gross_rate * interp * (1.0 + tax * share)
    moved = push_assets(density, fwd_bracket_ref[1, 0], fwd_weight_ref[1, 0], parts_ref, sums_ref)
    to_self, to_plus, to_minus = level_shares(moved, step_ref[1, 0], omega_ref[1, 0])
    self_ref[...] = to_self
    value_ref[...] = value
    up_ref[:rows, :] = to_plus
    up_ref[rows:, :] = value
    down_ref[:rows, :] = to_minus
    down_ref[rows:, :] = value


def close_kernel(
    keep_ref, got_ref, bracket_ref, lam_ref, energy_ref, tax_ref, mass_ref, demand_ref, value_ref, out_ref, terms_ref
):
    rows = keep_ref.shape[0] // 2
    out_ref[0] = keep_ref[:rows, :] + got_ref[:rows, :]
    mixed = keep_ref[rows:, :] + got_ref[rows:, :]
    interp = bracket_read(mixed, bracket_ref[0, 0], lam_ref[0, 0])
    tax = tax_ref[0]
    share = energy_ref[0]
    value_ref[0] = gross_rate * interp * (1.0 + tax * share)
    first = jnp.sum(mass_ref[0] * (share * lax.rsqrt(interp))) / (1.0 + tax)
    lane = lax.broadcasted_iota(jnp.int32, terms_ref.shape, 1)
    terms_ref[...] = jnp.where(lane == 0, first, jnp.where(lane == 1, demand_ref[0], 0.0))


def per_device(
    value_next,
    markov,
    energy_share,
    bwd_bracket,
    bwd_weight,
    fwd_bracket,
    fwd_weight,
    dur_step,
    dur_weight,
    mass_start,
    tax,
):
    _, rows, assets = value_next.shape
    states = markov.shape[0]
    levels = lax.axis_size("dur")
    incs = lax.axis_size("inc")
    scale = 1.0 / (levels * states * assets)
    chunks = assets // LANES
    slab = jax.ShapeDtypeStruct((rows, assets), F32)
    pair = jax.ShapeDtypeStruct((2 * rows, assets), F32)
    block = jax.ShapeDtypeStruct((1, rows, assets), F32)
    push_scratch = [pltpu.VMEM((4, rows, assets), F32), pltpu.VMEM((rows * 4 * chunks, LANES), F32)]
    upward = [(i, i + 1) for i in range(levels - 1)]
    downward = [(i + 1, i) for i in range(levels - 1)]

    weights = pl.pallas_call(
        weights_kernel,
        out_shape=jax.ShapeDtypeStruct((2, 4 * rows, states), BF16),
        in_specs=[VMEM],
        out_specs=VMEM,
        scratch_shapes=[pltpu.VMEM((states, states), F32)],
        name="weights",
    )(markov)

    def rounds(up, down, kept, value):
        from_low = lax.ppermute(up, "dur", upward)
        from_high = lax.ppermute(down, "dur", downward)
        mine = pl.pallas_call(merge_kernel, out_shape=pair, in_specs=[VMEM] * 4, out_specs=VMEM, name="merge")(
            kept, value, from_low, from_high
        )
        shifted = [lax.ppermute(mine, "inc", [(i, (i + 2 * k) % incs) for i in range(incs)]) for k in (1, 2, 3)]
        keep, send = pl.pallas_call(
            markov_kernel,
            out_shape=(pair, pair),
            in_specs=[VMEM] * 5,
            out_specs=(VMEM, VMEM),
            scratch_shapes=[pltpu.VMEM((states, assets), F32), pltpu.VMEM((2, 2 * rows, assets), F32)],
            name="markov",
        )(mine, *shifted, weights)
        return keep, lax.ppermute(send, "inc", [(i, i ^ 1) for i in range(incs)])

    up, down, kept = pl.pallas_call(
        open_kernel,
        out_shape=(pair, pair, slab),
        in_specs=[VMEM] * 6,
        out_specs=(VMEM,) * 3,
        scratch_shapes=push_scratch,
        name="open",
    )(value_next, mass_start, fwd_bracket, fwd_weight, dur_step, dur_weight)
    keep, got = rounds(up, down, kept, value_next)
    up, down, kept, value, second = pl.pallas_call(
        turn_kernel,
        out_shape=(pair, pair, slab, slab, jax.ShapeDtypeStruct((1,), F32)),
        in_specs=[VMEM] * 5 + [SMEM] + [VMEM] * 4,
        out_specs=(VMEM,) * 4 + (SMEM,),
        scratch_shapes=push_scratch,
        name="turn",
    )(keep, got, bwd_bracket, bwd_weight, energy_share, tax, fwd_bracket, fwd_weight, dur_step, dur_weight)
    keep, got = rounds(up, down, kept, value)
    value_start, mass_end, terms = pl.pallas_call(
        close_kernel,
        out_shape=(block, block, jax.ShapeDtypeStruct((1, LANES), F32)),
        in_specs=[VMEM] * 5 + [SMEM, VMEM, SMEM],
        out_specs=(VMEM,) * 3,
        name="close",
    )(keep, got, bwd_bracket, bwd_weight, energy_share, tax, mass_start, second)
    everyone = levels * incs
    every_term = lax.all_to_all(jnp.broadcast_to(terms[None], (everyone, 1, LANES)), ("dur", "inc"), 0, 0)
    demand = jnp.sum(every_term[:, 0, :2], axis=0) * scale
    return (value_start, mass_end, demand)


def solution(mesh):
    return jax.shard_map(
        per_device,
        mesh=mesh,
        in_specs=(
            P("dur", "inc", None),
            P(),
            P("dur", "inc", None),
            P(None, "dur", "inc", None),
            P(None, "dur", "inc", None),
            P(None, "dur", "inc", None),
            P(None, "dur", "inc", None),
            P(None, "dur", "inc", None),
            P(None, "dur", "inc", None),
            P("dur", "inc", None),
            P(),
        ),
        out_specs=(P("dur", "inc", None), P("dur", "inc", None), P()),
        check_vma=False,
    )
```

time: 663 us -> 87 us (0.13)
  local copies, waits for them, and re-layouts: 261 us -> 4.39 us
  other arithmetic: 230 us -> 0.8 us
  blocking collectives: 141 us -> 23.9 us
  Pallas kernels: 0 us -> 15.7 us
  waiting for transfers between devices: 3.21 us -> 18.5 us
    gather x4 -> x0, local copies, waits for them, and re-layouts: 259 us -> none  [bracket_read(): both_values = jnp.take_along_axis(mixed, both_index, axis=2)]
    scatter-add x2 -> x0, other arithmetic: 227 us -> none  [push_assets(): jnp.zeros((flat_rows * asset_count,), jnp.float32).at[both_position]]
    psum x1 -> x0, blocking collectives: 83.6 us -> none  [per_device(): partial_terms.append(lax.psum(local_demand, ('dur', 'inc')))]
    all_gather x4 -> x0, blocking collectives: 57 us -> none  [markov_apply(): lax.all_gather(field, 'inc', axis=1, tiled=True)]
    all_to_all x0 -> x1, blocking collectives: none -> 23.9 us  [per_device(): lax.all_to_all(jnp.broadcast_to(terms[None], (everyone, 1, LANES)), ('dur...]
    pallas_call x0 -> x8, Pallas kernels: none -> 15.7 us  [the longest x2 3.71 us: rounds(): pl.pallas_call(markov_kernel, out_shape=(pair, pair), in_specs=[VMEM] * 5...]
    ppermute x8 -> x12, waiting for transfers between devices: 3.21 us -> 18.5 us  [the longest x2 8.66 us: rounds(): from_high = lax.ppermute(down, 'dur', downward)]
    ppermute x8 -> x12, starting transfers between devices: 20.8 us -> 22.4 us  [the longest x2 7.91 us: rounds(): from_low = lax.ppermute(up, 'dur', upward)]
  transfers between devices with their start and end apart: 8 -> 12, of which waited for: 1 -> 11; matrix products, arithmetic and copies ran while one was open for 57% -> 0% of each run, Pallas kernels for 0% -> 2%
where the time goes in v1:
time: 87 us; the launch traced here: 86.3 us
  blocking collectives  23.9 us (27%)
  starting transfers between devices  22.4 us (26%)
  waiting for transfers between devices  18.5 us (21%)
  Pallas kernels  15.7 us (18%)
  local copies, waits for them, and re-layouts  4.39 us (5%)
    all_to_all x1, blocking collectives, per_device(): lax.all_to_all(jnp.broadcast_to(terms[None], (everyone, 1, LANES)), ('dur...  23.9 us
    ppermute x2, waiting for transfers between devices, rounds(): from_high = lax.ppermute(down, 'dur', downward)  8.66 us
    ppermute x2, starting transfers between devices, rounds(): from_low = lax.ppermute(up, 'dur', upward)  7.91 us
    ppermute x6, waiting for transfers between devices, rounds(): lax.ppermute(mine, 'inc', [(i, (i + 2 * k) % incs) for i in range(incs)])  6.93 us
    ppermute x2, starting transfers between devices, rounds(): return (keep, lax.ppermute(send, 'inc', [(i, i ^ 1) for i in range(incs)]))  6.35 us
    ppermute x6, starting transfers between devices, rounds(): lax.ppermute(mine, 'inc', [(i, (i + 2 * k) % incs) for i in range(incs)])  5.51 us
    unnamed x26, local copies, waits for them, and re-layouts  4.32 us
    pallas_call x2, Pallas kernels, rounds(): pl.pallas_call(markov_kernel, out_shape=(pair, pair), in_specs=[VMEM] * 5...  3.71 us
  transfers between devices with their start and end apart: 12, of which 11 were waited for; matrix products, arithmetic and copies ran while one was open for 0% of the time, Pallas kernels for 2%

profile of v1, /device:TPU:1, one launch (start us, length us, event | category | flops | bytes accessed | tf_op | source)
XLA Modules:
  0.0 86.3 jit_solution(17102244504321724610)
XLA Ops:
  0.6 2.4 %open.1 = (f32[32,512]{1,0:T(8,128)}, f32[32,512]{1,0:T(8,128)}, f32[16,512]{1,0:T(8,128)}) custom-call(f32[1,16,512]{2,1,0:T(8,128)} %value_ref.3, f32[1,16,512]{2,1,0:T(8,128)} %mass_ref.3, s32[2,1,16,512]{3,2,1,0:T(8,128)} %fwd_bracket_ref.1, f32[2,1,16,512]{3,2,1,0:T(8,128)} %fwd_weight_ref.1, s32[2,1,16,512]{3,2,1,0:T(8,128)} %step_ref.3, ...), custom_call_target="tpu_custom_call" | custom-call | tf_op jit(solution)/shard_map/open/pallas_call | solution.py:241
  3.0 4.4 %collective-permute-start = (f32[32,512]{1,0:T(8,128)}, f32[32,512]{1,0:T(8,128)S(1)}, u32[]{:S(2)}, u32[]{:S(2)}) collective-permute-start(f32[32,512]{1,0:T(8,128)} %get-tuple-element.19), channel_id=1, source_target_pairs={{0,8},{8,16},{16,24},{24,32},{32,40},{40,48},{48,56},{56,64},{64,7... | collective-permute-start | bytes 196616 | tf_op jit(solution)/shard_map/ppermute | solution.py:225
  7.4 1.3 %collective-permute-start.1 = (f32[32,512]{1,0:T(8,128)}, f32[32,512]{1,0:T(8,128)S(1)}, u32[]{:S(2)}, u32[]{:S(2)}) collective-permute-start(f32[32,512]{1,0:T(8,128)} %get-tuple-element.20), channel_id=1, source_target_pairs={{8,0},{16,8},{24,16},{32,24},{40,32},{48,40},{56,48},{64,56},{72,6... | collective-permute-start | bytes 196616 | tf_op jit(solution)/shard_map/ppermute | solution.py:226
  9.0 3.8 %collective-permute-done.1.from_high_ref = f32[32,512]{1,0:T(8,128)S(1)} collective-permute-done((f32[32,512]{1,0:T(8,128)}, f32[32,512]{1,0:T(8,128)S(1)}, u32[]{:S(2)}, u32[]{:S(2)}) %collective-permute-start.1) | collective-permute-done | bytes 65568 | tf_op jit(solution)/shard_map/ppermute | solution.py:226
  12.8 0.6 copy-done.10
  13.4 1.6 %merge.2.own_ref = f32[32,512]{1,0:T(8,128)} custom-call(f32[16,512]{1,0:T(8,128)} %get-tuple-element.18.self_ref, f32[1,16,512]{2,1,0:T(8,128)} %value_ref.3, f32[32,512]{1,0:T(8,128)} %copy-done.8, f32[32,512]{1,0:T(8,128)} %copy-done.10), custom_call_target="tpu_custom_call" | custom-call | tf_op jit(solution)/shard_map/merge/pallas_call | solution.py:227
  15.0 2.5 %collective-permute-start.4 = (f32[32,512]{1,0:T(8,128)}, f32[32,512]{1,0:T(8,128)S(1)}, u32[]{:S(2)}, u32[]{:S(2)}) collective-permute-start(f32[32,512]{1,0:T(8,128)} %merge.2.own_ref), channel_id=1, source_target_pairs={{0,6},{1,7},{2,0},{3,1},{4,2},{5,3},{6,4},{7,5},{8,14},{9,15},{10,... | collective-permute-start | bytes 196616 | tf_op jit(solution)/shard_map/ppermute | solution.py:230
  18.6 1.6 %weights.1.weights_ref = bf16[2,64,128]{2,1,0:T(8,128)(2,1)} custom-call(f32[128,128]{1,0:T(8,128)} %markov_ref.1), custom_call_target="tpu_custom_call" | custom-call | tf_op jit(solution)/shard_map/weights/pallas_call | solution.py:215
  20.1 2.2 %collective-permute-done.3.two_ref = f32[32,512]{1,0:T(8,128)S(1)} collective-permute-done((f32[32,512]{1,0:T(8,128)}, f32[32,512]{1,0:T(8,128)S(1)}, u32[]{:S(2)}, u32[]{:S(2)}) %collective-permute-start.3) | collective-permute-done | bytes 65568 | tf_op jit(solution)/shard_map/ppermute | solution.py:230
  22.3 0.7 collective-permute-done.2.one_ref
  23.0 0.6 copy-done.6
  23.6 1.8 %markov.2 = (f32[32,512]{1,0:T(8,128)}, f32[32,512]{1,0:T(8,128)}) custom-call(f32[32,512]{1,0:T(8,128)} %merge.2.own_ref, f32[32,512]{1,0:T(8,128)} %copy-done.6, f32[32,512]{1,0:T(8,128)} %copy-done.4, f32[32,512]{1,0:T(8,128)} %copy-done.2, bf16[2,64,128]{2,1,0:T(8,128)(2,1)} %weights.1.weights_ref), custom_call_target="tpu_custom_call" | custom-call | tf_op jit(solution)/shard_map/markov/pallas_call | solution.py:231
  25.5 3.4 %collective-permute-start.5 = (f32[32,512]{1,0:T(8,128)}, f32[32,512]{1,0:T(8,128)S(1)}, u32[]{:S(2)}, u32[]{:S(2)}) collective-permute-start(f32[32,512]{1,0:T(8,128)} %get-tuple-element.22), channel_id=1, source_target_pairs={{0,1},{1,0},{2,3},{3,2},{4,5},{5,4},{6,7},{7,6},{8,9},{9,8},{10,11... | collective-permute-start | bytes 196616 | tf_op jit(solution)/shard_map/ppermute | solution.py:239
  28.8 1.1 %collective-permute-done.5.got_ref = f32[32,512]{1,0:T(8,128)S(1)} collective-permute-done((f32[32,512]{1,0:T(8,128)}, f32[32,512]{1,0:T(8,128)S(1)}, u32[]{:S(2)}, u32[]{:S(2)}) %collective-permute-start.5) | collective-permute-done | bytes 65568 | tf_op jit(solution)/shard_map/ppermute | solution.py:239
  29.9 0.6 copy-done
  30.5 2.5 %turn.1 = (f32[32,512]{1,0:T(8,128)}, f32[32,512]{1,0:T(8,128)}, f32[16,512]{1,0:T(8,128)}, f32[16,512]{1,0:T(8,128)}, f32[1]{0:T(128)}) custom-call(f32[32,512]{1,0:T(8,128)} %get-tuple-element.21.keep_ref, f32[32,512]{1,0:T(8,128)} %copy-done, s32[2,1,16,512]{3,2,1,0:T(8,128)} %bracket_ref.5, f32[2,1,16,512]{3,2,1,0:T(8,128)} %lam_ref.3, ...), custom_call_target="tpu_custom_call" | custom-call | tf_op jit(solution)/shard_map/turn/pallas_call | solution.py:250
  33.1 3.5 %collective-permute-start.6 = (f32[32,512]{1,0:T(8,128)}, f32[32,512]{1,0:T(8,128)S(1)}, u32[]{:S(2)}, u32[]{:S(2)}) collective-permute-start(f32[32,512]{1,0:T(8,128)} %get-tuple-element.25), channel_id=1, source_target_pairs={{0,8},{8,16},{16,24},{24,32},{32,40},{40,48},{48,56},{56,64},{64,7... | collective-permute-start | bytes 196616 | tf_op jit(solution)/shard_map/ppermute | solution.py:225
  36.6 1.3 %collective-permute-start.7 = (f32[32,512]{1,0:T(8,128)}, f32[32,512]{1,0:T(8,128)S(1)}, u32[]{:S(2)}, u32[]{:S(2)}) collective-permute-start(f32[32,512]{1,0:T(8,128)} %get-tuple-element.26), channel_id=1, source_target_pairs={{8,0},{16,8},{24,16},{32,24},{40,32},{48,40},{56,48},{64,56},{72,6... | collective-permute-start | bytes 196616 | tf_op jit(solution)/shard_map/ppermute | solution.py:226
  38.2 4.9 %collective-permute-done.7.from_high_ref = f32[32,512]{1,0:T(8,128)S(1)} collective-permute-done((f32[32,512]{1,0:T(8,128)}, f32[32,512]{1,0:T(8,128)S(1)}, u32[]{:S(2)}, u32[]{:S(2)}) %collective-permute-start.7) | collective-permute-done | bytes 65568 | tf_op jit(solution)/shard_map/ppermute | solution.py:226
  43.1 0.6 copy-done.11
  43.8 1.5 %merge.3.own_ref = f32[32,512]{1,0:T(8,128)} custom-call(f32[16,512]{1,0:T(8,128)} %get-tuple-element.23.self_ref, f32[16,512]{1,0:T(8,128)} %get-tuple-element.24.value_ref, f32[32,512]{1,0:T(8,128)} %copy-done.9, f32[32,512]{1,0:T(8,128)} %copy-done.11), custom_call_target="tpu_custom_call" | custom-call | tf_op jit(solution)/shard_map/merge/pallas_call | solution.py:227
  46.3 0.9 collective-permute-start.8
  47.2 1.4 %collective-permute-done.10.three_ref = f32[32,512]{1,0:T(8,128)S(1)} collective-permute-done((f32[32,512]{1,0:T(8,128)}, f32[32,512]{1,0:T(8,128)S(1)}, u32[]{:S(2)}, u32[]{:S(2)}) %collective-permute-start.10) | collective-permute-done | bytes 65568 | tf_op jit(solution)/shard_map/ppermute | solution.py:230
  48.6 2.0 %collective-permute-done.9.two_ref = f32[32,512]{1,0:T(8,128)S(1)} collective-permute-done((f32[32,512]{1,0:T(8,128)}, f32[32,512]{1,0:T(8,128)S(1)}, u32[]{:S(2)}, u32[]{:S(2)}) %collective-permute-start.9) | collective-permute-done | bytes 65568 | tf_op jit(solution)/shard_map/ppermute | solution.py:230
  50.6 0.7 collective-permute-done.8.one_ref
  51.3 0.6 copy-done.7
  51.9 1.9 %markov.3 = (f32[32,512]{1,0:T(8,128)}, f32[32,512]{1,0:T(8,128)}) custom-call(f32[32,512]{1,0:T(8,128)} %merge.3.own_ref, f32[32,512]{1,0:T(8,128)} %copy-done.7, f32[32,512]{1,0:T(8,128)} %copy-done.5, f32[32,512]{1,0:T(8,128)} %copy-done.3, bf16[2,64,128]{2,1,0:T(8,128)(2,1)} %weights.1.weights_ref), custom_call_target="tpu_custom_call" | custom-call | tf_op jit(solution)/shard_map/markov/pallas_call | solution.py:231
  53.8 3.0 %collective-permute-start.11 = (f32[32,512]{1,0:T(8,128)}, f32[32,512]{1,0:T(8,128)S(1)}, u32[]{:S(2)}, u32[]{:S(2)}) collective-permute-start(f32[32,512]{1,0:T(8,128)} %get-tuple-element.28), channel_id=1, source_target_pairs={{0,1},{1,0},{2,3},{3,2},{4,5},{5,4},{6,7},{7,6},{8,9},{9,8},{10,11... | collective-permute-start | bytes 196616 | tf_op jit(solution)/shard_map/ppermute | solution.py:239
  56.8 1.1 %collective-permute-done.11.got_ref = f32[32,512]{1,0:T(8,128)S(1)} collective-permute-done((f32[32,512]{1,0:T(8,128)}, f32[32,512]{1,0:T(8,128)S(1)}, u32[]{:S(2)}, u32[]{:S(2)}) %collective-permute-start.11) | collective-permute-done | bytes 65568 | tf_op jit(solution)/shard_map/ppermute | solution.py:239
  57.9 0.6 copy-done.1
  58.5 2.4 %close.1 = (f32[1,16,512]{2,1,0:T(8,128)}, f32[1,16,512]{2,1,0:T(8,128)}, f32[1,128]{1,0:T(1,128)}) custom-call(f32[32,512]{1,0:T(8,128)} %get-tuple-element.27.keep_ref, f32[32,512]{1,0:T(8,128)} %copy-done.1, s32[2,1,16,512]{3,2,1,0:T(8,128)} %bracket_ref.5, f32[2,1,16,512]{3,2,1,0:T(8,128)} %lam_ref.3, f32[1,16,512]{2,1,0:T(8,128)} %energy_ref.3, ...), custom_call_target="tpu_custom_call" | custom-call | tf_op jit(solution)/shard_map/close/pallas_call | solution.py:259
  61.6 23.9 %all_to_all.5 = f32[256,1,128]{2,1,0:T(1,128)S(1)} all-to-all(f32[256,1,128]{2,1,0:T(1,128)S(1)} %broadcast_in_dim.9), channel_id=1, replica_groups=mesh['dur'=32,'inc'=8] {'dur','inc'}, dimensions={0} | all-to-all | bytes 262144 | tf_op jit(solution)/shard_map/all_to_all | solution.py:267
  (30 shorter events, 4.3 us)
Async XLA Ops:
  3.0 6.0 %collective-permute-start = (f32[32,512]{1,0:T(8,128)}, f32[32,512]{1,0:T(8,128)S(1)}, u32[]{:S(2)}, u32[]{:S(2)}) collective-permute-start(f32[32,512]{1,0:T(8,128)} %get-tuple-element.19), channel_id=1, source_target_pairs={{0,8},{8,16},{16,24},{24,32},{32,40},{40,48},{48,56},{56,64},{64,7... | collective-permute-start | bytes 196616 | tf_op jit(solution)/shard_map/ppermute | solution.py:225
  7.4 5.4 %collective-permute-start.1 = (f32[32,512]{1,0:T(8,128)}, f32[32,512]{1,0:T(8,128)S(1)}, u32[]{:S(2)}, u32[]{:S(2)}) collective-permute-start(f32[32,512]{1,0:T(8,128)} %get-tuple-element.20), channel_id=1, source_target_pairs={{8,0},{16,8},{24,16},{32,24},{40,32},{48,40},{56,48},{64,56},{72,6... | collective-permute-start | bytes 196616 | tf_op jit(solution)/shard_map/ppermute | solution.py:226
  9.0 3.8 %copy-start.8 = (f32[32,512]{1,0:T(8,128)}, f32[32,512]{1,0:T(8,128)S(1)}, u32[]{:S(2)}) copy-start(f32[32,512]{1,0:T(8,128)S(1)} %collective-permute-done.from_low_ref) | copy-start | bytes 196612
  12.8 0.6 copy-start.10
  15.0 5.2 %collective-permute-start.4 = (f32[32,512]{1,0:T(8,128)}, f32[32,512]{1,0:T(8,128)S(1)}, u32[]{:S(2)}, u32[]{:S(2)}) collective-permute-start(f32[32,512]{1,0:T(8,128)} %merge.2.own_ref), channel_id=1, source_target_pairs={{0,6},{1,7},{2,0},{3,1},{4,2},{5,3},{6,4},{7,5},{8,14},{9,15},{10,... | collective-permute-start | bytes 196616 | tf_op jit(solution)/shard_map/ppermute | solution.py:230
  17.4 4.9 %collective-permute-start.3 = (f32[32,512]{1,0:T(8,128)}, f32[32,512]{1,0:T(8,128)S(1)}, u32[]{:S(2)}, u32[]{:S(2)}) collective-permute-start(f32[32,512]{1,0:T(8,128)} %merge.2.own_ref), channel_id=1, source_target_pairs={{0,4},{1,5},{2,6},{3,7},{4,0},{5,1},{6,2},{7,3},{8,12},{9,13},{10,... | collective-permute-start | bytes 196616 | tf_op jit(solution)/shard_map/ppermute | solution.py:230
  18.0 5.0 %collective-permute-start.2 = (f32[32,512]{1,0:T(8,128)}, f32[32,512]{1,0:T(8,128)S(1)}, u32[]{:S(2)}, u32[]{:S(2)}) collective-permute-start(f32[32,512]{1,0:T(8,128)} %merge.2.own_ref), channel_id=1, source_target_pairs={{0,2},{1,3},{2,4},{3,5},{4,6},{5,7},{6,0},{7,1},{8,10},{9,11},{10,... | collective-permute-start | bytes 196616 | tf_op jit(solution)/shard_map/ppermute | solution.py:230
  20.1 2.8 %copy-start.2 = (f32[32,512]{1,0:T(8,128)}, f32[32,512]{1,0:T(8,128)S(1)}, u32[]{:S(2)}) copy-start(f32[32,512]{1,0:T(8,128)S(1)} %collective-permute-done.4.three_ref) | copy-start | bytes 196612
  22.3 0.7 copy-start.4
  23.0 0.6 copy-start.6
  25.5 4.5 %collective-permute-start.5 = (f32[32,512]{1,0:T(8,128)}, f32[32,512]{1,0:T(8,128)S(1)}, u32[]{:S(2)}, u32[]{:S(2)}) collective-permute-start(f32[32,512]{1,0:T(8,128)} %get-tuple-element.22), channel_id=1, source_target_pairs={{0,1},{1,0},{2,3},{3,2},{4,5},{5,4},{6,7},{7,6},{8,9},{9,8},{10,11... | collective-permute-start | bytes 196616 | tf_op jit(solution)/shard_map/ppermute | solution.py:239
  29.9 0.6 copy-start
  33.1 5.2 %collective-permute-start.6 = (f32[32,512]{1,0:T(8,128)}, f32[32,512]{1,0:T(8,128)S(1)}, u32[]{:S(2)}, u32[]{:S(2)}) collective-permute-start(f32[32,512]{1,0:T(8,128)} %get-tuple-element.25), channel_id=1, source_target_pairs={{0,8},{8,16},{16,24},{24,32},{32,40},{40,48},{48,56},{56,64},{64,7... | collective-permute-start | bytes 196616 | tf_op jit(solution)/shard_map/ppermute | solution.py:225
  36.6 6.5 %collective-permute-start.7 = (f32[32,512]{1,0:T(8,128)}, f32[32,512]{1,0:T(8,128)S(1)}, u32[]{:S(2)}, u32[]{:S(2)}) collective-permute-start(f32[32,512]{1,0:T(8,128)} %get-tuple-element.26), channel_id=1, source_target_pairs={{8,0},{16,8},{24,16},{32,24},{40,32},{48,40},{56,48},{64,56},{72,6... | collective-permute-start | bytes 196616 | tf_op jit(solution)/shard_map/ppermute | solution.py:226
  38.2 4.9 %copy-start.9 = (f32[32,512]{1,0:T(8,128)}, f32[32,512]{1,0:T(8,128)S(1)}, u32[]{:S(2)}) copy-start(f32[32,512]{1,0:T(8,128)S(1)} %collective-permute-done.6.from_low_ref) | copy-start | bytes 196612
  43.1 0.6 copy-start.11
  45.3 3.3 %collective-permute-start.10 = (f32[32,512]{1,0:T(8,128)}, f32[32,512]{1,0:T(8,128)S(1)}, u32[]{:S(2)}, u32[]{:S(2)}) collective-permute-start(f32[32,512]{1,0:T(8,128)} %merge.3.own_ref), channel_id=1, source_target_pairs={{0,6},{1,7},{2,0},{3,1},{4,2},{5,3},{6,4},{7,5},{8,14},{9,15},{10,... | collective-permute-start | bytes 196616 | tf_op jit(solution)/shard_map/ppermute | solution.py:230
  45.8 4.9 %collective-permute-start.9 = (f32[32,512]{1,0:T(8,128)}, f32[32,512]{1,0:T(8,128)S(1)}, u32[]{:S(2)}, u32[]{:S(2)}) collective-permute-start(f32[32,512]{1,0:T(8,128)} %merge.3.own_ref), channel_id=1, source_target_pairs={{0,4},{1,5},{2,6},{3,7},{4,0},{5,1},{6,2},{7,3},{8,12},{9,13},{10,... | collective-permute-start | bytes 196616 | tf_op jit(solution)/shard_map/ppermute | solution.py:230
  46.3 5.0 %collective-permute-start.8 = (f32[32,512]{1,0:T(8,128)}, f32[32,512]{1,0:T(8,128)S(1)}, u32[]{:S(2)}, u32[]{:S(2)}) collective-permute-start(f32[32,512]{1,0:T(8,128)} %merge.3.own_ref), channel_id=1, source_target_pairs={{0,2},{1,3},{2,4},{3,5},{4,6},{5,7},{6,0},{7,1},{8,10},{9,11},{10,... | collective-permute-start | bytes 196616 | tf_op jit(solution)/shard_map/ppermute | solution.py:230
  48.6 2.7 %copy-start.3 = (f32[32,512]{1,0:T(8,128)}, f32[32,512]{1,0:T(8,128)S(1)}, u32[]{:S(2)}) copy-start(f32[32,512]{1,0:T(8,128)S(1)} %collective-permute-done.10.three_ref) | copy-start | bytes 196612
  50.6 0.7 copy-start.5
  51.3 0.6 copy-start.7
  53.8 4.1 %collective-permute-start.11 = (f32[32,512]{1,0:T(8,128)}, f32[32,512]{1,0:T(8,128)S(1)}, u32[]{:S(2)}, u32[]{:S(2)}) collective-permute-start(f32[32,512]{1,0:T(8,128)} %get-tuple-element.28), channel_id=1, source_target_pairs={{0,1},{1,0},{2,3},{3,2},{4,5},{5,4},{6,7},{7,6},{8,9},{9,8},{10,11... | collective-permute-start | bytes 196616 | tf_op jit(solution)/shard_map/ppermute | solution.py:239
  57.9 0.6 copy-start.1
  60.9 0.6 copy-start.12

commit v2 on v1

--- a/solution.py
+++ b/solution.py
@@ -1,3 +1,5 @@
+import functools
+
 import jax
 import jax.numpy as jnp
 from jax import lax
@@ -14,6 +16,10 @@
 BF16 = jnp.bfloat16
 VMEM = pl.BlockSpec(memory_space=pltpu.VMEM)
 SMEM = pl.BlockSpec(memory_space=pltpu.SMEM)
+
+
+def in_vmem(*arrays):
+    return tuple(pltpu.with_memory_space_constraint(x, pltpu.VMEM) for x in arrays)
 
 
 def split_bf16(x):
@@ -159,7 +165,7 @@
     interp = bracket_read(mixed, bracket_ref[1, 0], lam_ref[1, 0])
     tax = tax_ref[1]
     share = energy_ref[0]
-    demand_ref[0] = jnp.sum(density * (share * lax.rsqrt(interp))) / (1.0 + tax)
+    demand_ref[...] = jnp.broadcast_to(jnp.sum(density * (share * lax.rsqrt(interp))) / (1.0 + tax), demand_ref.shape)
     value = gross_rate * interp * (1.0 + tax * share)
     moved = push_assets(density, fwd_bracket_ref[1, 0], fwd_weight_ref[1, 0], parts_ref, sums_ref)
     to_self, to_plus, to_minus = level_shares(moved, step_ref[1, 0], omega_ref[1, 0])
@@ -172,7 +178,7 @@
 
 
 def close_kernel(
-    keep_ref, got_ref, bracket_ref, lam_ref, energy_ref, tax_ref, mass_ref, demand_ref, value_ref, out_ref, terms_ref
+    scale, keep_ref, got_ref, bracket_ref, lam_ref, energy_ref, tax_ref, mass_ref, demand_ref, value_ref, out_ref, terms_ref
 ):
     rows = keep_ref.shape[0] // 2
     out_ref[0] = keep_ref[:rows, :] + got_ref[:rows, :]
@@ -182,8 +188,15 @@
     share = energy_ref[0]
     value_ref[0] = gross_rate * interp * (1.0 + tax * share)
     first = jnp.sum(mass_ref[0] * (share * lax.rsqrt(interp))) / (1.0 + tax)
-    lane = lax.broadcasted_iota(jnp.int32, terms_ref.shape, 1)
-    terms_ref[...] = jnp.where(lane == 0, first, jnp.where(lane == 1, demand_ref[0], 0.0))
+    lane = lax.broadcasted_iota(jnp.int32, demand_ref.shape, 1)
+    both = scale * jnp.where(lane == 0, first, demand_ref[...])
+    terms_ref[...] = jnp.broadcast_to(both[None], terms_ref.shape)
+
+
+def demand_kernel(terms_ref, out_ref):
+    total = jnp.sum(terms_ref[...], axis=0)
+    out_ref[0] = total[0, 0]
+    out_ref[1] = total[0, 1]
 
 
 def per_device(
@@ -205,27 +218,28 @@
     incs = lax.axis_size("inc")
     scale = 1.0 / (levels * states * assets)
     chunks = assets // LANES
-    slab = jax.ShapeDtypeStruct((rows, assets), F32)
-    pair = jax.ShapeDtypeStruct((2 * rows, assets), F32)
+    slab = pltpu.VMEM((rows, assets), F32)
+    pair = pltpu.VMEM((2 * rows, assets), F32)
     block = jax.ShapeDtypeStruct((1, rows, assets), F32)
     push_scratch = [pltpu.VMEM((4, rows, assets), F32), pltpu.VMEM((rows * 4 * chunks, LANES), F32)]
     upward = [(i, i + 1) for i in range(levels - 1)]
     downward = [(i + 1, i) for i in range(levels - 1)]
+    everyone = levels * incs
 
     weights = pl.pallas_call(
         weights_kernel,
-        out_shape=jax.ShapeDtypeStruct((2, 4 * rows, states), BF16),
+        out_shape=pltpu.VMEM((2, 4 * rows, states), BF16),
         in_specs=[VMEM],
         out_specs=VMEM,
         scratch_shapes=[pltpu.VMEM((states, states), F32)],
         name="weights",
-    )(markov)
+    )(*in_vmem(markov))
 
     def rounds(up, down, kept, value):
         from_low = lax.ppermute(up, "dur", upward)
         from_high = lax.ppermute(down, "dur", downward)
         mine = pl.pallas_call(merge_kernel, out_shape=pair, in_specs=[VMEM] * 4, out_specs=VMEM, name="merge")(
-            kept, value, from_low, from_high
+            *in_vmem(kept, value, from_low, from_high)
         )
         shifted = [lax.ppermute(mine, "inc", [(i, (i + 2 * k) % incs) for i in range(incs)]) for k in (1, 2, 3)]
         keep, send = pl.pallas_call(
@@ -235,7 +249,7 @@
             out_specs=(VMEM, VMEM),
             scratch_shapes=[pltpu.VMEM((states, assets), F32), pltpu.VMEM((2, 2 * rows, assets), F32)],
             name="markov",
-        )(mine, *shifted, weights)
+        )(*in_vmem(mine, *shifted, weights))
         return keep, lax.ppermute(send, "inc", [(i, i ^ 1) for i in range(incs)])
 
     up, down, kept = pl.pallas_call(
@@ -249,23 +263,32 @@
     keep, got = rounds(up, down, kept, value_next)
     up, down, kept, value, second = pl.pallas_call(
         turn_kernel,
-        out_shape=(pair, pair, slab, slab, jax.ShapeDtypeStruct((1,), F32)),
+        out_shape=(pair, pair, slab, slab, pltpu.VMEM((1, LANES), F32)),
         in_specs=[VMEM] * 5 + [SMEM] + [VMEM] * 4,
-        out_specs=(VMEM,) * 4 + (SMEM,),
+        out_specs=(VMEM,) * 5,
         scratch_shapes=push_scratch,
         name="turn",
-    )(keep, got, bwd_bracket, bwd_weight, energy_share, tax, fwd_bracket, fwd_weight, dur_step, dur_weight)
+    )(
+        *in_vmem(keep, got, bwd_bracket, bwd_weight, energy_share),
+        tax,
+        *in_vmem(fwd_bracket, fwd_weight, dur_step, dur_weight),
+    )
     keep, got = rounds(up, down, kept, value)
     value_start, mass_end, terms = pl.pallas_call(
-        close_kernel,
-        out_shape=(block, block, jax.ShapeDtypeStruct((1, LANES), F32)),
-        in_specs=[VMEM] * 5 + [SMEM, VMEM, SMEM],
+        functools.partial(close_kernel, scale),
+        out_shape=(block, block, pltpu.VMEM((everyone, 1, LANES), F32)),
+        in_specs=[VMEM] * 5 + [SMEM] + [VMEM] * 2,
         out_specs=(VMEM,) * 3,
         name="close",
-    )(keep, got, bwd_bracket, bwd_weight, energy_share, tax, mass_start, second)
-    everyone = levels * incs
-    every_term = lax.all_to_all(jnp.broadcast_to(terms[None], (everyone, 1, LANES)), ("dur", "inc"), 0, 0)
-    demand = jnp.sum(every_term[:, 0, :2], axis=0) * scale
+    )(*in_vmem(keep, got, bwd_bracket, bwd_weight, energy_share), tax, *in_vmem(mass_start, second))
+    every_term = lax.all_to_all(terms, ("dur", "inc"), 0, 0)
+    demand = pl.pallas_call(
+        demand_kernel,
+        out_shape=jax.ShapeDtypeStruct((2,), F32),
+        in_specs=[VMEM],
+        out_specs=SMEM,
+        name="demand",
+    )(*in_vmem(every_term))
     return (value_start, mass_end, demand)
 
 

time: 87 us -> 72.6 us (0.83)
  Pallas kernels: 15.7 us -> 6.23 us
  local copies, waits for them, and re-layouts: 4.39 us -> 0.05 us
    unnamed x26 -> x20, local copies, waits for them, and re-layouts: 4.32 us -> 0.05 us
    pallas_call x2, Pallas kernels: 3.71 us -> 0.54 us  [rounds(): pl.pallas_call(markov_kernel, out_shape=(pair, pair), in_specs=[VMEM] * 5...]
    pallas_call x2, Pallas kernels: 3.1 us -> 0.04 us  [rounds(): pl.pallas_call(merge_kernel, out_shape=pair, in_specs=[VMEM] * 4, out_spe...]
    pallas_call x3 -> x4, Pallas kernels: 6.51 us -> 3.92 us  [the longest x1 1.5 us: per_device(): pl.pallas_call(functools.partial(close_kernel, scale), out_shape=(block,...]
  transfers between devices with their start and end apart: 12 -> 12, of which waited for: 11 -> 9; matrix products, arithmetic and copies ran while one was open for 0% -> 0% of each run, Pallas kernels for 2% -> 0%
where the time goes in v2:
time: 72.6 us; the launch traced here: 72.3 us
  blocking collectives  23.9 us (33%)
  starting transfers between devices  22.9 us (32%)
  waiting for transfers between devices  18.4 us (25%)
  Pallas kernels  6.23 us (9%)
  between operations  0.8 us (1%)
    all_to_all x1, blocking collectives, per_device(): every_term = lax.all_to_all(terms, ('dur', 'inc'), 0, 0)  23.9 us
    ppermute x2, waiting for transfers between devices, rounds(): from_high = lax.ppermute(down, 'dur', downward)  8.88 us
    ppermute x2, starting transfers between devices, rounds(): from_low = lax.ppermute(up, 'dur', upward)  7.92 us
    ppermute x6, waiting for transfers between devices, rounds(): lax.ppermute(mine, 'inc', [(i, (i + 2 * k) % incs) for i in range(incs)])  7.73 us
    ppermute x2, starting transfers between devices, rounds(): return (keep, lax.ppermute(send, 'inc', [(i, i ^ 1) for i in range(incs)]))  6.7 us
    ppermute x6, starting transfers between devices, rounds(): lax.ppermute(mine, 'inc', [(i, (i + 2 * k) % incs) for i in range(incs)])  5.67 us
    ppermute x2, starting transfers between devices, rounds(): from_high = lax.ppermute(down, 'dur', downward)  2.58 us
    ppermute x2, waiting for transfers between devices, rounds(): return (keep, lax.ppermute(send, 'inc', [(i, i ^ 1) for i in range(incs)]))  1.8 us
  transfers between devices with their start and end apart: 12, of which 9 were waited for; matrix products, arithmetic and copies ran while one was open for 0% of the time, Pallas kernels for 0%

profile of v2, /device:TPU:1, one launch (start us, length us, event | category | flops | bytes accessed | tf_op | source)
XLA Modules:
  0.0 72.3 jit_solution(15636871853739576367)
XLA Ops:
  0.6 1.7 %open.1 = (f32[32,512]{1,0:T(8,128)S(1)}, f32[32,512]{1,0:T(8,128)S(1)}, f32[16,512]{1,0:T(8,128)S(1)}) custom-call(f32[1,16,512]{2,1,0:T(8,128)} %value_ref.3, f32[1,16,512]{2,1,0:T(8,128)} %mass_ref.3, s32[2,1,16,512]{3,2,1,0:T(8,128)} %fwd_bracket_ref.1, f32[2,1,16,512]{3,2,1,0:T(8,128)} %fwd_weight_ref.1, s32[2,1,16,512]{3,2,1,0:T(8,128)} %step_ref.3, ...), custom_call_target="tpu_custom_call" | custom-call | tf_op jit(solution)/shard_map/open/pallas_call | solution.py:255
  2.4 4.4 %collective-permute-start = (f32[32,512]{1,0:T(8,128)S(1)}, f32[32,512]{1,0:T(8,128)S(1)}, u32[]{:S(2)}, u32[]{:S(2)}) collective-permute-start(f32[32,512]{1,0:T(8,128)S(1)} %get-tuple-element.19), channel_id=1, source_target_pairs={{0,8},{8,16},{16,24},{24,32},{32,40},{40,48},{48,56},{56,64},{64,7... | collective-permute-start | bytes 196616 | tf_op jit(solution)/shard_map/ppermute | solution.py:239
  6.8 1.3 %collective-permute-start.1 = (f32[32,512]{1,0:T(8,128)S(1)}, f32[32,512]{1,0:T(8,128)S(1)}, u32[]{:S(2)}, u32[]{:S(2)}) collective-permute-start(f32[32,512]{1,0:T(8,128)S(1)} %get-tuple-element.20), channel_id=1, source_target_pairs={{8,0},{16,8},{24,16},{32,24},{40,32},{48,40},{56,48},{64,56},{72,6... | collective-permute-start | bytes 196616 | tf_op jit(solution)/shard_map/ppermute | solution.py:240
  8.1 0.0 collective-permute-done.from_low_ref
  8.1 3.9 %collective-permute-done.1.from_high_ref = f32[32,512]{1,0:T(8,128)S(1)} collective-permute-done((f32[32,512]{1,0:T(8,128)S(1)}, f32[32,512]{1,0:T(8,128)S(1)}, u32[]{:S(2)}, u32[]{:S(2)}) %collective-permute-start.1) | collective-permute-done | bytes 65568 | tf_op jit(solution)/shard_map/ppermute | solution.py:240
  12.0 2.6 %collective-permute-start.4 = (f32[32,512]{1,0:T(8,128)S(1)}, f32[32,512]{1,0:T(8,128)S(1)}, u32[]{:S(2)}, u32[]{:S(2)}) collective-permute-start(f32[32,512]{1,0:T(8,128)S(1)} %merge.2.own_ref), channel_id=1, source_target_pairs={{0,6},{1,7},{2,0},{3,1},{4,2},{5,3},{6,4},{7,5},{8,14},{9,15},{10,... | collective-permute-start | bytes 196616 | tf_op jit(solution)/shard_map/ppermute | solution.py:244
  14.5 0.5 collective-permute-start.3
  15.1 0.6 collective-permute-start.2
  15.7 0.1 weights.1.weights_ref
  15.8 0.0 collective-permute-done.4.three_ref
  15.9 3.3 %collective-permute-done.3.two_ref = f32[32,512]{1,0:T(8,128)S(1)} collective-permute-done((f32[32,512]{1,0:T(8,128)S(1)}, f32[32,512]{1,0:T(8,128)S(1)}, u32[]{:S(2)}, u32[]{:S(2)}) %collective-permute-start.3) | collective-permute-done | bytes 65568 | tf_op jit(solution)/shard_map/ppermute | solution.py:244
  19.2 0.7 collective-permute-done.2.one_ref
  19.9 0.3 markov.2
  20.1 3.4 %collective-permute-start.5 = (f32[32,512]{1,0:T(8,128)S(1)}, f32[32,512]{1,0:T(8,128)S(1)}, u32[]{:S(2)}, u32[]{:S(2)}) collective-permute-start(f32[32,512]{1,0:T(8,128)S(1)} %get-tuple-element.22), channel_id=1, source_target_pairs={{0,1},{1,0},{2,3},{3,2},{4,5},{5,4},{6,7},{7,6},{8,9},{9,8},{10,11... | collective-permute-start | bytes 196616 | tf_op jit(solution)/shard_map/ppermute | solution.py:253
  23.6 0.9 %collective-permute-done.5.got_ref = f32[32,512]{1,0:T(8,128)S(1)} collective-permute-done((f32[32,512]{1,0:T(8,128)S(1)}, f32[32,512]{1,0:T(8,128)S(1)}, u32[]{:S(2)}, u32[]{:S(2)}) %collective-permute-start.5) | collective-permute-done | bytes 65568 | tf_op jit(solution)/shard_map/ppermute | solution.py:253
  24.5 1.4 %turn.1 = (f32[32,512]{1,0:T(8,128)S(1)}, f32[32,512]{1,0:T(8,128)S(1)}, f32[16,512]{1,0:T(8,128)S(1)}, f32[16,512]{1,0:T(8,128)S(1)}, f32[1,128]{1,0:T(1,128)S(1)}) custom-call(f32[32,512]{1,0:T(8,128)S(1)} %get-tuple-element.21.keep_ref, f32[32,512]{1,0:T(8,128)S(1)} %collective-permute-done.5.got_ref, s32[2,1,16,512]{3,2,1,0:T(8,128)S(1)} %copy-done.4, ...), custom_call_target="tpu_custom_call" | custom-call | tf_op jit(solution)/shard_map/turn/pallas_call | solution.py:264
  26.0 3.5 %collective-permute-start.6 = (f32[32,512]{1,0:T(8,128)S(1)}, f32[32,512]{1,0:T(8,128)S(1)}, u32[]{:S(2)}, u32[]{:S(2)}) collective-permute-start(f32[32,512]{1,0:T(8,128)S(1)} %get-tuple-element.25), channel_id=1, source_target_pairs={{0,8},{8,16},{16,24},{24,32},{32,40},{40,48},{48,56},{56,64},{64,7... | collective-permute-start | bytes 196616 | tf_op jit(solution)/shard_map/ppermute | solution.py:239
  29.5 1.3 %collective-permute-start.7 = (f32[32,512]{1,0:T(8,128)S(1)}, f32[32,512]{1,0:T(8,128)S(1)}, u32[]{:S(2)}, u32[]{:S(2)}) collective-permute-start(f32[32,512]{1,0:T(8,128)S(1)} %get-tuple-element.26), channel_id=1, source_target_pairs={{8,0},{16,8},{24,16},{32,24},{40,32},{48,40},{56,48},{64,56},{72,6... | collective-permute-start | bytes 196616 | tf_op jit(solution)/shard_map/ppermute | solution.py:240
  30.8 0.0 collective-permute-done.6.from_low_ref
  30.8 5.0 %collective-permute-done.7.from_high_ref = f32[32,512]{1,0:T(8,128)S(1)} collective-permute-done((f32[32,512]{1,0:T(8,128)S(1)}, f32[32,512]{1,0:T(8,128)S(1)}, u32[]{:S(2)}, u32[]{:S(2)}) %collective-permute-start.7) | collective-permute-done | bytes 65568 | tf_op jit(solution)/shard_map/ppermute | solution.py:240
  35.9 0.4 collective-permute-start.10
  36.2 0.9 %collective-permute-start.9 = (f32[32,512]{1,0:T(8,128)S(1)}, f32[32,512]{1,0:T(8,128)S(1)}, u32[]{:S(2)}, u32[]{:S(2)}) collective-permute-start(f32[32,512]{1,0:T(8,128)S(1)} %merge.3.own_ref), channel_id=1, source_target_pairs={{0,4},{1,5},{2,6},{3,7},{4,0},{5,1},{6,2},{7,3},{8,12},{9,13},{10,... | collective-permute-start | bytes 196616 | tf_op jit(solution)/shard_map/ppermute | solution.py:244
  37.1 0.8 %collective-permute-start.8 = (f32[32,512]{1,0:T(8,128)S(1)}, f32[32,512]{1,0:T(8,128)S(1)}, u32[]{:S(2)}, u32[]{:S(2)}) collective-permute-start(f32[32,512]{1,0:T(8,128)S(1)} %merge.3.own_ref), channel_id=1, source_target_pairs={{0,2},{1,3},{2,4},{3,5},{4,6},{5,7},{6,0},{7,1},{8,10},{9,11},{10,... | collective-permute-start | bytes 196616 | tf_op jit(solution)/shard_map/ppermute | solution.py:244
  37.8 1.2 %collective-permute-done.10.three_ref = f32[32,512]{1,0:T(8,128)S(1)} collective-permute-done((f32[32,512]{1,0:T(8,128)S(1)}, f32[32,512]{1,0:T(8,128)S(1)}, u32[]{:S(2)}, u32[]{:S(2)}) %collective-permute-start.10) | collective-permute-done | bytes 65568 | tf_op jit(solution)/shard_map/ppermute | solution.py:244
  39.1 1.8 %collective-permute-done.9.two_ref = f32[32,512]{1,0:T(8,128)S(1)} collective-permute-done((f32[32,512]{1,0:T(8,128)S(1)}, f32[32,512]{1,0:T(8,128)S(1)}, u32[]{:S(2)}, u32[]{:S(2)}) %collective-permute-start.9) | collective-permute-done | bytes 65568 | tf_op jit(solution)/shard_map/ppermute | solution.py:244
  40.9 0.7 collective-permute-done.8.one_ref
  41.6 0.3 markov.3
  41.8 3.3 %collective-permute-start.11 = (f32[32,512]{1,0:T(8,128)S(1)}, f32[32,512]{1,0:T(8,128)S(1)}, u32[]{:S(2)}, u32[]{:S(2)}) collective-permute-start(f32[32,512]{1,0:T(8,128)S(1)} %get-tuple-element.28), channel_id=1, source_target_pairs={{0,1},{1,0},{2,3},{3,2},{4,5},{5,4},{6,7},{7,6},{8,9},{9,8},{10,11... | collective-permute-start | bytes 196616 | tf_op jit(solution)/shard_map/ppermute | solution.py:253
  45.1 0.9 %collective-permute-done.11.got_ref = f32[32,512]{1,0:T(8,128)S(1)} collective-permute-done((f32[32,512]{1,0:T(8,128)S(1)}, f32[32,512]{1,0:T(8,128)S(1)}, u32[]{:S(2)}, u32[]{:S(2)}) %collective-permute-start.11) | collective-permute-done | bytes 65568 | tf_op jit(solution)/shard_map/ppermute | solution.py:253
  46.0 1.5 %close.1 = (f32[1,16,512]{2,1,0:T(8,128)}, f32[1,16,512]{2,1,0:T(8,128)}, f32[256,1,128]{2,1,0:T(1,128)S(1)}) custom-call(f32[32,512]{1,0:T(8,128)S(1)} %get-tuple-element.27.keep_ref, f32[32,512]{1,0:T(8,128)S(1)} %collective-permute-done.11.got_ref, s32[2,1,16,512]{3,2,1,0:T(8,128)S(1)} %copy-done.4, f32[2,1,16,512]{3,2,1,0:T(8,128)S(1)} %copy-done.5, ...), custom_call_target="tpu_custom_call" | custom-call | tf_op jit(solution)/shard_map/close/pallas_call | solution.py:277
  47.5 23.9 %all_to_all.5.terms_ref = f32[256,1,128]{2,1,0:T(1,128)S(1)} all-to-all(f32[256,1,128]{2,1,0:T(1,128)S(1)} %get-tuple-element.32), channel_id=1, replica_groups=mesh['dur'=32,'inc'=8] {'dur','inc'}, dimensions={0} | all-to-all | bytes 262144 | tf_op jit(solution)/shard_map/all_to_all | solution.py:284
  71.4 0.9 %demand.1 = f32[2]{0:T(128)} custom-call(f32[256,1,128]{2,1,0:T(1,128)S(1)} %all_to_all.5.terms_ref), custom_call_target="tpu_custom_call" | custom-call | tf_op jit(solution)/shard_map/demand/pallas_call | solution.py:285
  (22 shorter events, 0.1 us)
Async XLA Ops:
  0.6 11.3 %copy-start.8 = (f32[1,16,512]{2,1,0:T(8,128)S(1)}, f32[1,16,512]{2,1,0:T(8,128)}, u32[]{:S(2)}) copy-start(f32[1,16,512]{2,1,0:T(8,128)} %value_ref.3) | copy-start | bytes 98308
  2.4 5.7 %collective-permute-start = (f32[32,512]{1,0:T(8,128)S(1)}, f32[32,512]{1,0:T(8,128)S(1)}, u32[]{:S(2)}, u32[]{:S(2)}) collective-permute-start(f32[32,512]{1,0:T(8,128)S(1)} %get-tuple-element.19), channel_id=1, source_target_pairs={{0,8},{8,16},{16,24},{24,32},{32,40},{40,48},{48,56},{56,64},{64,7... | collective-permute-start | bytes 196616 | tf_op jit(solution)/shard_map/ppermute | solution.py:239
  6.8 5.2 %collective-permute-start.1 = (f32[32,512]{1,0:T(8,128)S(1)}, f32[32,512]{1,0:T(8,128)S(1)}, u32[]{:S(2)}, u32[]{:S(2)}) collective-permute-start(f32[32,512]{1,0:T(8,128)S(1)} %get-tuple-element.20), channel_id=1, source_target_pairs={{8,0},{16,8},{24,16},{32,24},{40,32},{48,40},{56,48},{64,56},{72,6... | collective-permute-start | bytes 196616 | tf_op jit(solution)/shard_map/ppermute | solution.py:240
  12.0 3.7 %copy-start.9 = (f32[128,128]{1,0:T(8,128)S(1)}, f32[128,128]{1,0:T(8,128)}, u32[]{:S(2)}) copy-start(f32[128,128]{1,0:T(8,128)} %markov_ref.1) | copy-start | bytes 196612
  12.0 12.5 %copy-start.7 = (f32[1,16,512]{2,1,0:T(8,128)S(1)}, f32[1,16,512]{2,1,0:T(8,128)}, u32[]{:S(2)}) copy-start(f32[1,16,512]{2,1,0:T(8,128)} %energy_ref.3) | copy-start | bytes 98308
  12.0 3.9 %collective-permute-start.4 = (f32[32,512]{1,0:T(8,128)S(1)}, f32[32,512]{1,0:T(8,128)S(1)}, u32[]{:S(2)}, u32[]{:S(2)}) collective-permute-start(f32[32,512]{1,0:T(8,128)S(1)} %merge.2.own_ref), channel_id=1, source_target_pairs={{0,6},{1,7},{2,0},{3,1},{4,2},{5,3},{6,4},{7,5},{8,14},{9,15},{10,... | collective-permute-start | bytes 196616 | tf_op jit(solution)/shard_map/ppermute | solution.py:244
  14.5 4.7 %collective-permute-start.3 = (f32[32,512]{1,0:T(8,128)S(1)}, f32[32,512]{1,0:T(8,128)S(1)}, u32[]{:S(2)}, u32[]{:S(2)}) collective-permute-start(f32[32,512]{1,0:T(8,128)S(1)} %merge.2.own_ref), channel_id=1, source_target_pairs={{0,4},{1,5},{2,6},{3,7},{4,0},{5,1},{6,2},{7,3},{8,12},{9,13},{10,... | collective-permute-start | bytes 196616 | tf_op jit(solution)/shard_map/ppermute | solution.py:244
  15.1 4.8 %collective-permute-start.2 = (f32[32,512]{1,0:T(8,128)S(1)}, f32[32,512]{1,0:T(8,128)S(1)}, u32[]{:S(2)}, u32[]{:S(2)}) collective-permute-start(f32[32,512]{1,0:T(8,128)S(1)} %merge.2.own_ref), channel_id=1, source_target_pairs={{0,2},{1,3},{2,4},{3,5},{4,6},{5,7},{6,0},{7,1},{8,10},{9,11},{10,... | collective-permute-start | bytes 196616 | tf_op jit(solution)/shard_map/ppermute | solution.py:244
  15.7 8.8 %copy-start.4 = (s32[2,1,16,512]{3,2,1,0:T(8,128)S(1)}, s32[2,1,16,512]{3,2,1,0:T(8,128)}, u32[]{:S(2)}) copy-start(s32[2,1,16,512]{3,2,1,0:T(8,128)} %bracket_ref.5) | copy-start | bytes 196612
  15.7 8.8 %copy-start.5 = (f32[2,1,16,512]{3,2,1,0:T(8,128)S(1)}, f32[2,1,16,512]{3,2,1,0:T(8,128)}, u32[]{:S(2)}) copy-start(f32[2,1,16,512]{3,2,1,0:T(8,128)} %lam_ref.3) | copy-start | bytes 196612
  15.8 8.7 %copy-start = (s32[2,1,16,512]{3,2,1,0:T(8,128)S(1)}, s32[2,1,16,512]{3,2,1,0:T(8,128)}, u32[]{:S(2)}) copy-start(s32[2,1,16,512]{3,2,1,0:T(8,128)} %fwd_bracket_ref.1) | copy-start | bytes 196612
  15.8 8.7 %copy-start.1 = (f32[2,1,16,512]{3,2,1,0:T(8,128)S(1)}, f32[2,1,16,512]{3,2,1,0:T(8,128)}, u32[]{:S(2)}) copy-start(f32[2,1,16,512]{3,2,1,0:T(8,128)} %fwd_weight_ref.1) | copy-start | bytes 196612
  15.8 8.7 %copy-start.2 = (s32[2,1,16,512]{3,2,1,0:T(8,128)S(1)}, s32[2,1,16,512]{3,2,1,0:T(8,128)}, u32[]{:S(2)}) copy-start(s32[2,1,16,512]{3,2,1,0:T(8,128)} %step_ref.3) | copy-start | bytes 196612
  15.8 8.7 %copy-start.3 = (f32[2,1,16,512]{3,2,1,0:T(8,128)S(1)}, f32[2,1,16,512]{3,2,1,0:T(8,128)}, u32[]{:S(2)}) copy-start(f32[2,1,16,512]{3,2,1,0:T(8,128)} %omega_ref.3) | copy-start | bytes 196612
  20.1 4.3 %collective-permute-start.5 = (f32[32,512]{1,0:T(8,128)S(1)}, f32[32,512]{1,0:T(8,128)S(1)}, u32[]{:S(2)}, u32[]{:S(2)}) collective-permute-start(f32[32,512]{1,0:T(8,128)S(1)} %get-tuple-element.22), channel_id=1, source_target_pairs={{0,1},{1,0},{2,3},{3,2},{4,5},{5,4},{6,7},{7,6},{8,9},{9,8},{10,11... | collective-permute-start | bytes 196616 | tf_op jit(solution)/shard_map/ppermute | solution.py:253
  26.0 4.9 %collective-permute-start.6 = (f32[32,512]{1,0:T(8,128)S(1)}, f32[32,512]{1,0:T(8,128)S(1)}, u32[]{:S(2)}, u32[]{:S(2)}) collective-permute-start(f32[32,512]{1,0:T(8,128)S(1)} %get-tuple-element.25), channel_id=1, source_target_pairs={{0,8},{8,16},{16,24},{24,32},{32,40},{40,48},{48,56},{56,64},{64,7... | collective-permute-start | bytes 196616 | tf_op jit(solution)/shard_map/ppermute | solution.py:239
  29.5 6.3 %collective-permute-start.7 = (f32[32,512]{1,0:T(8,128)S(1)}, f32[32,512]{1,0:T(8,128)S(1)}, u32[]{:S(2)}, u32[]{:S(2)}) collective-permute-start(f32[32,512]{1,0:T(8,128)S(1)} %get-tuple-element.26), channel_id=1, source_target_pairs={{8,0},{16,8},{24,16},{32,24},{40,32},{48,40},{56,48},{64,56},{72,6... | collective-permute-start | bytes 196616 | tf_op jit(solution)/shard_map/ppermute | solution.py:240
  35.9 10.1 %copy-start.6 = (f32[1,16,512]{2,1,0:T(8,128)S(1)}, f32[1,16,512]{2,1,0:T(8,128)}, u32[]{:S(2)}) copy-start(f32[1,16,512]{2,1,0:T(8,128)} %mass_ref.3) | copy-start | bytes 98308
  35.9 3.2 %collective-permute-start.10 = (f32[32,512]{1,0:T(8,128)S(1)}, f32[32,512]{1,0:T(8,128)S(1)}, u32[]{:S(2)}, u32[]{:S(2)}) collective-permute-start(f32[32,512]{1,0:T(8,128)S(1)} %merge.3.own_ref), channel_id=1, source_target_pairs={{0,6},{1,7},{2,0},{3,1},{4,2},{5,3},{6,4},{7,5},{8,14},{9,15},{10,... | collective-permute-start | bytes 196616 | tf_op jit(solution)/shard_map/ppermute | solution.py:244
  36.2 4.6 %collective-permute-start.9 = (f32[32,512]{1,0:T(8,128)S(1)}, f32[32,512]{1,0:T(8,128)S(1)}, u32[]{:S(2)}, u32[]{:S(2)}) collective-permute-start(f32[32,512]{1,0:T(8,128)S(1)} %merge.3.own_ref), channel_id=1, source_target_pairs={{0,4},{1,5},{2,6},{3,7},{4,0},{5,1},{6,2},{7,3},{8,12},{9,13},{10,... | collective-permute-start | bytes 196616 | tf_op jit(solution)/shard_map/ppermute | solution.py:244
  37.1 4.5 %collective-permute-start.8 = (f32[32,512]{1,0:T(8,128)S(1)}, f32[32,512]{1,0:T(8,128)S(1)}, u32[]{:S(2)}, u32[]{:S(2)}) collective-permute-start(f32[32,512]{1,0:T(8,128)S(1)} %merge.3.own_ref), channel_id=1, source_target_pairs={{0,2},{1,3},{2,4},{3,5},{4,6},{5,7},{6,0},{7,1},{8,10},{9,11},{10,... | collective-permute-start | bytes 196616 | tf_op jit(solution)/shard_map/ppermute | solution.py:244
  41.8 4.2 %collective-permute-start.11 = (f32[32,512]{1,0:T(8,128)S(1)}, f32[32,512]{1,0:T(8,128)S(1)}, u32[]{:S(2)}, u32[]{:S(2)}) collective-permute-start(f32[32,512]{1,0:T(8,128)S(1)} %get-tuple-element.28), channel_id=1, source_target_pairs={{0,1},{1,0},{2,3},{3,2},{4,5},{5,4},{6,7},{7,6},{8,9},{9,8},{10,11... | collective-permute-start | bytes 196616 | tf_op jit(solution)/shard_map/ppermute | solution.py:253

commit v3 on v2

v3 whole, which is shorter than its diff:
```python
import functools

import jax
import jax.numpy as jnp
from jax import lax
from jax.experimental import pallas as pl
from jax.experimental.pallas import tpu as pltpu
from jax.sharding import Mesh, PartitionSpec as P

discount = 0.985
gross_rate = 1.01
adjust_share = 0.3

LANES = 128
SHIFTS = (0, 1, 3, 2)
F32 = jnp.float32
BF16 = jnp.bfloat16
VMEM = pl.BlockSpec(memory_space=pltpu.VMEM)
SMEM = pl.BlockSpec(memory_space=pltpu.SMEM)


def in_vmem(*arrays):
    return tuple(pltpu.with_memory_space_constraint(x, pltpu.VMEM) for x in arrays)


def split_bf16(x):
    high = x.astype(BF16)
    return high, (x - high.astype(F32)).astype(BF16)


def bracket_read(mixed, bracket, weight):
    rows, assets = mixed.shape
    upper = pltpu.roll(mixed, assets - 1, 1)
    chunk_of = bracket >> 7
    lane_of = bracket & (LANES - 1)
    pieces = []
    for out in range(assets // LANES):
        span = slice(out * LANES, (out + 1) * LANES)
        lane, chunk = lane_of[:, span], chunk_of[:, span]
        low = high = None
        for source in range(assets // LANES):
            table = slice(source * LANES, (source + 1) * LANES)
            got_low = jnp.take_along_axis(mixed[:, table], lane, axis=1, mode="promise_in_bounds")
            got_high = jnp.take_along_axis(upper[:, table], lane, axis=1, mode="promise_in_bounds")
            low = got_low if source == 0 else jnp.where(chunk == source, got_low, low)
            high = got_high if source == 0 else jnp.where(chunk == source, got_high, high)
        lam = weight[:, span]
        pieces.append((1.0 - lam) * low + lam * high)
    return jnp.concatenate(pieces, axis=1)


def push_assets(density, bracket, weight, parts_ref, sums_ref):
    rows, assets = density.shape
    chunks = assets // LANES
    chunk_of = bracket >> 7
    lane_of = bracket & (LANES - 1)
    share = weight * density
    stay = density - share
    parts = []
    for value in (stay, share):
        high, low = split_bf16(value)
        parts += [high.astype(F32), low.astype(F32)]
    for k, part in enumerate(parts):
        parts_ref[k] = part
    height = 4 * chunks
    place = lax.broadcasted_iota(jnp.int32, (height, assets), 0)
    lane_iota = lax.broadcasted_iota(jnp.int32, (LANES, assets), 0)
    for r in range(rows):
        picked = jnp.broadcast_to(parts_ref[3, r : r + 1, :], (height, assets))
        for k in (2, 1, 0):
            picked = jnp.where(
                place < (k + 1) * chunks, jnp.broadcast_to(parts_ref[k, r : r + 1, :], (height, assets)), picked
            )
        left = jnp.where((place & (chunks - 1)) == chunk_of[r : r + 1, :], picked, 0.0).astype(BF16)
        right = jnp.where(lane_iota == lane_of[r : r + 1, :], 1.0, 0.0).astype(BF16)
        sums_ref[r * height : (r + 1) * height, :] = lax.dot_general(
            left, right, (((1,), (1,)), ((), ())), preferred_element_type=F32
        )

    def gathered(k, h):
        return sums_ref[pl.ds(k * chunks + h, rows, stride=height), :]

    stayed = jnp.concatenate([gathered(0, h) + gathered(1, h) for h in range(chunks)], axis=1)
    shared = jnp.concatenate([gathered(2, h) + gathered(3, h) for h in range(chunks)], axis=1)
    return stayed + pltpu.roll(shared, 1, 1)


def level_shares(moved, step, omega):
    level = lax.axis_index("dur")
    total = lax.axis_size("dur")
    lower = jnp.clip(level + step, 0, total - 2)
    down = lower - level == -1
    upper_part = moved * omega
    lower_part = moved - upper_part
    to_self = jnp.where(down, upper_part, lower_part)
    to_minus = jnp.where(down, lower_part, 0.0)
    to_plus = jnp.where(down, 0.0, upper_part)
    return to_self, to_plus, to_minus


def store_halo(pair_ref, other_ref, to_plus, to_minus, value):
    rows = value.shape[0]
    even = lax.axis_index("dur") % 2 == 0
    pair_ref[:rows, :] = jnp.where(even, to_plus, to_minus)
    other_ref[:rows, :] = jnp.where(even, to_minus, to_plus)
    pair_ref[rows:, :] = value
    other_ref[rows:, :] = value


def weights_kernel(markov_ref, back_ref, ahead_ref, flip_ref):
    chip = lax.axis_index("x")
    states = markov_ref.shape[0]
    wide = ahead_ref.shape[0] // 2
    flip_ref[...] = markov_ref[...].T
    high, low = split_bf16(discount * markov_ref[...])
    back_ref[:states, :] = high
    back_ref[states:, :] = low
    high, low = split_bf16(flip_ref[pl.ds(pl.multiple_of(chip * wide, wide), wide), :])
    ahead_ref[:wide, :] = high
    ahead_ref[wide:, :] = low


def open_kernel(
    scale, value_ref, mass_ref, bracket_ref, weight_ref, step_ref, omega_ref, energy_ref, bwd_bracket_ref, lam_ref,
    tax_ref, pair_ref, other_ref, self_ref, fixed_ref, parts_ref, sums_ref,
):
    rows = self_ref.shape[0]
    moved = push_assets(mass_ref[0], bracket_ref[0, 0], weight_ref[0, 0], parts_ref, sums_ref)
    to_self, to_plus, to_minus = level_shares(moved, step_ref[0, 0], omega_ref[0, 0])
    self_ref[...] = to_self
    store_halo(pair_ref, other_ref, to_plus, to_minus, value_ref[0])
    fixed_ref[:rows, :] = scale * mass_ref[0] * energy_ref[0] / (1.0 + tax_ref[0])
    fixed_ref[rows : 2 * rows, :] = bwd_bracket_ref[0, 0].astype(F32)
    fixed_ref[2 * rows :, :] = lam_ref[0, 0]


def merge_kernel(self_ref, value_ref, other_ref, pair_ref, rider_ref, out_ref):
    rows = self_ref.shape[0]
    level = lax.axis_index("dur")
    value = value_ref[...].reshape(self_ref.shape)
    alone = (level == 0) | (level == lax.axis_size("dur") - 1)
    beside = pair_ref[rows:, :] + jnp.where(alone, value, other_ref[rows:, :])
    incoming = pair_ref[:rows, :] + jnp.where(alone, 0.0, other_ref[:rows, :])
    out_ref[:rows, :] = self_ref[...] + incoming
    out_ref[rows : 2 * rows, :] = (1.0 - adjust_share) * value + adjust_share * 0.5 * beside
    out_ref[2 * rows :, :] = rider_ref[...]


def place_field(refs, part, rows, field_ref):
    chip, core = lax.axis_index("x"), lax.axis_index("core")
    field_ref[...] = jnp.zeros_like(field_ref)
    for shift, ref in zip(SHIFTS, refs):
        at = pl.ds(pl.multiple_of((chip ^ shift) * 2 * rows + core * rows, rows), rows)
        field_ref[at, :] = ref[part * rows : (part + 1) * rows, :]
    return split_bf16(field_ref[...])


def product(factor_high, factor_low, high, low):
    count = factor_high.shape[0]
    both = jnp.dot(jnp.concatenate([factor_high, factor_low], axis=0), high, preferred_element_type=F32)
    return both[:count] + (both[count:] + jnp.dot(factor_high, low, preferred_element_type=F32))


def markov_kernel(
    own_ref, one_ref, two_ref, three_ref, back_ref, ahead_ref, keep_ref, send_ref, field_ref, total_ref
):
    refs = (own_ref, one_ref, two_ref, three_ref)
    chip, core = lax.axis_index("x"), lax.axis_index("core")
    states = back_ref.shape[0] // 2
    wide = ahead_ref.shape[0] // 2
    rows = wide // 2
    mine = pl.ds(pl.multiple_of(core * rows, rows), rows)
    theirs = pl.ds(pl.multiple_of((1 - core) * rows, rows), rows)
    total_ref[:wide, :] = product(ahead_ref[:wide, :], ahead_ref[wide:, :], *place_field(refs, 0, rows, field_ref))
    keep_ref[:rows, :] = total_ref[mine, :]
    send_ref[:rows, :] = total_ref[theirs, :]
    at = pl.multiple_of(chip * wide, wide)
    total_ref[:wide, :] = product(
        back_ref[pl.ds(at, wide), :],
        back_ref[pl.ds(states + at, wide), :],
        *place_field(refs, 1, rows, field_ref),
    )
    keep_ref[rows:, :] = total_ref[mine, :]
    send_ref[rows:, :] = total_ref[theirs, :]


def markov_wide_kernel(
    own_ref, one_ref, two_ref, three_ref, back_ref, ahead_ref, keep_ref, send_ref, demand_ref, field_ref, total_ref,
    terms_ref,
):
    refs = (own_ref, one_ref, two_ref, three_ref)
    chip, core = lax.axis_index("x"), lax.axis_index("core")
    states = back_ref.shape[0] // 2
    wide = ahead_ref.shape[0] // 2
    rows = wide // 2
    mine = pl.ds(pl.multiple_of(core * rows, rows), rows)
    theirs = pl.ds(pl.multiple_of((1 - core) * rows, rows), rows)
    total_ref[:wide, :] = product(ahead_ref[:wide, :], ahead_ref[wide:, :], *place_field(refs, 0, rows, field_ref))
    keep_ref[:rows, :] = total_ref[mine, :]
    send_ref[:rows, :] = total_ref[theirs, :]
    total_ref[...] = product(back_ref[:states, :], back_ref[states:, :], *place_field(refs, 1, rows, field_ref))
    for k in range(len(refs)):
        part = slice((k + 1) * rows, (k + 2) * rows)
        keep_ref[part, :] = total_ref[pl.ds(pl.multiple_of(k * wide + core * rows, rows), rows), :]
        send_ref[part, :] = total_ref[pl.ds(pl.multiple_of(k * wide + (1 - core) * rows, rows), rows), :]
    for shift, ref in zip(SHIFTS, refs):
        terms_ref[chip ^ shift] = ref[2 * rows :, :]
    demand_ref[...] = (terms_ref[0] + terms_ref[1]) + (terms_ref[2] + terms_ref[3])


def turn_kernel(
    scale, keep_ref, got_ref, bracket_ref, lam_ref, energy_ref, tax_ref, fwd_bracket_ref, fwd_weight_ref, step_ref,
    omega_ref, pair_ref, other_ref, self_ref, value_ref, demand_ref, parts_ref, sums_ref,
):
    rows = self_ref.shape[0]
    density = keep_ref[:rows, :] + got_ref[:rows, :]
    mixed = keep_ref[rows:, :] + got_ref[rows:, :]
    interp = bracket_read(mixed, bracket_ref[1, 0], lam_ref[1, 0])
    tax = tax_ref[1]
    share = energy_ref[0]
    spent = density * (share * lax.rsqrt(interp))
    half = demand_ref.shape[0]
    demand_ref[...] = (scale / (1.0 + tax)) * sum(spent[k : k + half] for k in range(0, rows, half))
    value = gross_rate * interp * (1.0 + tax * share)
    moved = push_assets(density, fwd_bracket_ref[1, 0], fwd_weight_ref[1, 0], parts_ref, sums_ref)
    to_self, to_plus, to_minus = level_shares(moved, step_ref[1, 0], omega_ref[1, 0])
    self_ref[...] = to_self
    value_ref[...] = value
    store_halo(pair_ref, other_ref, to_plus, to_minus, value)


def close_kernel(
    keep_ref, got_ref, own_ref, one_ref, two_ref, three_ref, energy_ref, tax_ref, demand_ref,
    value_ref, mass_ref, terms_ref, fixed_ref, interp_ref,
):
    rows = energy_ref.shape[1]
    chip = lax.axis_index("x")
    refs = (own_ref, one_ref, two_ref, three_ref)
    for shift, ref in zip(SHIFTS, refs):
        fixed_ref[chip ^ shift] = ref[2 * rows :, :]
    spent = []
    for k in range(len(refs)):
        part = slice((k + 1) * rows, (k + 2) * rows)
        bracket = fixed_ref[k, rows : 2 * rows, :].astype(jnp.int32)
        interp = bracket_read(keep_ref[part, :] + got_ref[part, :], bracket, fixed_ref[k, 2 * rows :, :])
        interp_ref[k] = interp
        spent.append(fixed_ref[k, :rows, :] * lax.rsqrt(interp))
    first = jnp.sum((spent[0] + spent[1]) + (spent[2] + spent[3]))
    second = jnp.sum(demand_ref[...])
    lane = lax.broadcasted_iota(jnp.int32, terms_ref.shape, 2)
    terms_ref[...] = jnp.where(lane == 0, first, second)
    mass_ref[0] = keep_ref[:rows, :] + got_ref[:rows, :]
    value_ref[0] = gross_rate * interp_ref[chip] * (1.0 + tax_ref[0] * energy_ref[0])


def demand_kernel(terms_ref, out_ref):
    out_ref[...] = jnp.sum(terms_ref[...], axis=0)[0, : out_ref.shape[0]]


def per_device(
    value_next,
    markov,
    energy_share,
    bwd_bracket,
    bwd_weight,
    fwd_bracket,
    fwd_weight,
    dur_step,
    dur_weight,
    mass_start,
    tax,
):
    _, rows, assets = value_next.shape
    states = markov.shape[0]
    levels, chips, cores = (lax.axis_size(axis) for axis in ("dur", "x", "core"))
    scale = 1.0 / (levels * states * assets)
    chunks = assets // LANES
    slab = pltpu.VMEM((rows, assets), F32)
    pair = pltpu.VMEM((2 * rows, assets), F32)
    block = jax.ShapeDtypeStruct((1, rows, assets), F32)
    eight = pltpu.VMEM((8, assets), F32)
    push_scratch = [pltpu.VMEM((4, rows, assets), F32), pltpu.VMEM((rows * 4 * chunks, LANES), F32)]
    pairs = [(i, i ^ 1) for i in range(levels)]
    others = [(i, ((i + 1) ^ 1) - 1) for i in range(1, levels - 1)]

    def over_chips(array):
        return [lax.ppermute(array, "x", [(i, i ^ k) for i in range(chips)]) for k in SHIFTS[1:]]

    def over_cores(array):
        return lax.ppermute(array, "core", [(i, i ^ 1) for i in range(cores)])

    def over_levels(pair_out, other_out):
        other_in = lax.ppermute(other_out, "dur", others)
        return other_in, lax.ppermute(pair_out, "dur", pairs)

    weights = pl.pallas_call(
        weights_kernel,
        out_shape=(pltpu.VMEM((2 * states, states), BF16), pltpu.VMEM((4 * rows, states), BF16)),
        in_specs=[VMEM],
        out_specs=(VMEM, VMEM),
        scratch_shapes=[pltpu.VMEM((states, states), F32)],
        name="weights",
    )(*in_vmem(markov))
    pair_out, other_out, kept, fixed = pl.pallas_call(
        functools.partial(open_kernel, scale),
        out_shape=(pair, pair, slab, pltpu.VMEM((3 * rows, assets), F32)),
        in_specs=[VMEM] * 9 + [SMEM],
        out_specs=(VMEM,) * 4,
        scratch_shapes=push_scratch,
        name="open",
    )(
        value_next, mass_start, fwd_bracket, fwd_weight, dur_step, dur_weight, energy_share, bwd_bracket, bwd_weight, tax
    )
    halo = over_levels(pair_out, other_out)
    mine = pl.pallas_call(
        merge_kernel,
        out_shape=pltpu.VMEM((5 * rows, assets), F32),
        in_specs=[VMEM] * 5,
        out_specs=VMEM,
        name="merge_with_fixed",
    )(*in_vmem(kept, value_next, *halo, fixed))
    every_first = [mine] + over_chips(mine)
    keep, send = pl.pallas_call(
        markov_kernel,
        out_shape=(pair, pair),
        in_specs=[VMEM] * 6,
        out_specs=(VMEM, VMEM),
        scratch_shapes=[pltpu.VMEM((states, assets), F32), pltpu.VMEM((2 * rows, assets), F32)],
        name="markov",
    )(*in_vmem(*every_first, *weights))
    pair_out, other_out, kept, value, second = pl.pallas_call(
        functools.partial(turn_kernel, scale),
        out_shape=(pair, pair, slab, slab, eight),
        in_specs=[VMEM] * 5 + [SMEM] + [VMEM] * 4,
        out_specs=(VMEM,) * 5,
        scratch_shapes=push_scratch,
        name="turn",
    )(
        *in_vmem(keep, over_cores(send), bwd_bracket, bwd_weight, energy_share),
        tax,
        *in_vmem(fwd_bracket, fwd_weight, dur_step, dur_weight),
    )
    halo = over_levels(pair_out, other_out)
    mine = pl.pallas_call(
        merge_kernel,
        out_shape=pltpu.VMEM((2 * rows + 8, assets), F32),
        in_specs=[VMEM] * 5,
        out_specs=VMEM,
        name="merge_with_demand",
    )(*in_vmem(kept, value, *halo, second))
    wide = pltpu.VMEM(((1 + chips) * rows, assets), F32)
    keep, send, second = pl.pallas_call(
        markov_wide_kernel,
        out_shape=(wide, wide, eight),
        in_specs=[VMEM] * 6,
        out_specs=(VMEM,) * 3,
        scratch_shapes=[
            pltpu.VMEM((states, assets), F32),
            pltpu.VMEM((states, assets), F32),
            pltpu.VMEM((chips, 8, assets), F32),
        ],
        name="markov_wide",
    )(*in_vmem(mine, *over_chips(mine), *weights))
    value_start, mass_end, terms = pl.pallas_call(
        close_kernel,
        out_shape=(block, block, pltpu.VMEM((levels * cores, 1, LANES), F32)),
        in_specs=[VMEM] * 7 + [SMEM, VMEM],
        out_specs=(VMEM,) * 3,
        scratch_shapes=[pltpu.VMEM((chips, 3 * rows, assets), F32), pltpu.VMEM((chips, rows, assets), F32)],
        name="close",
    )(*in_vmem(keep, over_cores(send), *every_first, energy_share), tax, *in_vmem(second))
    every_term = lax.all_to_all(terms, ("dur", "core"), 0, 0)
    demand = pl.pallas_call(
        demand_kernel,
        out_shape=jax.ShapeDtypeStruct((2,), F32),
        in_specs=[VMEM],
        out_specs=VMEM,
        name="demand",
    )(*in_vmem(every_term))
    return (value_start, mass_end, demand)


def solution(mesh):
    levels, incs = mesh.devices.shape
    mesh = Mesh(mesh.devices.reshape(levels, incs // 2, 2), ("dur", "x", "core"))
    inc = ("x", "core")
    return jax.shard_map(
        per_device,
        mesh=mesh,
        in_specs=(
            P("dur", inc, None),
            P(),
            P("dur", inc, None),
            P(None, "dur", inc, None),
            P(None, "dur", inc, None),
            P(None, "dur", inc, None),
            P(None, "dur", inc, None),
            P(None, "dur", inc, None),
            P(None, "dur", inc, None),
            P("dur", inc, None),
            P(),
        ),
        out_specs=(P("dur", inc, None), P("dur", inc, None), P()),
        check_vma=False,
    )
```

time: 72.6 us -> 66.9 us (0.921)
  blocking collectives: 23.9 us -> 19.2 us
  waiting for transfers between devices: 18.4 us -> 16.6 us
    all_to_all x1, blocking collectives: 23.9 us -> 19.2 us  [per_device(): every_term = lax.all_to_all(terms, ('dur', 'core'), 0, 0)]
    ppermute x12, waiting for transfers between devices: 18.4 us -> 16.6 us  [the longest x6 11.4 us: over_chips(): lax.ppermute(array, 'x', [(i, i ^ k) for i in range(chips)])]
    pallas_call x8, Pallas kernels: 5.35 us -> 6.19 us  [the longest x1 2.15 us: per_device(): pl.pallas_call(close_kernel, out_shape=(block, block, pltpu.VMEM((levels...]
where the time goes in v3:
time: 66.9 us; the launch traced here: 66.7 us
  starting transfers between devices  23.3 us (35%)
  blocking collectives  19.2 us (29%)
  waiting for transfers between devices  16.6 us (25%)
  Pallas kernels  6.77 us (10%)
  between operations  0.77 us (1%)
    all_to_all x1, blocking collectives, per_device(): every_term = lax.all_to_all(terms, ('dur', 'core'), 0, 0)  19.2 us
    ppermute x6, waiting for transfers between devices, over_chips(): lax.ppermute(array, 'x', [(i, i ^ k) for i in range(chips)])  11.4 us
    ppermute x2, starting transfers between devices, over_levels(): return (other_in, lax.ppermute(pair_out, 'dur', pairs))  11.2 us
    ppermute x6, starting transfers between devices, over_chips(): lax.ppermute(array, 'x', [(i, i ^ k) for i in range(chips)])  6.92 us
    ppermute x2, starting transfers between devices, over_cores(): return lax.ppermute(array, 'core', [(i, i ^ 1) for i in range(cores)])  3.76 us
    ppermute x2, waiting for transfers between devices, over_levels(): return (other_in, lax.ppermute(pair_out, 'dur', pairs))  3.31 us
    pallas_call x1, Pallas kernels, per_device(): pl.pallas_call(close_kernel, out_shape=(block, block, pltpu.VMEM((levels...  2.15 us
    ppermute x2, waiting for transfers between devices, over_cores(): return lax.ppermute(array, 'core', [(i, i ^ 1) for i in range(cores)])  1.93 us
  transfers between devices with their start and end apart: 12, of which 9 were waited for; matrix products, arithmetic and copies ran while one was open for 0% of the time, Pallas kernels for 0%

profile of v3, /device:TPU:1, one launch (start us, length us, event | category | flops | bytes accessed | tf_op | source)
XLA Modules:
  0.0 66.7 jit_solution(2746159761049382582)
XLA Ops:
  0.6 1.8 %open.1 = (f32[32,512]{1,0:T(8,128)S(1)}, f32[32,512]{1,0:T(8,128)S(1)}, f32[16,512]{1,0:T(8,128)S(1)}, f32[48,512]{1,0:T(8,128)S(1)}) custom-call(f32[1,16,512]{2,1,0:T(8,128)} %value_ref.3, f32[1,16,512]{2,1,0:T(8,128)} %mass_ref.1, s32[2,1,16,512]{3,2,1,0:T(8,128)} %fwd_bracket_ref.1, f32[2,1,16,512]{3,2,1,0:T(8,128)} %fwd_weight_ref.1, ...), custom_call_target="tpu_custom_call" | custom-call | tf_op jit(solution)/shard_map/open/pallas_call | solution.py:304
  2.5 0.7 collective-permute-start
  3.1 5.4 %collective-permute-start.1 = (f32[32,512]{1,0:T(8,128)S(1)}, f32[32,512]{1,0:T(8,128)S(1)}, u32[]{:S(2)}, u32[]{:S(2)}) collective-permute-start(f32[32,512]{1,0:T(8,128)S(1)} %get-tuple-element.24), channel_id=1, source_target_pairs={{0,8},{8,0},{16,24},{24,16},{32,40},{40,32},{48,56},{56,48},{64,72... | collective-permute-start | bytes 196616 | tf_op jit(solution)/shard_map/ppermute | solution.py:294
  8.6 1.7 %collective-permute-done.1.pair_ref = f32[32,512]{1,0:T(8,128)S(1)} collective-permute-done((f32[32,512]{1,0:T(8,128)S(1)}, f32[32,512]{1,0:T(8,128)S(1)}, u32[]{:S(2)}, u32[]{:S(2)}) %collective-permute-start.1) | collective-permute-done | bytes 65568 | tf_op jit(solution)/shard_map/ppermute | solution.py:294
  10.3 2.8 %collective-permute-start.4 = (f32[80,512]{1,0:T(8,128)S(1)}, f32[80,512]{1,0:T(8,128)S(1)}, u32[]{:S(2)}, u32[]{:S(2)}) collective-permute-start(f32[80,512]{1,0:T(8,128)S(1)} %merge_with_fixed.1.own_ref), channel_id=1, source_target_pairs={{0,4},{2,6},{4,0},{6,2},{1,5},{3,7},{5,1},{7,3},{8,12},{10,14},{12... | collective-permute-start | bytes 491528 | tf_op jit(solution)/shard_map/ppermute | solution.py:287
  13.1 0.9 %collective-permute-start.3 = (f32[80,512]{1,0:T(8,128)S(1)}, f32[80,512]{1,0:T(8,128)S(1)}, u32[]{:S(2)}, u32[]{:S(2)}) collective-permute-start(f32[80,512]{1,0:T(8,128)S(1)} %merge_with_fixed.1.own_ref), channel_id=1, source_target_pairs={{0,6},{2,4},{4,2},{6,0},{1,7},{3,5},{5,3},{7,1},{8,14},{10,12},{12... | collective-permute-start | bytes 491528 | tf_op jit(solution)/shard_map/ppermute | solution.py:287
  14.0 0.0 collective-permute-start.2
  14.0 0.1 weights.1
  14.1 2.0 %collective-permute-done.4.three_ref = f32[80,512]{1,0:T(8,128)S(1)} collective-permute-done((f32[80,512]{1,0:T(8,128)S(1)}, f32[80,512]{1,0:T(8,128)S(1)}, u32[]{:S(2)}, u32[]{:S(2)}) %collective-permute-start.4) | collective-permute-done | bytes 163872 | tf_op jit(solution)/shard_map/ppermute | solution.py:287
  16.0 5.0 %collective-permute-done.3.two_ref = f32[80,512]{1,0:T(8,128)S(1)} collective-permute-done((f32[80,512]{1,0:T(8,128)S(1)}, f32[80,512]{1,0:T(8,128)S(1)}, u32[]{:S(2)}, u32[]{:S(2)}) %collective-permute-start.3) | collective-permute-done | bytes 163872 | tf_op jit(solution)/shard_map/ppermute | solution.py:287
  21.1 0.0 copy-start.3
  21.1 0.0 copy-start.4
  21.1 0.0 copy-start.5
  21.1 0.0 copy-start.6
  21.1 0.3 markov.1
  21.4 1.5 %collective-permute-start.5 = (f32[32,512]{1,0:T(8,128)S(1)}, f32[32,512]{1,0:T(8,128)S(1)}, u32[]{:S(2)}, u32[]{:S(2)}) collective-permute-start(f32[32,512]{1,0:T(8,128)S(1)} %get-tuple-element.29), channel_id=1, source_target_pairs={{0,1},{1,0},{2,3},{3,2},{4,5},{5,4},{6,7},{7,6},{8,9},{9,8},{10,11... | collective-permute-start | bytes 196616 | tf_op jit(solution)/shard_map/ppermute | solution.py:290
  22.9 0.9 %collective-permute-done.5.got_ref = f32[32,512]{1,0:T(8,128)S(1)} collective-permute-done((f32[32,512]{1,0:T(8,128)S(1)}, f32[32,512]{1,0:T(8,128)S(1)}, u32[]{:S(2)}, u32[]{:S(2)}) %collective-permute-start.5) | collective-permute-done | bytes 65568 | tf_op jit(solution)/shard_map/ppermute | solution.py:290
  23.9 1.4 %turn.1 = (f32[32,512]{1,0:T(8,128)S(1)}, f32[32,512]{1,0:T(8,128)S(1)}, f32[16,512]{1,0:T(8,128)S(1)}, f32[16,512]{1,0:T(8,128)S(1)}, f32[8,512]{1,0:T(8,128)S(1)}) custom-call(f32[32,512]{1,0:T(8,128)S(1)} %get-tuple-element.28.keep_ref, f32[32,512]{1,0:T(8,128)S(1)} %collective-permute-done.5.got_ref, s32[2,1,16,512]{3,2,1,0:T(8,128)S(1)} %copy-done.5, ...), custom_call_target="tpu_custom_call" | custom-call | tf_op jit(solution)/shard_map/turn/pallas_call | solution.py:331
  25.3 0.7 collective-permute-start.6
  26.0 5.8 %collective-permute-start.7 = (f32[32,512]{1,0:T(8,128)S(1)}, f32[32,512]{1,0:T(8,128)S(1)}, u32[]{:S(2)}, u32[]{:S(2)}) collective-permute-start(f32[32,512]{1,0:T(8,128)S(1)} %get-tuple-element.33), channel_id=1, source_target_pairs={{0,8},{8,0},{16,24},{24,16},{32,40},{40,32},{48,56},{56,48},{64,72... | collective-permute-start | bytes 196616 | tf_op jit(solution)/shard_map/ppermute | solution.py:294
  31.8 1.7 %collective-permute-done.7.pair_ref = f32[32,512]{1,0:T(8,128)S(1)} collective-permute-done((f32[32,512]{1,0:T(8,128)S(1)}, f32[32,512]{1,0:T(8,128)S(1)}, u32[]{:S(2)}, u32[]{:S(2)}) %collective-permute-start.7) | collective-permute-done | bytes 65568 | tf_op jit(solution)/shard_map/ppermute | solution.py:294
  33.5 1.4 %collective-permute-start.10 = (f32[40,512]{1,0:T(8,128)S(1)}, f32[40,512]{1,0:T(8,128)S(1)}, u32[]{:S(2)}, u32[]{:S(2)}) collective-permute-start(f32[40,512]{1,0:T(8,128)S(1)} %merge_with_demand.1.own_ref), channel_id=1, source_target_pairs={{0,4},{2,6},{4,0},{6,2},{1,5},{3,7},{5,1},{7,3},{8,12},{10,14},{12... | collective-permute-start | bytes 245768 | tf_op jit(solution)/shard_map/ppermute | solution.py:287
  34.9 1.8 %collective-permute-start.9 = (f32[40,512]{1,0:T(8,128)S(1)}, f32[40,512]{1,0:T(8,128)S(1)}, u32[]{:S(2)}, u32[]{:S(2)}) collective-permute-start(f32[40,512]{1,0:T(8,128)S(1)} %merge_with_demand.1.own_ref), channel_id=1, source_target_pairs={{0,6},{2,4},{4,2},{6,0},{1,7},{3,5},{5,3},{7,1},{8,14},{10,12},{12... | collective-permute-start | bytes 245768 | tf_op jit(solution)/shard_map/ppermute | solution.py:287
  36.7 1.7 %collective-permute-done.10.three_ref = f32[40,512]{1,0:T(8,128)S(1)} collective-permute-done((f32[40,512]{1,0:T(8,128)S(1)}, f32[40,512]{1,0:T(8,128)S(1)}, u32[]{:S(2)}, u32[]{:S(2)}) %collective-permute-start.10) | collective-permute-done | bytes 81952 | tf_op jit(solution)/shard_map/ppermute | solution.py:287
  38.4 1.1 %collective-permute-done.9.two_ref = f32[40,512]{1,0:T(8,128)S(1)} collective-permute-done((f32[40,512]{1,0:T(8,128)S(1)}, f32[40,512]{1,0:T(8,128)S(1)}, u32[]{:S(2)}, u32[]{:S(2)}) %collective-permute-start.9) | collective-permute-done | bytes 81952 | tf_op jit(solution)/shard_map/ppermute | solution.py:287
  39.4 1.6 %collective-permute-done.8.one_ref = f32[40,512]{1,0:T(8,128)S(1)} collective-permute-done((f32[40,512]{1,0:T(8,128)S(1)}, f32[40,512]{1,0:T(8,128)S(1)}, u32[]{:S(2)}, u32[]{:S(2)}) %collective-permute-start.8) | collective-permute-done | bytes 81952 | tf_op jit(solution)/shard_map/ppermute | solution.py:287
  41.1 0.4 markov_wide.1
  41.4 2.2 %collective-permute-start.11 = (f32[80,512]{1,0:T(8,128)S(1)}, f32[80,512]{1,0:T(8,128)S(1)}, u32[]{:S(2)}, u32[]{:S(2)}) collective-permute-start(f32[80,512]{1,0:T(8,128)S(1)} %get-tuple-element.36), channel_id=1, source_target_pairs={{0,1},{1,0},{2,3},{3,2},{4,5},{5,4},{6,7},{7,6},{8,9},{9,8},{10,11... | collective-permute-start | bytes 491528 | tf_op jit(solution)/shard_map/ppermute | solution.py:290
  43.7 1.0 %collective-permute-done.11.got_ref = f32[80,512]{1,0:T(8,128)S(1)} collective-permute-done((f32[80,512]{1,0:T(8,128)S(1)}, f32[80,512]{1,0:T(8,128)S(1)}, u32[]{:S(2)}, u32[]{:S(2)}) %collective-permute-start.11) | collective-permute-done | bytes 163872 | tf_op jit(solution)/shard_map/ppermute | solution.py:290
  44.7 2.2 %close.1 = (f32[1,16,512]{2,1,0:T(8,128)}, f32[1,16,512]{2,1,0:T(8,128)}, f32[64,1,128]{2,1,0:T(1,128)S(1)}) custom-call(f32[80,512]{1,0:T(8,128)S(1)} %get-tuple-element.35.keep_ref, f32[80,512]{1,0:T(8,128)S(1)} %collective-permute-done.11.got_ref, f32[80,512]{1,0:T(8,128)S(1)} %merge_with_fixed.1.own_ref, f32[80,512]{1,0:T(8,128)S(1)} %collective-permute-done.2.one_ref, ...), custom_call_target="tpu_custom_call" | custom-call | tf_op jit(solution)/shard_map/close/pallas_call | solution.py:364
  46.9 19.2 %all_to_all.5.terms_ref = f32[64,1,128]{2,1,0:T(1,128)S(1)} all-to-all(f32[64,1,128]{2,1,0:T(1,128)S(1)} %get-tuple-element.40), channel_id=1, replica_groups=mesh['dur'=32,'x'=4,'core'=2] {'dur','core'}, dimensions={0} | all-to-all | bytes 65536 | tf_op jit(solution)/shard_map/all_to_all | solution.py:372
  66.1 0.6 demand.1
  (20 shorter events, 0.1 us)
Async XLA Ops:
  0.6 9.6 %copy-start.7 = (f32[1,16,512]{2,1,0:T(8,128)S(1)}, f32[1,16,512]{2,1,0:T(8,128)}, u32[]{:S(2)}) copy-start(f32[1,16,512]{2,1,0:T(8,128)} %value_ref.3) | copy-start | bytes 98308
  2.5 6.1 %collective-permute-start = (f32[32,512]{1,0:T(8,128)S(1)}, f32[32,512]{1,0:T(8,128)S(1)}, u32[]{:S(2)}, u32[]{:S(2)}) collective-permute-start(f32[32,512]{1,0:T(8,128)S(1)} %get-tuple-element.23), channel_id=1, source_target_pairs={{8,16},{16,8},{24,32},{32,24},{40,48},{48,40},{56,64},{64,56},{72,... | collective-permute-start | bytes 196616 | tf_op jit(solution)/shard_map/ppermute | solution.py:293
  3.1 7.1 %collective-permute-start.1 = (f32[32,512]{1,0:T(8,128)S(1)}, f32[32,512]{1,0:T(8,128)S(1)}, u32[]{:S(2)}, u32[]{:S(2)}) collective-permute-start(f32[32,512]{1,0:T(8,128)S(1)} %get-tuple-element.24), channel_id=1, source_target_pairs={{0,8},{8,0},{16,24},{24,16},{32,40},{40,32},{48,56},{56,48},{64,72... | collective-permute-start | bytes 196616 | tf_op jit(solution)/shard_map/ppermute | solution.py:294
  10.2 3.7 %copy-start.8 = (f32[128,128]{1,0:T(8,128)S(1)}, f32[128,128]{1,0:T(8,128)}, u32[]{:S(2)}) copy-start(f32[128,128]{1,0:T(8,128)} %markov_ref.1) | copy-start | bytes 196612
  10.3 5.8 %collective-permute-start.4 = (f32[80,512]{1,0:T(8,128)S(1)}, f32[80,512]{1,0:T(8,128)S(1)}, u32[]{:S(2)}, u32[]{:S(2)}) collective-permute-start(f32[80,512]{1,0:T(8,128)S(1)} %merge_with_fixed.1.own_ref), channel_id=1, source_target_pairs={{0,4},{2,6},{4,0},{6,2},{1,5},{3,7},{5,1},{7,3},{8,12},{10,14},{12... | collective-permute-start | bytes 491528 | tf_op jit(solution)/shard_map/ppermute | solution.py:287
  13.1 8.0 %collective-permute-start.3 = (f32[80,512]{1,0:T(8,128)S(1)}, f32[80,512]{1,0:T(8,128)S(1)}, u32[]{:S(2)}, u32[]{:S(2)}) collective-permute-start(f32[80,512]{1,0:T(8,128)S(1)} %merge_with_fixed.1.own_ref), channel_id=1, source_target_pairs={{0,6},{2,4},{4,2},{6,0},{1,7},{3,5},{5,3},{7,1},{8,14},{10,12},{12... | collective-permute-start | bytes 491528 | tf_op jit(solution)/shard_map/ppermute | solution.py:287
  14.0 7.1 %collective-permute-start.2 = (f32[80,512]{1,0:T(8,128)S(1)}, f32[80,512]{1,0:T(8,128)S(1)}, u32[]{:S(2)}, u32[]{:S(2)}) collective-permute-start(f32[80,512]{1,0:T(8,128)S(1)} %merge_with_fixed.1.own_ref), channel_id=1, source_target_pairs={{0,2},{2,0},{4,6},{6,4},{1,3},{3,1},{5,7},{7,5},{8,10},{10,8},{12,... | collective-permute-start | bytes 491528 | tf_op jit(solution)/shard_map/ppermute | solution.py:287
  21.1 2.8 %copy-start = (f32[1,16,512]{2,1,0:T(8,128)S(1)}, f32[1,16,512]{2,1,0:T(8,128)}, u32[]{:S(2)}) copy-start(f32[1,16,512]{2,1,0:T(8,128)} %energy_ref.5) | copy-start | bytes 98308
  21.1 2.8 %copy-start.1 = (s32[2,1,16,512]{3,2,1,0:T(8,128)S(1)}, s32[2,1,16,512]{3,2,1,0:T(8,128)}, u32[]{:S(2)}) copy-start(s32[2,1,16,512]{3,2,1,0:T(8,128)} %fwd_bracket_ref.1) | copy-start | bytes 196612
  21.1 2.8 %copy-start.2 = (f32[2,1,16,512]{3,2,1,0:T(8,128)S(1)}, f32[2,1,16,512]{3,2,1,0:T(8,128)}, u32[]{:S(2)}) copy-start(f32[2,1,16,512]{3,2,1,0:T(8,128)} %fwd_weight_ref.1) | copy-start | bytes 196612
  21.1 2.8 %copy-start.3 = (s32[2,1,16,512]{3,2,1,0:T(8,128)S(1)}, s32[2,1,16,512]{3,2,1,0:T(8,128)}, u32[]{:S(2)}) copy-start(s32[2,1,16,512]{3,2,1,0:T(8,128)} %step_ref.3) | copy-start | bytes 196612
  21.1 2.7 %copy-start.4 = (f32[2,1,16,512]{3,2,1,0:T(8,128)S(1)}, f32[2,1,16,512]{3,2,1,0:T(8,128)}, u32[]{:S(2)}) copy-start(f32[2,1,16,512]{3,2,1,0:T(8,128)} %omega_ref.3) | copy-start | bytes 196612
  21.1 2.7 %copy-start.5 = (s32[2,1,16,512]{3,2,1,0:T(8,128)S(1)}, s32[2,1,16,512]{3,2,1,0:T(8,128)}, u32[]{:S(2)}) copy-start(s32[2,1,16,512]{3,2,1,0:T(8,128)} %bracket_ref.3) | copy-start | bytes 196612
  21.1 2.7 %copy-start.6 = (f32[2,1,16,512]{3,2,1,0:T(8,128)S(1)}, f32[2,1,16,512]{3,2,1,0:T(8,128)}, u32[]{:S(2)}) copy-start(f32[2,1,16,512]{3,2,1,0:T(8,128)} %lam_ref.3) | copy-start | bytes 196612
  21.4 2.4 %collective-permute-start.5 = (f32[32,512]{1,0:T(8,128)S(1)}, f32[32,512]{1,0:T(8,128)S(1)}, u32[]{:S(2)}, u32[]{:S(2)}) collective-permute-start(f32[32,512]{1,0:T(8,128)S(1)} %get-tuple-element.29), channel_id=1, source_target_pairs={{0,1},{1,0},{2,3},{3,2},{4,5},{5,4},{6,7},{7,6},{8,9},{9,8},{10,11... | collective-permute-start | bytes 196616 | tf_op jit(solution)/shard_map/ppermute | solution.py:290
  25.3 6.5 %collective-permute-start.6 = (f32[32,512]{1,0:T(8,128)S(1)}, f32[32,512]{1,0:T(8,128)S(1)}, u32[]{:S(2)}, u32[]{:S(2)}) collective-permute-start(f32[32,512]{1,0:T(8,128)S(1)} %get-tuple-element.32), channel_id=1, source_target_pairs={{8,16},{16,8},{24,32},{32,24},{40,48},{48,40},{56,64},{64,56},{72,... | collective-permute-start | bytes 196616 | tf_op jit(solution)/shard_map/ppermute | solution.py:293
  26.0 7.5 %collective-permute-start.7 = (f32[32,512]{1,0:T(8,128)S(1)}, f32[32,512]{1,0:T(8,128)S(1)}, u32[]{:S(2)}, u32[]{:S(2)}) collective-permute-start(f32[32,512]{1,0:T(8,128)S(1)} %get-tuple-element.33), channel_id=1, source_target_pairs={{0,8},{8,0},{16,24},{24,16},{32,40},{40,32},{48,56},{56,48},{64,72... | collective-permute-start | bytes 196616 | tf_op jit(solution)/shard_map/ppermute | solution.py:294
  33.5 4.9 %collective-permute-start.10 = (f32[40,512]{1,0:T(8,128)S(1)}, f32[40,512]{1,0:T(8,128)S(1)}, u32[]{:S(2)}, u32[]{:S(2)}) collective-permute-start(f32[40,512]{1,0:T(8,128)S(1)} %merge_with_demand.1.own_ref), channel_id=1, source_target_pairs={{0,4},{2,6},{4,0},{6,2},{1,5},{3,7},{5,1},{7,3},{8,12},{10,14},{12... | collective-permute-start | bytes 245768 | tf_op jit(solution)/shard_map/ppermute | solution.py:287
  34.9 4.5 %collective-permute-start.9 = (f32[40,512]{1,0:T(8,128)S(1)}, f32[40,512]{1,0:T(8,128)S(1)}, u32[]{:S(2)}, u32[]{:S(2)}) collective-permute-start(f32[40,512]{1,0:T(8,128)S(1)} %merge_with_demand.1.own_ref), channel_id=1, source_target_pairs={{0,6},{2,4},{4,2},{6,0},{1,7},{3,5},{5,3},{7,1},{8,14},{10,12},{12... | collective-permute-start | bytes 245768 | tf_op jit(solution)/shard_map/ppermute | solution.py:287
  36.7 4.4 %collective-permute-start.8 = (f32[40,512]{1,0:T(8,128)S(1)}, f32[40,512]{1,0:T(8,128)S(1)}, u32[]{:S(2)}, u32[]{:S(2)}) collective-permute-start(f32[40,512]{1,0:T(8,128)S(1)} %merge_with_demand.1.own_ref), channel_id=1, source_target_pairs={{0,2},{2,0},{4,6},{6,4},{1,3},{3,1},{5,7},{7,5},{8,10},{10,8},{12,... | collective-permute-start | bytes 245768 | tf_op jit(solution)/shard_map/ppermute | solution.py:287
  41.4 3.3 %collective-permute-start.11 = (f32[80,512]{1,0:T(8,128)S(1)}, f32[80,512]{1,0:T(8,128)S(1)}, u32[]{:S(2)}, u32[]{:S(2)}) collective-permute-start(f32[80,512]{1,0:T(8,128)S(1)} %get-tuple-element.36), channel_id=1, source_target_pairs={{0,1},{1,0},{2,3},{3,2},{4,5},{5,4},{6,7},{7,6},{8,9},{9,8},{10,11... | collective-permute-start | bytes 491528 | tf_op jit(solution)/shard_map/ppermute | solution.py:290

commit v4 on v3

--- a/solution.py
+++ b/solution.py
@@ -30,59 +30,82 @@
 
 def bracket_read(mixed, bracket, weight):
     rows, assets = mixed.shape
+    chunks = assets // LANES
     upper = pltpu.roll(mixed, assets - 1, 1)
-    chunk_of = bracket >> 7
+    chunk_of = bracket >> (LANES.bit_length() - 1)
     lane_of = bracket & (LANES - 1)
-    pieces = []
-    for out in range(assets // LANES):
-        span = slice(out * LANES, (out + 1) * LANES)
-        lane, chunk = lane_of[:, span], chunk_of[:, span]
-        low = high = None
-        for source in range(assets // LANES):
-            table = slice(source * LANES, (source + 1) * LANES)
-            got_low = jnp.take_along_axis(mixed[:, table], lane, axis=1, mode="promise_in_bounds")
-            got_high = jnp.take_along_axis(upper[:, table], lane, axis=1, mode="promise_in_bounds")
-            low = got_low if source == 0 else jnp.where(chunk == source, got_low, low)
-            high = got_high if source == 0 else jnp.where(chunk == source, got_high, high)
-        lam = weight[:, span]
-        pieces.append((1.0 - lam) * low + lam * high)
-    return jnp.concatenate(pieces, axis=1)
+
+    def chosen(values, chunk, first):
+        if len(values) == 1:
+            return values[0]
+        half = len(values) // 2
+        return jnp.where(
+            chunk < first + half, chosen(values[:half], chunk, first), chosen(values[half:], chunk, first + half)
+        )
+
+    groups = []
+    for top in range(0, rows, 8):
+        part = slice(top, top + 8)
+        pieces = []
+        for out in range(chunks):
+            span = slice(out * LANES, (out + 1) * LANES)
+            lane, chunk, lam = lane_of[part, span], chunk_of[part, span], weight[part, span]
+            low, high = (
+                chosen(
+                    [
+                        jnp.take_along_axis(
+                            table[part, k * LANES : (k + 1) * LANES], lane, axis=1, mode="promise_in_bounds"
+                        )
+                        for k in range(chunks)
+                    ],
+                    chunk,
+                    0,
+                )
+                for table in (mixed, upper)
+            )
+            pieces.append((1.0 - lam) * low + lam * high)
+        groups.append(jnp.concatenate(pieces, axis=1))
+    return jnp.concatenate(groups, axis=0)
 
 
 def push_assets(density, bracket, weight, parts_ref, sums_ref):
     rows, assets = density.shape
-    chunks = assets // LANES
-    chunk_of = bracket >> 7
-    lane_of = bracket & (LANES - 1)
+    width = LANES // 2
+    chunks = assets // width
+    chunk_of = bracket >> (width.bit_length() - 1)
+    place_of = bracket & (width - 1)
     share = weight * density
-    stay = density - share
-    parts = []
-    for value in (stay, share):
+    for k, value in enumerate((density - share, share)):
         high, low = split_bf16(value)
-        parts += [high.astype(F32), low.astype(F32)]
-    for k, part in enumerate(parts):
-        parts_ref[k] = part
+        parts_ref[2 * k] = high.astype(F32)
+        parts_ref[2 * k + 1] = low.astype(F32)
     height = 4 * chunks
-    place = lax.broadcasted_iota(jnp.int32, (height, assets), 0)
-    lane_iota = lax.broadcasted_iota(jnp.int32, (LANES, assets), 0)
+    chunk_iota = lax.broadcasted_iota(jnp.int32, (chunks, assets), 0)
+    place_iota = lax.broadcasted_iota(jnp.int32, (width, assets), 0)
     for r in range(rows):
-        picked = jnp.broadcast_to(parts_ref[3, r : r + 1, :], (height, assets))
-        for k in (2, 1, 0):
-            picked = jnp.where(
-                place < (k + 1) * chunks, jnp.broadcast_to(parts_ref[k, r : r + 1, :], (height, assets)), picked
-            )
-        left = jnp.where((place & (chunks - 1)) == chunk_of[r : r + 1, :], picked, 0.0).astype(BF16)
-        right = jnp.where(lane_iota == lane_of[r : r + 1, :], 1.0, 0.0).astype(BF16)
-        sums_ref[r * height : (r + 1) * height, :] = lax.dot_general(
+        row = slice(r, r + 1)
+        here = chunk_iota == chunk_of[row, :]
+        left = jnp.concatenate([jnp.where(here, parts_ref[k, row, :], 0.0) for k in range(4)], axis=0).astype(BF16)
+        right = jnp.where(place_iota == place_of[row, :], 1.0, 0.0).astype(BF16)
+        sums_ref[r * height : (r + 1) * height, :width] = lax.dot_general(
             left, right, (((1,), (1,)), ((), ())), preferred_element_type=F32
         )
+    low_half = lax.broadcasted_iota(jnp.int32, (rows, LANES), 1) < width
 
     def gathered(k, h):
-        return sums_ref[pl.ds(k * chunks + h, rows, stride=height), :]
-
-    stayed = jnp.concatenate([gathered(0, h) + gathered(1, h) for h in range(chunks)], axis=1)
-    shared = jnp.concatenate([gathered(2, h) + gathered(3, h) for h in range(chunks)], axis=1)
-    return stayed + pltpu.roll(shared, 1, 1)
+        high, low = (sums_ref[pl.ds((k + term) * chunks + h, rows, stride=height), :] for term in range(2))
+        return high + low
+
+    def assembled(k):
+        return jnp.concatenate(
+            [
+                jnp.where(low_half, gathered(k, h), pltpu.roll(gathered(k, h + 1), width, 1))
+                for h in range(0, chunks, 2)
+            ],
+            axis=1,
+        )
+
+    return assembled(0) + pltpu.roll(assembled(2), 1, 1)
 
 
 def level_shares(moved, step, omega):
@@ -229,28 +252,28 @@
     store_halo(pair_ref, other_ref, to_plus, to_minus, value)
 
 
-def close_kernel(
-    keep_ref, got_ref, own_ref, one_ref, two_ref, three_ref, energy_ref, tax_ref, demand_ref,
-    value_ref, mass_ref, terms_ref, fixed_ref, interp_ref,
-):
+def close_kernel(keep_ref, got_ref, own_ref, *rest):
+    (*other_refs, energy_ref, tax_ref, demand_ref, value_ref, mass_ref, terms_ref, out_ref, spent_ref, sems) = rest
     rows = energy_ref.shape[1]
     chip = lax.axis_index("x")
-    refs = (own_ref, one_ref, two_ref, three_ref)
-    for shift, ref in zip(SHIFTS, refs):
-        fixed_ref[chip ^ shift] = ref[2 * rows :, :]
-    spent = []
-    for k in range(len(refs)):
-        part = slice((k + 1) * rows, (k + 2) * rows)
-        bracket = fixed_ref[k, rows : 2 * rows, :].astype(jnp.int32)
-        interp = bracket_read(keep_ref[part, :] + got_ref[part, :], bracket, fixed_ref[k, 2 * rows :, :])
-        interp_ref[k] = interp
-        spent.append(fixed_ref[k, :rows, :] * lax.rsqrt(interp))
-    first = jnp.sum((spent[0] + spent[1]) + (spent[2] + spent[3]))
-    second = jnp.sum(demand_ref[...])
-    lane = lax.broadcasted_iota(jnp.int32, terms_ref.shape, 2)
-    terms_ref[...] = jnp.where(lane == 0, first, second)
-    mass_ref[0] = keep_ref[:rows, :] + got_ref[:rows, :]
-    value_ref[0] = gross_rate * interp_ref[chip] * (1.0 + tax_ref[0] * energy_ref[0])
+    out_ref[1, 0] = keep_ref[:rows, :] + got_ref[:rows, :]
+    mass_copy = pltpu.make_async_copy(out_ref.at[1], mass_ref, sems.at[1])
+    mass_copy.start()
+    value_copy = pltpu.make_async_copy(out_ref.at[0], value_ref, sems.at[0])
+    for shift, ref in zip(SHIFTS, (own_ref, *other_refs)):
+        part = pl.ds(pl.multiple_of(((chip ^ shift) + 1) * rows, rows), rows)
+        bracket = ref[3 * rows : 4 * rows, :].astype(jnp.int32)
+        interp = bracket_read(keep_ref[part, :] + got_ref[part, :], bracket, ref[4 * rows :, :])
+        spent_ref[chip ^ shift] = ref[2 * rows : 3 * rows, :] * lax.rsqrt(interp)
+        if shift == 0:
+            out_ref[0, 0] = gross_rate * interp * (1.0 + tax_ref[0] * energy_ref[0])
+            value_copy.start()
+    first = jnp.sum((spent_ref[0] + spent_ref[1]) + (spent_ref[2] + spent_ref[3]), axis=(0, 1), keepdims=True)
+    second = jnp.sum(demand_ref[...], axis=(0, 1), keepdims=True)
+    lane = lax.broadcasted_iota(jnp.int32, (1, LANES), 1)
+    terms_ref[...] = jnp.broadcast_to(jnp.where(lane == 0, first, second)[None], terms_ref.shape)
+    mass_copy.wait()
+    value_copy.wait()
 
 
 def demand_kernel(terms_ref, out_ref):
@@ -274,7 +297,7 @@
     states = markov.shape[0]
     levels, chips, cores = (lax.axis_size(axis) for axis in ("dur", "x", "core"))
     scale = 1.0 / (levels * states * assets)
-    chunks = assets // LANES
+    chunks = assets // (LANES // 2)
     slab = pltpu.VMEM((rows, assets), F32)
     pair = pltpu.VMEM((2 * rows, assets), F32)
     block = jax.ShapeDtypeStruct((1, rows, assets), F32)
@@ -365,8 +388,12 @@
         close_kernel,
         out_shape=(block, block, pltpu.VMEM((levels * cores, 1, LANES), F32)),
         in_specs=[VMEM] * 7 + [SMEM, VMEM],
-        out_specs=(VMEM,) * 3,
-        scratch_shapes=[pltpu.VMEM((chips, 3 * rows, assets), F32), pltpu.VMEM((chips, rows, assets), F32)],
+        out_specs=(pl.BlockSpec(memory_space=pl.ANY),) * 2 + (VMEM,),
+        scratch_shapes=[
+            pltpu.VMEM((2, 1, rows, assets), F32),
+            pltpu.VMEM((chips, rows, assets), F32),
+            pltpu.SemaphoreType.DMA((2,)),
+        ],
         name="close",
     )(*in_vmem(keep, over_cores(send), *every_first, energy_share), tax, *in_vmem(second))
     every_term = lax.all_to_all(terms, ("dur", "core"), 0, 0)

time: 66.9 us -> 66.3 us (level)
  no operation moved by 1% of the time
where the time goes in v4:
time: 66.3 us; the launch traced here: 66.1 us
  starting transfers between devices  23.3 us (35%)
  blocking collectives  19.2 us (29%)
  waiting for transfers between devices  16.6 us (25%)
  Pallas kernels  6.19 us (9%)
  between operations  0.78 us (1%)
    all_to_all x1, blocking collectives, per_device(): every_term = lax.all_to_all(terms, ('dur', 'core'), 0, 0)  19.2 us
    ppermute x6, waiting for transfers between devices, over_chips(): lax.ppermute(array, 'x', [(i, i ^ k) for i in range(chips)])  11.4 us
    ppermute x2, starting transfers between devices, over_levels(): return (other_in, lax.ppermute(pair_out, 'dur', pairs))  11.3 us
    ppermute x6, starting transfers between devices, over_chips(): lax.ppermute(array, 'x', [(i, i ^ k) for i in range(chips)])  6.92 us
    ppermute x2, starting transfers between devices, over_cores(): return lax.ppermute(array, 'core', [(i, i ^ 1) for i in range(cores)])  3.76 us
    ppermute x2, waiting for transfers between devices, over_levels(): return (other_in, lax.ppermute(pair_out, 'dur', pairs))  3.31 us
    pallas_call x1, Pallas kernels, per_device(): pl.pallas_call(close_kernel, out_shape=(block, block, pltpu.VMEM((levels...  1.96 us
    ppermute x2, waiting for transfers between devices, over_cores(): return lax.ppermute(array, 'core', [(i, i ^ 1) for i in range(cores)])  1.93 us
  transfers between devices with their start and end apart: 12, of which 9 were waited for; matrix products, arithmetic and copies ran while one was open for 0% of the time, Pallas kernels for 0%

profile of v4, /device:TPU:1, one launch (start us, length us, event | category | flops | bytes accessed | tf_op | source)
XLA Modules:
  0.0 66.1 jit_solution(18071705783443620780)
XLA Ops:
  0.6 1.6 %open.1 = (f32[32,512]{1,0:T(8,128)S(1)}, f32[32,512]{1,0:T(8,128)S(1)}, f32[16,512]{1,0:T(8,128)S(1)}, f32[48,512]{1,0:T(8,128)S(1)}) custom-call(f32[1,16,512]{2,1,0:T(8,128)} %value_ref.3, f32[1,16,512]{2,1,0:T(8,128)} %mass_ref.1, s32[2,1,16,512]{3,2,1,0:T(8,128)} %fwd_bracket_ref.1, f32[2,1,16,512]{3,2,1,0:T(8,128)} %fwd_weight_ref.1, ...), custom_call_target="tpu_custom_call" | custom-call | tf_op jit(solution)/shard_map/open/pallas_call | solution.py:327
  2.3 0.7 %collective-permute-start = (f32[32,512]{1,0:T(8,128)S(1)}, f32[32,512]{1,0:T(8,128)S(1)}, u32[]{:S(2)}, u32[]{:S(2)}) collective-permute-start(f32[32,512]{1,0:T(8,128)S(1)} %get-tuple-element.23), channel_id=1, source_target_pairs={{8,16},{16,8},{24,32},{32,24},{40,48},{48,40},{56,64},{64,56},{72,... | collective-permute-start | bytes 196616 | tf_op jit(solution)/shard_map/ppermute | solution.py:316
  2.9 5.4 %collective-permute-start.1 = (f32[32,512]{1,0:T(8,128)S(1)}, f32[32,512]{1,0:T(8,128)S(1)}, u32[]{:S(2)}, u32[]{:S(2)}) collective-permute-start(f32[32,512]{1,0:T(8,128)S(1)} %get-tuple-element.24), channel_id=1, source_target_pairs={{0,8},{8,0},{16,24},{24,16},{32,40},{40,32},{48,56},{56,48},{64,72... | collective-permute-start | bytes 196616 | tf_op jit(solution)/shard_map/ppermute | solution.py:317
  8.4 0.0 collective-permute-done.other_ref
  8.4 1.7 %collective-permute-done.1.pair_ref = f32[32,512]{1,0:T(8,128)S(1)} collective-permute-done((f32[32,512]{1,0:T(8,128)S(1)}, f32[32,512]{1,0:T(8,128)S(1)}, u32[]{:S(2)}, u32[]{:S(2)}) %collective-permute-start.1) | collective-permute-done | bytes 65568 | tf_op jit(solution)/shard_map/ppermute | solution.py:317
  10.1 2.8 %collective-permute-start.4 = (f32[80,512]{1,0:T(8,128)S(1)}, f32[80,512]{1,0:T(8,128)S(1)}, u32[]{:S(2)}, u32[]{:S(2)}) collective-permute-start(f32[80,512]{1,0:T(8,128)S(1)} %merge_with_fixed.1.own_ref), channel_id=1, source_target_pairs={{0,4},{2,6},{4,0},{6,2},{1,5},{3,7},{5,1},{7,3},{8,12},{10,14},{12... | collective-permute-start | bytes 491528 | tf_op jit(solution)/shard_map/ppermute | solution.py:310
  12.9 0.9 %collective-permute-start.3 = (f32[80,512]{1,0:T(8,128)S(1)}, f32[80,512]{1,0:T(8,128)S(1)}, u32[]{:S(2)}, u32[]{:S(2)}) collective-permute-start(f32[80,512]{1,0:T(8,128)S(1)} %merge_with_fixed.1.own_ref), channel_id=1, source_target_pairs={{0,6},{2,4},{4,2},{6,0},{1,7},{3,5},{5,3},{7,1},{8,14},{10,12},{12... | collective-permute-start | bytes 491528 | tf_op jit(solution)/shard_map/ppermute | solution.py:310
  13.8 0.1 weights.1
  13.9 2.0 %collective-permute-done.4.three_ref.rest_2_ = f32[80,512]{1,0:T(8,128)S(1)} collective-permute-done((f32[80,512]{1,0:T(8,128)S(1)}, f32[80,512]{1,0:T(8,128)S(1)}, u32[]{:S(2)}, u32[]{:S(2)}) %collective-permute-start.4) | collective-permute-done | bytes 163872 | tf_op jit(solution)/shard_map/ppermute | solution.py:310
  15.8 5.0 %collective-permute-done.3.two_ref.rest_1_ = f32[80,512]{1,0:T(8,128)S(1)} collective-permute-done((f32[80,512]{1,0:T(8,128)S(1)}, f32[80,512]{1,0:T(8,128)S(1)}, u32[]{:S(2)}, u32[]{:S(2)}) %collective-permute-start.3) | collective-permute-done | bytes 163872 | tf_op jit(solution)/shard_map/ppermute | solution.py:310
  20.9 0.0 copy-start.3
  20.9 0.0 copy-start.4
  20.9 0.0 copy-start.5
  20.9 0.0 copy-start.6
  20.9 0.3 markov.1
  21.2 1.5 %collective-permute-start.5 = (f32[32,512]{1,0:T(8,128)S(1)}, f32[32,512]{1,0:T(8,128)S(1)}, u32[]{:S(2)}, u32[]{:S(2)}) collective-permute-start(f32[32,512]{1,0:T(8,128)S(1)} %get-tuple-element.29), channel_id=1, source_target_pairs={{0,1},{1,0},{2,3},{3,2},{4,5},{5,4},{6,7},{7,6},{8,9},{9,8},{10,11... | collective-permute-start | bytes 196616 | tf_op jit(solution)/shard_map/ppermute | solution.py:313
  22.7 0.9 %collective-permute-done.5.got_ref = f32[32,512]{1,0:T(8,128)S(1)} collective-permute-done((f32[32,512]{1,0:T(8,128)S(1)}, f32[32,512]{1,0:T(8,128)S(1)}, u32[]{:S(2)}, u32[]{:S(2)}) %collective-permute-start.5) | collective-permute-done | bytes 65568 | tf_op jit(solution)/shard_map/ppermute | solution.py:313
  23.7 1.2 %turn.1 = (f32[32,512]{1,0:T(8,128)S(1)}, f32[32,512]{1,0:T(8,128)S(1)}, f32[16,512]{1,0:T(8,128)S(1)}, f32[16,512]{1,0:T(8,128)S(1)}, f32[8,512]{1,0:T(8,128)S(1)}) custom-call(f32[32,512]{1,0:T(8,128)S(1)} %get-tuple-element.28.keep_ref, f32[32,512]{1,0:T(8,128)S(1)} %collective-permute-done.5.got_ref, s32[2,1,16,512]{3,2,1,0:T(8,128)S(1)} %copy-done.5, ...), custom_call_target="tpu_custom_call" | custom-call | tf_op jit(solution)/shard_map/turn/pallas_call | solution.py:354
  24.9 0.7 %collective-permute-start.6 = (f32[32,512]{1,0:T(8,128)S(1)}, f32[32,512]{1,0:T(8,128)S(1)}, u32[]{:S(2)}, u32[]{:S(2)}) collective-permute-start(f32[32,512]{1,0:T(8,128)S(1)} %get-tuple-element.32), channel_id=1, source_target_pairs={{8,16},{16,8},{24,32},{32,24},{40,48},{48,40},{56,64},{64,56},{72,... | collective-permute-start | bytes 196616 | tf_op jit(solution)/shard_map/ppermute | solution.py:316
  25.6 5.8 %collective-permute-start.7 = (f32[32,512]{1,0:T(8,128)S(1)}, f32[32,512]{1,0:T(8,128)S(1)}, u32[]{:S(2)}, u32[]{:S(2)}) collective-permute-start(f32[32,512]{1,0:T(8,128)S(1)} %get-tuple-element.33), channel_id=1, source_target_pairs={{0,8},{8,0},{16,24},{24,16},{32,40},{40,32},{48,56},{56,48},{64,72... | collective-permute-start | bytes 196616 | tf_op jit(solution)/shard_map/ppermute | solution.py:317
  31.4 1.7 %collective-permute-done.7.pair_ref = f32[32,512]{1,0:T(8,128)S(1)} collective-permute-done((f32[32,512]{1,0:T(8,128)S(1)}, f32[32,512]{1,0:T(8,128)S(1)}, u32[]{:S(2)}, u32[]{:S(2)}) %collective-permute-start.7) | collective-permute-done | bytes 65568 | tf_op jit(solution)/shard_map/ppermute | solution.py:317
  33.1 1.4 %collective-permute-start.10 = (f32[40,512]{1,0:T(8,128)S(1)}, f32[40,512]{1,0:T(8,128)S(1)}, u32[]{:S(2)}, u32[]{:S(2)}) collective-permute-start(f32[40,512]{1,0:T(8,128)S(1)} %merge_with_demand.1.own_ref), channel_id=1, source_target_pairs={{0,4},{2,6},{4,0},{6,2},{1,5},{3,7},{5,1},{7,3},{8,12},{10,14},{12... | collective-permute-start | bytes 245768 | tf_op jit(solution)/shard_map/ppermute | solution.py:310
  34.5 1.8 %collective-permute-start.9 = (f32[40,512]{1,0:T(8,128)S(1)}, f32[40,512]{1,0:T(8,128)S(1)}, u32[]{:S(2)}, u32[]{:S(2)}) collective-permute-start(f32[40,512]{1,0:T(8,128)S(1)} %merge_with_demand.1.own_ref), channel_id=1, source_target_pairs={{0,6},{2,4},{4,2},{6,0},{1,7},{3,5},{5,3},{7,1},{8,14},{10,12},{12... | collective-permute-start | bytes 245768 | tf_op jit(solution)/shard_map/ppermute | solution.py:310
  36.3 1.7 %collective-permute-done.10.three_ref = f32[40,512]{1,0:T(8,128)S(1)} collective-permute-done((f32[40,512]{1,0:T(8,128)S(1)}, f32[40,512]{1,0:T(8,128)S(1)}, u32[]{:S(2)}, u32[]{:S(2)}) %collective-permute-start.10) | collective-permute-done | bytes 81952 | tf_op jit(solution)/shard_map/ppermute | solution.py:310
  38.0 1.1 %collective-permute-done.9.two_ref = f32[40,512]{1,0:T(8,128)S(1)} collective-permute-done((f32[40,512]{1,0:T(8,128)S(1)}, f32[40,512]{1,0:T(8,128)S(1)}, u32[]{:S(2)}, u32[]{:S(2)}) %collective-permute-start.9) | collective-permute-done | bytes 81952 | tf_op jit(solution)/shard_map/ppermute | solution.py:310
  39.0 1.6 %collective-permute-done.8.one_ref = f32[40,512]{1,0:T(8,128)S(1)} collective-permute-done((f32[40,512]{1,0:T(8,128)S(1)}, f32[40,512]{1,0:T(8,128)S(1)}, u32[]{:S(2)}, u32[]{:S(2)}) %collective-permute-start.8) | collective-permute-done | bytes 81952 | tf_op jit(solution)/shard_map/ppermute | solution.py:310
  40.7 0.4 markov_wide.1
  41.1 2.2 %collective-permute-start.11 = (f32[80,512]{1,0:T(8,128)S(1)}, f32[80,512]{1,0:T(8,128)S(1)}, u32[]{:S(2)}, u32[]{:S(2)}) collective-permute-start(f32[80,512]{1,0:T(8,128)S(1)} %get-tuple-element.36), channel_id=1, source_target_pairs={{0,1},{1,0},{2,3},{3,2},{4,5},{5,4},{6,7},{7,6},{8,9},{9,8},{10,11... | collective-permute-start | bytes 491528 | tf_op jit(solution)/shard_map/ppermute | solution.py:313
  43.3 1.0 %collective-permute-done.11.got_ref = f32[80,512]{1,0:T(8,128)S(1)} collective-permute-done((f32[80,512]{1,0:T(8,128)S(1)}, f32[80,512]{1,0:T(8,128)S(1)}, u32[]{:S(2)}, u32[]{:S(2)}) %collective-permute-start.11) | collective-permute-done | bytes 163872 | tf_op jit(solution)/shard_map/ppermute | solution.py:313
  44.3 2.0 %close.1 = (f32[1,16,512]{2,1,0:T(8,128)}, f32[1,16,512]{2,1,0:T(8,128)}, f32[64,1,128]{2,1,0:T(1,128)S(1)}) custom-call(f32[80,512]{1,0:T(8,128)S(1)} %get-tuple-element.35.keep_ref, f32[80,512]{1,0:T(8,128)S(1)} %collective-permute-done.11.got_ref, f32[80,512]{1,0:T(8,128)S(1)} %merge_with_fixed.1.own_ref, ...), custom_call_target="tpu_custom_call" | custom-call | tf_op jit(solution)/shard_map/close/pallas_call | solution.py:387
  46.3 19.2 %all_to_all.5.terms_ref = f32[64,1,128]{2,1,0:T(1,128)S(1)} all-to-all(f32[64,1,128]{2,1,0:T(1,128)S(1)} %get-tuple-element.40), channel_id=1, replica_groups=mesh['dur'=32,'x'=4,'core'=2] {'dur','core'}, dimensions={0} | all-to-all | bytes 65536 | tf_op jit(solution)/shard_map/all_to_all | solution.py:399
  65.5 0.6 demand.1
  (20 shorter events, 0.1 us)
Async XLA Ops:
  0.6 9.4 %copy-start.7 = (f32[1,16,512]{2,1,0:T(8,128)S(1)}, f32[1,16,512]{2,1,0:T(8,128)}, u32[]{:S(2)}) copy-start(f32[1,16,512]{2,1,0:T(8,128)} %value_ref.3) | copy-start | bytes 98308
  2.3 6.1 %collective-permute-start = (f32[32,512]{1,0:T(8,128)S(1)}, f32[32,512]{1,0:T(8,128)S(1)}, u32[]{:S(2)}, u32[]{:S(2)}) collective-permute-start(f32[32,512]{1,0:T(8,128)S(1)} %get-tuple-element.23), channel_id=1, source_target_pairs={{8,16},{16,8},{24,32},{32,24},{40,48},{48,40},{56,64},{64,56},{72,... | collective-permute-start | bytes 196616 | tf_op jit(solution)/shard_map/ppermute | solution.py:316
  2.9 7.1 %collective-permute-start.1 = (f32[32,512]{1,0:T(8,128)S(1)}, f32[32,512]{1,0:T(8,128)S(1)}, u32[]{:S(2)}, u32[]{:S(2)}) collective-permute-start(f32[32,512]{1,0:T(8,128)S(1)} %get-tuple-element.24), channel_id=1, source_target_pairs={{0,8},{8,0},{16,24},{24,16},{32,40},{40,32},{48,56},{56,48},{64,72... | collective-permute-start | bytes 196616 | tf_op jit(solution)/shard_map/ppermute | solution.py:317
  10.0 3.7 %copy-start.8 = (f32[128,128]{1,0:T(8,128)S(1)}, f32[128,128]{1,0:T(8,128)}, u32[]{:S(2)}) copy-start(f32[128,128]{1,0:T(8,128)} %markov_ref.1) | copy-start | bytes 196612
  10.1 5.8 %collective-permute-start.4 = (f32[80,512]{1,0:T(8,128)S(1)}, f32[80,512]{1,0:T(8,128)S(1)}, u32[]{:S(2)}, u32[]{:S(2)}) collective-permute-start(f32[80,512]{1,0:T(8,128)S(1)} %merge_with_fixed.1.own_ref), channel_id=1, source_target_pairs={{0,4},{2,6},{4,0},{6,2},{1,5},{3,7},{5,1},{7,3},{8,12},{10,14},{12... | collective-permute-start | bytes 491528 | tf_op jit(solution)/shard_map/ppermute | solution.py:310
  12.9 8.0 %collective-permute-start.3 = (f32[80,512]{1,0:T(8,128)S(1)}, f32[80,512]{1,0:T(8,128)S(1)}, u32[]{:S(2)}, u32[]{:S(2)}) collective-permute-start(f32[80,512]{1,0:T(8,128)S(1)} %merge_with_fixed.1.own_ref), channel_id=1, source_target_pairs={{0,6},{2,4},{4,2},{6,0},{1,7},{3,5},{5,3},{7,1},{8,14},{10,12},{12... | collective-permute-start | bytes 491528 | tf_op jit(solution)/shard_map/ppermute | solution.py:310
  13.8 7.1 %collective-permute-start.2 = (f32[80,512]{1,0:T(8,128)S(1)}, f32[80,512]{1,0:T(8,128)S(1)}, u32[]{:S(2)}, u32[]{:S(2)}) collective-permute-start(f32[80,512]{1,0:T(8,128)S(1)} %merge_with_fixed.1.own_ref), channel_id=1, source_target_pairs={{0,2},{2,0},{4,6},{6,4},{1,3},{3,1},{5,7},{7,5},{8,10},{10,8},{12,... | collective-permute-start | bytes 491528 | tf_op jit(solution)/shard_map/ppermute | solution.py:310
  20.9 2.8 %copy-start = (f32[1,16,512]{2,1,0:T(8,128)S(1)}, f32[1,16,512]{2,1,0:T(8,128)}, u32[]{:S(2)}) copy-start(f32[1,16,512]{2,1,0:T(8,128)} %rest_3_.1) | copy-start | bytes 98308
  20.9 2.8 %copy-start.1 = (s32[2,1,16,512]{3,2,1,0:T(8,128)S(1)}, s32[2,1,16,512]{3,2,1,0:T(8,128)}, u32[]{:S(2)}) copy-start(s32[2,1,16,512]{3,2,1,0:T(8,128)} %fwd_bracket_ref.1) | copy-start | bytes 196612
  20.9 2.8 %copy-start.2 = (f32[2,1,16,512]{3,2,1,0:T(8,128)S(1)}, f32[2,1,16,512]{3,2,1,0:T(8,128)}, u32[]{:S(2)}) copy-start(f32[2,1,16,512]{3,2,1,0:T(8,128)} %fwd_weight_ref.1) | copy-start | bytes 196612
  20.9 2.7 %copy-start.3 = (s32[2,1,16,512]{3,2,1,0:T(8,128)S(1)}, s32[2,1,16,512]{3,2,1,0:T(8,128)}, u32[]{:S(2)}) copy-start(s32[2,1,16,512]{3,2,1,0:T(8,128)} %step_ref.3) | copy-start | bytes 196612
  20.9 2.7 %copy-start.4 = (f32[2,1,16,512]{3,2,1,0:T(8,128)S(1)}, f32[2,1,16,512]{3,2,1,0:T(8,128)}, u32[]{:S(2)}) copy-start(f32[2,1,16,512]{3,2,1,0:T(8,128)} %omega_ref.3) | copy-start | bytes 196612
  20.9 2.7 %copy-start.5 = (s32[2,1,16,512]{3,2,1,0:T(8,128)S(1)}, s32[2,1,16,512]{3,2,1,0:T(8,128)}, u32[]{:S(2)}) copy-start(s32[2,1,16,512]{3,2,1,0:T(8,128)} %bracket_ref.3) | copy-start | bytes 196612
  20.9 2.7 %copy-start.6 = (f32[2,1,16,512]{3,2,1,0:T(8,128)S(1)}, f32[2,1,16,512]{3,2,1,0:T(8,128)}, u32[]{:S(2)}) copy-start(f32[2,1,16,512]{3,2,1,0:T(8,128)} %lam_ref.3) | copy-start | bytes 196612
  21.2 2.4 %collective-permute-start.5 = (f32[32,512]{1,0:T(8,128)S(1)}, f32[32,512]{1,0:T(8,128)S(1)}, u32[]{:S(2)}, u32[]{:S(2)}) collective-permute-start(f32[32,512]{1,0:T(8,128)S(1)} %get-tuple-element.29), channel_id=1, source_target_pairs={{0,1},{1,0},{2,3},{3,2},{4,5},{5,4},{6,7},{7,6},{8,9},{9,8},{10,11... | collective-permute-start | bytes 196616 | tf_op jit(solution)/shard_map/ppermute | solution.py:313
  24.9 6.5 %collective-permute-start.6 = (f32[32,512]{1,0:T(8,128)S(1)}, f32[32,512]{1,0:T(8,128)S(1)}, u32[]{:S(2)}, u32[]{:S(2)}) collective-permute-start(f32[32,512]{1,0:T(8,128)S(1)} %get-tuple-element.32), channel_id=1, source_target_pairs={{8,16},{16,8},{24,32},{32,24},{40,48},{48,40},{56,64},{64,56},{72,... | collective-permute-start | bytes 196616 | tf_op jit(solution)/shard_map/ppermute | solution.py:316
  25.6 7.5 %collective-permute-start.7 = (f32[32,512]{1,0:T(8,128)S(1)}, f32[32,512]{1,0:T(8,128)S(1)}, u32[]{:S(2)}, u32[]{:S(2)}) collective-permute-start(f32[32,512]{1,0:T(8,128)S(1)} %get-tuple-element.33), channel_id=1, source_target_pairs={{0,8},{8,0},{16,24},{24,16},{32,40},{40,32},{48,56},{56,48},{64,72... | collective-permute-start | bytes 196616 | tf_op jit(solution)/shard_map/ppermute | solution.py:317
  33.1 4.9 %collective-permute-start.10 = (f32[40,512]{1,0:T(8,128)S(1)}, f32[40,512]{1,0:T(8,128)S(1)}, u32[]{:S(2)}, u32[]{:S(2)}) collective-permute-start(f32[40,512]{1,0:T(8,128)S(1)} %merge_with_demand.1.own_ref), channel_id=1, source_target_pairs={{0,4},{2,6},{4,0},{6,2},{1,5},{3,7},{5,1},{7,3},{8,12},{10,14},{12... | collective-permute-start | bytes 245768 | tf_op jit(solution)/shard_map/ppermute | solution.py:310
  34.5 4.5 %collective-permute-start.9 = (f32[40,512]{1,0:T(8,128)S(1)}, f32[40,512]{1,0:T(8,128)S(1)}, u32[]{:S(2)}, u32[]{:S(2)}) collective-permute-start(f32[40,512]{1,0:T(8,128)S(1)} %merge_with_demand.1.own_ref), channel_id=1, source_target_pairs={{0,6},{2,4},{4,2},{6,0},{1,7},{3,5},{5,3},{7,1},{8,14},{10,12},{12... | collective-permute-start | bytes 245768 | tf_op jit(solution)/shard_map/ppermute | solution.py:310
  36.3 4.4 %collective-permute-start.8 = (f32[40,512]{1,0:T(8,128)S(1)}, f32[40,512]{1,0:T(8,128)S(1)}, u32[]{:S(2)}, u32[]{:S(2)}) collective-permute-start(f32[40,512]{1,0:T(8,128)S(1)} %merge_with_demand.1.own_ref), channel_id=1, source_target_pairs={{0,2},{2,0},{4,6},{6,4},{1,3},{3,1},{5,7},{7,5},{8,10},{10,8},{12,... | collective-permute-start | bytes 245768 | tf_op jit(solution)/shard_map/ppermute | solution.py:310
  41.1 3.3 %collective-permute-start.11 = (f32[80,512]{1,0:T(8,128)S(1)}, f32[80,512]{1,0:T(8,128)S(1)}, u32[]{:S(2)}, u32[]{:S(2)}) collective-permute-start(f32[80,512]{1,0:T(8,128)S(1)} %get-tuple-element.36), channel_id=1, source_target_pairs={{0,1},{1,0},{2,3},{3,2},{4,5},{5,4},{6,7},{7,6},{8,9},{9,8},{10,11... | collective-permute-start | bytes 491528 | tf_op jit(solution)/shard_map/ppermute | solution.py:313

commit v5 on v4

--- a/solution.py
+++ b/solution.py
@@ -130,7 +130,9 @@
     other_ref[rows:, :] = value
 
 
-def weights_kernel(markov_ref, back_ref, ahead_ref, flip_ref):
+def weights_kernel(markov_ref, tax_ref, back_ref, ahead_ref, rates_ref, flip_ref):
+    for quarter in range(2):
+        rates_ref[quarter : quarter + 1, :] = jnp.full((1, LANES), tax_ref[quarter], F32)
     chip = lax.axis_index("x")
     states = markov_ref.shape[0]
     wide = ahead_ref.shape[0] // 2
@@ -143,18 +145,20 @@
     ahead_ref[wide:, :] = low
 
 
+def fixed_kernel(scale, energy_ref, mass_ref, bracket_ref, lam_ref, tax_ref, out_ref):
+    rows = energy_ref.shape[1]
+    out_ref[:rows, :] = scale * mass_ref[0] * energy_ref[0] / (1.0 + tax_ref[0])
+    out_ref[rows : 2 * rows, :] = bracket_ref[0, 0].astype(F32)
+    out_ref[2 * rows :, :] = lam_ref[0, 0]
+
+
 def open_kernel(
-    scale, value_ref, mass_ref, bracket_ref, weight_ref, step_ref, omega_ref, energy_ref, bwd_bracket_ref, lam_ref,
-    tax_ref, pair_ref, other_ref, self_ref, fixed_ref, parts_ref, sums_ref,
+    value_ref, mass_ref, bracket_ref, weight_ref, step_ref, omega_ref, pair_ref, other_ref, self_ref, parts_ref, sums_ref
 ):
-    rows = self_ref.shape[0]
     moved = push_assets(mass_ref[0], bracket_ref[0, 0], weight_ref[0, 0], parts_ref, sums_ref)
     to_self, to_plus, to_minus = level_shares(moved, step_ref[0, 0], omega_ref[0, 0])
     self_ref[...] = to_self
     store_halo(pair_ref, other_ref, to_plus, to_minus, value_ref[0])
-    fixed_ref[:rows, :] = scale * mass_ref[0] * energy_ref[0] / (1.0 + tax_ref[0])
-    fixed_ref[rows : 2 * rows, :] = bwd_bracket_ref[0, 0].astype(F32)
-    fixed_ref[2 * rows :, :] = lam_ref[0, 0]
 
 
 def merge_kernel(self_ref, value_ref, other_ref, pair_ref, rider_ref, out_ref):
@@ -232,14 +236,14 @@
 
 
 def turn_kernel(
-    scale, keep_ref, got_ref, bracket_ref, lam_ref, energy_ref, tax_ref, fwd_bracket_ref, fwd_weight_ref, step_ref,
+    scale, keep_ref, got_ref, bracket_ref, lam_ref, energy_ref, rates_ref, fwd_bracket_ref, fwd_weight_ref, step_ref,
     omega_ref, pair_ref, other_ref, self_ref, value_ref, demand_ref, parts_ref, sums_ref,
 ):
     rows = self_ref.shape[0]
     density = keep_ref[:rows, :] + got_ref[:rows, :]
     mixed = keep_ref[rows:, :] + got_ref[rows:, :]
     interp = bracket_read(mixed, bracket_ref[1, 0], lam_ref[1, 0])
-    tax = tax_ref[1]
+    tax = rates_ref[1:2, :1]
     share = energy_ref[0]
     spent = density * (share * lax.rsqrt(interp))
     half = demand_ref.shape[0]
@@ -252,8 +256,16 @@
     store_halo(pair_ref, other_ref, to_plus, to_minus, value)
 
 
+def folded(terms):
+    return sum(
+        terms[top : top + 8, left : left + LANES]
+        for top in range(0, terms.shape[0], 8)
+        for left in range(0, terms.shape[1], LANES)
+    )
+
+
 def close_kernel(keep_ref, got_ref, own_ref, *rest):
-    (*other_refs, energy_ref, tax_ref, demand_ref, value_ref, mass_ref, terms_ref, out_ref, spent_ref, sems) = rest
+    (*other_refs, energy_ref, rates_ref, demand_ref, value_ref, mass_ref, terms_ref, out_ref, spent_ref, sems) = rest
     rows = energy_ref.shape[1]
     chip = lax.axis_index("x")
     out_ref[1, 0] = keep_ref[:rows, :] + got_ref[:rows, :]
@@ -264,12 +276,13 @@
         part = pl.ds(pl.multiple_of(((chip ^ shift) + 1) * rows, rows), rows)
         bracket = ref[3 * rows : 4 * rows, :].astype(jnp.int32)
         interp = bracket_read(keep_ref[part, :] + got_ref[part, :], bracket, ref[4 * rows :, :])
-        spent_ref[chip ^ shift] = ref[2 * rows : 3 * rows, :] * lax.rsqrt(interp)
+        spent = ref[2 * rows : 3 * rows, :] * lax.rsqrt(interp)
+        spent_ref[chip ^ shift] = folded(spent)
         if shift == 0:
-            out_ref[0, 0] = gross_rate * interp * (1.0 + tax_ref[0] * energy_ref[0])
+            out_ref[0, 0] = gross_rate * interp * (1.0 + rates_ref[:1, :1] * energy_ref[0])
             value_copy.start()
     first = jnp.sum((spent_ref[0] + spent_ref[1]) + (spent_ref[2] + spent_ref[3]), axis=(0, 1), keepdims=True)
-    second = jnp.sum(demand_ref[...], axis=(0, 1), keepdims=True)
+    second = jnp.sum(folded(demand_ref[...]), axis=(0, 1), keepdims=True)
     lane = lax.broadcasted_iota(jnp.int32, (1, LANES), 1)
     terms_ref[...] = jnp.broadcast_to(jnp.where(lane == 0, first, second)[None], terms_ref.shape)
     mass_copy.wait()
@@ -316,24 +329,33 @@
         other_in = lax.ppermute(other_out, "dur", others)
         return other_in, lax.ppermute(pair_out, "dur", pairs)
 
-    weights = pl.pallas_call(
+    *weights, rates = pl.pallas_call(
         weights_kernel,
-        out_shape=(pltpu.VMEM((2 * states, states), BF16), pltpu.VMEM((4 * rows, states), BF16)),
-        in_specs=[VMEM],
-        out_specs=(VMEM, VMEM),
+        out_shape=(
+            pltpu.VMEM((2 * states, states), BF16),
+            pltpu.VMEM((4 * rows, states), BF16),
+            pltpu.VMEM((8, LANES), F32),
+        ),
+        in_specs=[VMEM, SMEM],
+        out_specs=(VMEM,) * 3,
         scratch_shapes=[pltpu.VMEM((states, states), F32)],
         name="weights",
-    )(*in_vmem(markov))
-    pair_out, other_out, kept, fixed = pl.pallas_call(
-        functools.partial(open_kernel, scale),
-        out_shape=(pair, pair, slab, pltpu.VMEM((3 * rows, assets), F32)),
-        in_specs=[VMEM] * 9 + [SMEM],
-        out_specs=(VMEM,) * 4,
+    )(*in_vmem(markov), tax)
+    fixed = pl.pallas_call(
+        functools.partial(fixed_kernel, scale),
+        out_shape=pltpu.VMEM((3 * rows, assets), F32),
+        in_specs=[VMEM] * 4 + [SMEM],
+        out_specs=VMEM,
+        name="fixed",
+    )(*in_vmem(energy_share, mass_start, bwd_bracket, bwd_weight), tax)
+    pair_out, other_out, kept = pl.pallas_call(
+        open_kernel,
+        out_shape=(pair, pair, slab),
+        in_specs=[VMEM] * 6,
+        out_specs=(VMEM,) * 3,
         scratch_shapes=push_scratch,
         name="open",
-    )(
-        value_next, mass_start, fwd_bracket, fwd_weight, dur_step, dur_weight, energy_share, bwd_bracket, bwd_weight, tax
-    )
+    )(value_next, mass_start, fwd_bracket, fwd_weight, dur_step, dur_weight)
     halo = over_levels(pair_out, other_out)
     mine = pl.pallas_call(
         merge_kernel,
@@ -354,13 +376,12 @@
     pair_out, other_out, kept, value, second = pl.pallas_call(
         functools.partial(turn_kernel, scale),
         out_shape=(pair, pair, slab, slab, eight),
-        in_specs=[VMEM] * 5 + [SMEM] + [VMEM] * 4,
+        in_specs=[VMEM] * 10,
         out_specs=(VMEM,) * 5,
         scratch_shapes=push_scratch,
         name="turn",
     )(
-        *in_vmem(keep, over_cores(send), bwd_bracket, bwd_weight, energy_share),
-        tax,
+        *in_vmem(keep, over_cores(send), bwd_bracket, bwd_weight, energy_share, rates),
         *in_vmem(fwd_bracket, fwd_weight, dur_step, dur_weight),
     )
     halo = over_levels(pair_out, other_out)
@@ -387,15 +408,15 @@
     value_start, mass_end, terms = pl.pallas_call(
         close_kernel,
         out_shape=(block, block, pltpu.VMEM((levels * cores, 1, LANES), F32)),
-        in_specs=[VMEM] * 7 + [SMEM, VMEM],
+        in_specs=[VMEM] * 9,
         out_specs=(pl.BlockSpec(memory_space=pl.ANY),) * 2 + (VMEM,),
         scratch_shapes=[
             pltpu.VMEM((2, 1, rows, assets), F32),
-            pltpu.VMEM((chips, rows, assets), F32),
+            pltpu.VMEM((chips, 8, LANES), F32),
             pltpu.SemaphoreType.DMA((2,)),
         ],
         name="close",
-    )(*in_vmem(keep, over_cores(send), *every_first, energy_share), tax, *in_vmem(second))
+    )(*in_vmem(keep, over_cores(send), *every_first, energy_share, rates, second))
     every_term = lax.all_to_all(terms, ("dur", "core"), 0, 0)
     demand = pl.pallas_call(
         demand_kernel,

time: 66.3 us -> 64.7 us (0.976)
  waiting for transfers between devices: 16.6 us -> 15.2 us
    pallas_call x1, Pallas kernels: 1.96 us -> 1.04 us  [per_device(): pl.pallas_call(close_kernel, out_shape=(block, block, pltpu.VMEM((levels...]
    ppermute x2, waiting for transfers between devices: 3.31 us -> 2.6 us  [over_levels(): return (other_in, lax.ppermute(pair_out, 'dur', pairs))]
    pallas_call x1, Pallas kernels: 0.1 us -> 0.76 us  [per_device(): pl.pallas_call(weights_kernel, out_shape=(pltpu.VMEM((2 * states, states)...]
    ppermute x6, waiting for transfers between devices: 11.4 us -> 10.7 us  [over_chips(): lax.ppermute(array, 'x', [(i, i ^ k) for i in range(chips)])]
    pallas_call x1 -> x2, Pallas kernels: 1.63 us -> 2.26 us  [the longest x1 1.58 us: per_device(): pl.pallas_call(open_kernel, out_shape=(pair, pair, slab), in_specs=[VMEM]...]
  transfers between devices with their start and end apart: 12 -> 12, of which waited for: 9 -> 9; matrix products, arithmetic and copies ran while one was open for 0% -> 0% of each run, Pallas kernels for 0% -> 2%
where the time goes in v5:
time: 64.7 us; the launch traced here: 64.5 us
  starting transfers between devices  23.3 us (36%)
  blocking collectives  19.2 us (30%)
  waiting for transfers between devices  15.2 us (23%)
  Pallas kernels  5.91 us (9%)
  between operations  0.78 us (1%)
    all_to_all x1, blocking collectives, per_device(): every_term = lax.all_to_all(terms, ('dur', 'core'), 0, 0)  19.2 us
    ppermute x2, starting transfers between devices, over_levels(): return (other_in, lax.ppermute(pair_out, 'dur', pairs))  11.2 us
    ppermute x6, waiting for transfers between devices, over_chips(): lax.ppermute(array, 'x', [(i, i ^ k) for i in range(chips)])  10.7 us
    ppermute x6, starting transfers between devices, over_chips(): lax.ppermute(array, 'x', [(i, i ^ k) for i in range(chips)])  6.92 us
    ppermute x2, starting transfers between devices, over_cores(): return lax.ppermute(array, 'core', [(i, i ^ 1) for i in range(cores)])  3.76 us
    ppermute x2, waiting for transfers between devices, over_levels(): return (other_in, lax.ppermute(pair_out, 'dur', pairs))  2.6 us
    ppermute x2, waiting for transfers between devices, over_cores(): return lax.ppermute(array, 'core', [(i, i ^ 1) for i in range(cores)])  1.93 us
    pallas_call x1, Pallas kernels, per_device(): pl.pallas_call(open_kernel, out_shape=(pair, pair, slab), in_specs=[VMEM]...  1.58 us
  transfers between devices with their start and end apart: 12, of which 9 were waited for; matrix products, arithmetic and copies ran while one was open for 0% of the time, Pallas kernels for 2%

profile of v5, /device:TPU:1, one launch (start us, length us, event | category | flops | bytes accessed | tf_op | source)
XLA Modules:
  0.0 64.5 jit_solution(7532504429256070539)
XLA Ops:
  0.7 1.6 %open.1 = (f32[32,512]{1,0:T(8,128)S(1)}, f32[32,512]{1,0:T(8,128)S(1)}, f32[16,512]{1,0:T(8,128)S(1)}) custom-call(f32[1,16,512]{2,1,0:T(8,128)} %value_ref.3, f32[1,16,512]{2,1,0:T(8,128)} %mass_ref.3, s32[2,1,16,512]{3,2,1,0:T(8,128)} %fwd_bracket_ref.1, f32[2,1,16,512]{3,2,1,0:T(8,128)} %fwd_weight_ref.1, s32[2,1,16,512]{3,2,1,0:T(8,128)} %step_ref.3, ...), custom_call_target="tpu_custom_call" | custom-call | tf_op jit(solution)/shard_map/open/pallas_call | solution.py:351
  2.3 0.7 %collective-permute-start = (f32[32,512]{1,0:T(8,128)S(1)}, f32[32,512]{1,0:T(8,128)S(1)}, u32[]{:S(2)}, u32[]{:S(2)}) collective-permute-start(f32[32,512]{1,0:T(8,128)S(1)} %get-tuple-element.23), channel_id=1, source_target_pairs={{8,16},{16,8},{24,32},{32,24},{40,48},{48,40},{56,64},{64,56},{72,... | collective-permute-start | bytes 196616 | tf_op jit(solution)/shard_map/ppermute | solution.py:329
  2.9 0.0 copy-start.7
  2.9 5.4 %collective-permute-start.1 = (f32[32,512]{1,0:T(8,128)S(1)}, f32[32,512]{1,0:T(8,128)S(1)}, u32[]{:S(2)}, u32[]{:S(2)}) collective-permute-start(f32[32,512]{1,0:T(8,128)S(1)} %get-tuple-element.24), channel_id=1, source_target_pairs={{0,8},{8,0},{16,24},{24,16},{32,40},{40,32},{48,56},{56,48},{64,72... | collective-permute-start | bytes 196616 | tf_op jit(solution)/shard_map/ppermute | solution.py:330
  8.4 0.7 %fixed.1.rider_ref = f32[48,512]{1,0:T(8,128)S(1)} custom-call(f32[1,16,512]{2,1,0:T(8,128)S(1)} %copy-done, f32[1,16,512]{2,1,0:T(8,128)S(1)} %copy-done.8, s32[2,1,16,512]{3,2,1,0:T(8,128)S(1)} %copy-done.5, f32[2,1,16,512]{3,2,1,0:T(8,128)S(1)} %copy-done.6, f32[2]{0:T(128)} %tax_ref.3), custom_call_target="tpu_custom_call" | custom-call | tf_op jit(solution)/shard_map/fixed/pallas_call | solution.py:344
  9.1 0.0 collective-permute-done.other_ref
  9.1 0.9 %collective-permute-done.1.pair_ref = f32[32,512]{1,0:T(8,128)S(1)} collective-permute-done((f32[32,512]{1,0:T(8,128)S(1)}, f32[32,512]{1,0:T(8,128)S(1)}, u32[]{:S(2)}, u32[]{:S(2)}) %collective-permute-start.1) | collective-permute-done | bytes 65568 | tf_op jit(solution)/shard_map/ppermute | solution.py:330
  10.1 2.8 %collective-permute-start.4 = (f32[80,512]{1,0:T(8,128)S(1)}, f32[80,512]{1,0:T(8,128)S(1)}, u32[]{:S(2)}, u32[]{:S(2)}) collective-permute-start(f32[80,512]{1,0:T(8,128)S(1)} %merge_with_fixed.1.own_ref), channel_id=1, source_target_pairs={{0,4},{2,6},{4,0},{6,2},{1,5},{3,7},{5,1},{7,3},{8,12},{10,14},{12... | collective-permute-start | bytes 491528 | tf_op jit(solution)/shard_map/ppermute | solution.py:323
  12.9 0.9 %collective-permute-start.3 = (f32[80,512]{1,0:T(8,128)S(1)}, f32[80,512]{1,0:T(8,128)S(1)}, u32[]{:S(2)}, u32[]{:S(2)}) collective-permute-start(f32[80,512]{1,0:T(8,128)S(1)} %merge_with_fixed.1.own_ref), channel_id=1, source_target_pairs={{0,6},{2,4},{4,2},{6,0},{1,7},{3,5},{5,3},{7,1},{8,14},{10,12},{12... | collective-permute-start | bytes 491528 | tf_op jit(solution)/shard_map/ppermute | solution.py:323
  13.8 0.0 collective-permute-start.2
  13.8 0.8 %weights.1 = (bf16[256,128]{1,0:T(8,128)(2,1)S(1)}, bf16[64,128]{1,0:T(8,128)(2,1)S(1)}, f32[8,128]{1,0:T(8,128)S(1)}) custom-call(f32[128,128]{1,0:T(8,128)S(1)} %copy-done.9, f32[2]{0:T(128)} %tax_ref.3), custom_call_target="tpu_custom_call" | custom-call | tf_op jit(solution)/shard_map/weights/pallas_call | solution.py:332
  14.5 1.3 %collective-permute-done.4.three_ref.rest_2_ = f32[80,512]{1,0:T(8,128)S(1)} collective-permute-done((f32[80,512]{1,0:T(8,128)S(1)}, f32[80,512]{1,0:T(8,128)S(1)}, u32[]{:S(2)}, u32[]{:S(2)}) %collective-permute-start.4) | collective-permute-done | bytes 163872 | tf_op jit(solution)/shard_map/ppermute | solution.py:323
  15.8 5.0 %collective-permute-done.3.two_ref.rest_1_ = f32[80,512]{1,0:T(8,128)S(1)} collective-permute-done((f32[80,512]{1,0:T(8,128)S(1)}, f32[80,512]{1,0:T(8,128)S(1)}, u32[]{:S(2)}, u32[]{:S(2)}) %collective-permute-start.3) | collective-permute-done | bytes 163872 | tf_op jit(solution)/shard_map/ppermute | solution.py:323
  20.9 0.0 copy-start.4
  20.9 0.3 markov.1
  21.2 1.5 %collective-permute-start.5 = (f32[32,512]{1,0:T(8,128)S(1)}, f32[32,512]{1,0:T(8,128)S(1)}, u32[]{:S(2)}, u32[]{:S(2)}) collective-permute-start(f32[32,512]{1,0:T(8,128)S(1)} %get-tuple-element.28), channel_id=1, source_target_pairs={{0,1},{1,0},{2,3},{3,2},{4,5},{5,4},{6,7},{7,6},{8,9},{9,8},{10,11... | collective-permute-start | bytes 196616 | tf_op jit(solution)/shard_map/ppermute | solution.py:326
  22.7 0.9 %collective-permute-done.5.got_ref = f32[32,512]{1,0:T(8,128)S(1)} collective-permute-done((f32[32,512]{1,0:T(8,128)S(1)}, f32[32,512]{1,0:T(8,128)S(1)}, u32[]{:S(2)}, u32[]{:S(2)}) %collective-permute-start.5) | collective-permute-done | bytes 65568 | tf_op jit(solution)/shard_map/ppermute | solution.py:326
  23.6 0.6 turn.1
  24.2 0.7 %collective-permute-start.6 = (f32[32,512]{1,0:T(8,128)S(1)}, f32[32,512]{1,0:T(8,128)S(1)}, u32[]{:S(2)}, u32[]{:S(2)}) collective-permute-start(f32[32,512]{1,0:T(8,128)S(1)} %get-tuple-element.32), channel_id=1, source_target_pairs={{8,16},{16,8},{24,32},{32,24},{40,48},{48,40},{56,64},{64,56},{72,... | collective-permute-start | bytes 196616 | tf_op jit(solution)/shard_map/ppermute | solution.py:329
  24.9 5.8 %collective-permute-start.7 = (f32[32,512]{1,0:T(8,128)S(1)}, f32[32,512]{1,0:T(8,128)S(1)}, u32[]{:S(2)}, u32[]{:S(2)}) collective-permute-start(f32[32,512]{1,0:T(8,128)S(1)} %get-tuple-element.33), channel_id=1, source_target_pairs={{0,8},{8,0},{16,24},{24,16},{32,40},{40,32},{48,56},{56,48},{64,72... | collective-permute-start | bytes 196616 | tf_op jit(solution)/shard_map/ppermute | solution.py:330
  30.7 1.7 %collective-permute-done.7.pair_ref = f32[32,512]{1,0:T(8,128)S(1)} collective-permute-done((f32[32,512]{1,0:T(8,128)S(1)}, f32[32,512]{1,0:T(8,128)S(1)}, u32[]{:S(2)}, u32[]{:S(2)}) %collective-permute-start.7) | collective-permute-done | bytes 65568 | tf_op jit(solution)/shard_map/ppermute | solution.py:330
  32.4 1.4 %collective-permute-start.10 = (f32[40,512]{1,0:T(8,128)S(1)}, f32[40,512]{1,0:T(8,128)S(1)}, u32[]{:S(2)}, u32[]{:S(2)}) collective-permute-start(f32[40,512]{1,0:T(8,128)S(1)} %merge_with_demand.1.own_ref), channel_id=1, source_target_pairs={{0,4},{2,6},{4,0},{6,2},{1,5},{3,7},{5,1},{7,3},{8,12},{10,14},{12... | collective-permute-start | bytes 245768 | tf_op jit(solution)/shard_map/ppermute | solution.py:323
  33.8 1.8 %collective-permute-start.9 = (f32[40,512]{1,0:T(8,128)S(1)}, f32[40,512]{1,0:T(8,128)S(1)}, u32[]{:S(2)}, u32[]{:S(2)}) collective-permute-start(f32[40,512]{1,0:T(8,128)S(1)} %merge_with_demand.1.own_ref), channel_id=1, source_target_pairs={{0,6},{2,4},{4,2},{6,0},{1,7},{3,5},{5,3},{7,1},{8,14},{10,12},{12... | collective-permute-start | bytes 245768 | tf_op jit(solution)/shard_map/ppermute | solution.py:323
  35.6 1.7 %collective-permute-done.10.three_ref = f32[40,512]{1,0:T(8,128)S(1)} collective-permute-done((f32[40,512]{1,0:T(8,128)S(1)}, f32[40,512]{1,0:T(8,128)S(1)}, u32[]{:S(2)}, u32[]{:S(2)}) %collective-permute-start.10) | collective-permute-done | bytes 81952 | tf_op jit(solution)/shard_map/ppermute | solution.py:323
  37.2 1.1 %collective-permute-done.9.two_ref = f32[40,512]{1,0:T(8,128)S(1)} collective-permute-done((f32[40,512]{1,0:T(8,128)S(1)}, f32[40,512]{1,0:T(8,128)S(1)}, u32[]{:S(2)}, u32[]{:S(2)}) %collective-permute-start.9) | collective-permute-done | bytes 81952 | tf_op jit(solution)/shard_map/ppermute | solution.py:323
  38.3 1.6 %collective-permute-done.8.one_ref = f32[40,512]{1,0:T(8,128)S(1)} collective-permute-done((f32[40,512]{1,0:T(8,128)S(1)}, f32[40,512]{1,0:T(8,128)S(1)}, u32[]{:S(2)}, u32[]{:S(2)}) %collective-permute-start.8) | collective-permute-done | bytes 81952 | tf_op jit(solution)/shard_map/ppermute | solution.py:323
  40.0 0.4 markov_wide.1
  40.3 2.2 %collective-permute-start.11 = (f32[80,512]{1,0:T(8,128)S(1)}, f32[80,512]{1,0:T(8,128)S(1)}, u32[]{:S(2)}, u32[]{:S(2)}) collective-permute-start(f32[80,512]{1,0:T(8,128)S(1)} %get-tuple-element.36), channel_id=1, source_target_pairs={{0,1},{1,0},{2,3},{3,2},{4,5},{5,4},{6,7},{7,6},{8,9},{9,8},{10,11... | collective-permute-start | bytes 491528 | tf_op jit(solution)/shard_map/ppermute | solution.py:326
  42.6 1.0 %collective-permute-done.11.got_ref = f32[80,512]{1,0:T(8,128)S(1)} collective-permute-done((f32[80,512]{1,0:T(8,128)S(1)}, f32[80,512]{1,0:T(8,128)S(1)}, u32[]{:S(2)}, u32[]{:S(2)}) %collective-permute-start.11) | collective-permute-done | bytes 163872 | tf_op jit(solution)/shard_map/ppermute | solution.py:326
  43.6 1.0 %close.1 = (f32[1,16,512]{2,1,0:T(8,128)}, f32[1,16,512]{2,1,0:T(8,128)}, f32[64,1,128]{2,1,0:T(1,128)S(1)}) custom-call(f32[80,512]{1,0:T(8,128)S(1)} %get-tuple-element.35.keep_ref, f32[80,512]{1,0:T(8,128)S(1)} %collective-permute-done.11.got_ref, f32[80,512]{1,0:T(8,128)S(1)} %merge_with_fixed.1.own_ref, ...), custom_call_target="tpu_custom_call" | custom-call | tf_op jit(solution)/shard_map/close/pallas_call | solution.py:408
  44.7 19.2 %all_to_all.5.terms_ref = f32[64,1,128]{2,1,0:T(1,128)S(1)} all-to-all(f32[64,1,128]{2,1,0:T(1,128)S(1)} %get-tuple-element.40), channel_id=1, replica_groups=mesh['dur'=32,'x'=4,'core'=2] {'dur','core'}, dimensions={0} | all-to-all | bytes 65536 | tf_op jit(solution)/shard_map/all_to_all | solution.py:420
  63.9 0.6 demand.1
  (23 shorter events, 0.1 us)
Async XLA Ops:
  0.6 7.8 %copy-start.8 = (f32[1,16,512]{2,1,0:T(8,128)S(1)}, f32[1,16,512]{2,1,0:T(8,128)}, u32[]{:S(2)}) copy-start(f32[1,16,512]{2,1,0:T(8,128)} %mass_ref.3) | copy-start | bytes 98308
  0.6 7.7 %copy-start = (f32[1,16,512]{2,1,0:T(8,128)S(1)}, f32[1,16,512]{2,1,0:T(8,128)}, u32[]{:S(2)}) copy-start(f32[1,16,512]{2,1,0:T(8,128)} %rest_3_.1) | copy-start | bytes 98308
  0.7 7.7 %copy-start.6 = (f32[2,1,16,512]{3,2,1,0:T(8,128)S(1)}, f32[2,1,16,512]{3,2,1,0:T(8,128)}, u32[]{:S(2)}) copy-start(f32[2,1,16,512]{3,2,1,0:T(8,128)} %lam_ref.3) | copy-start | bytes 196612
  0.7 7.7 %copy-start.5 = (s32[2,1,16,512]{3,2,1,0:T(8,128)S(1)}, s32[2,1,16,512]{3,2,1,0:T(8,128)}, u32[]{:S(2)}) copy-start(s32[2,1,16,512]{3,2,1,0:T(8,128)} %bracket_ref.5) | copy-start | bytes 196612
  2.3 6.8 %collective-permute-start = (f32[32,512]{1,0:T(8,128)S(1)}, f32[32,512]{1,0:T(8,128)S(1)}, u32[]{:S(2)}, u32[]{:S(2)}) collective-permute-start(f32[32,512]{1,0:T(8,128)S(1)} %get-tuple-element.23), channel_id=1, source_target_pairs={{8,16},{16,8},{24,32},{32,24},{40,48},{48,40},{56,64},{64,56},{72,... | collective-permute-start | bytes 196616 | tf_op jit(solution)/shard_map/ppermute | solution.py:329
  2.9 7.1 %copy-start.7 = (f32[1,16,512]{2,1,0:T(8,128)S(1)}, f32[1,16,512]{2,1,0:T(8,128)}, u32[]{:S(2)}) copy-start(f32[1,16,512]{2,1,0:T(8,128)} %value_ref.3) | copy-start | bytes 98308
  2.9 7.1 %collective-permute-start.1 = (f32[32,512]{1,0:T(8,128)S(1)}, f32[32,512]{1,0:T(8,128)S(1)}, u32[]{:S(2)}, u32[]{:S(2)}) collective-permute-start(f32[32,512]{1,0:T(8,128)S(1)} %get-tuple-element.24), channel_id=1, source_target_pairs={{0,8},{8,0},{16,24},{24,16},{32,40},{40,32},{48,56},{56,48},{64,72... | collective-permute-start | bytes 196616 | tf_op jit(solution)/shard_map/ppermute | solution.py:330
  10.0 3.7 %copy-start.9 = (f32[128,128]{1,0:T(8,128)S(1)}, f32[128,128]{1,0:T(8,128)}, u32[]{:S(2)}) copy-start(f32[128,128]{1,0:T(8,128)} %markov_ref.1) | copy-start | bytes 196612
  10.1 5.8 %collective-permute-start.4 = (f32[80,512]{1,0:T(8,128)S(1)}, f32[80,512]{1,0:T(8,128)S(1)}, u32[]{:S(2)}, u32[]{:S(2)}) collective-permute-start(f32[80,512]{1,0:T(8,128)S(1)} %merge_with_fixed.1.own_ref), channel_id=1, source_target_pairs={{0,4},{2,6},{4,0},{6,2},{1,5},{3,7},{5,1},{7,3},{8,12},{10,14},{12... | collective-permute-start | bytes 491528 | tf_op jit(solution)/shard_map/ppermute | solution.py:323
  12.9 8.0 %collective-permute-start.3 = (f32[80,512]{1,0:T(8,128)S(1)}, f32[80,512]{1,0:T(8,128)S(1)}, u32[]{:S(2)}, u32[]{:S(2)}) collective-permute-start(f32[80,512]{1,0:T(8,128)S(1)} %merge_with_fixed.1.own_ref), channel_id=1, source_target_pairs={{0,6},{2,4},{4,2},{6,0},{1,7},{3,5},{5,3},{7,1},{8,14},{10,12},{12... | collective-permute-start | bytes 491528 | tf_op jit(solution)/shard_map/ppermute | solution.py:323
  13.8 7.1 %collective-permute-start.2 = (f32[80,512]{1,0:T(8,128)S(1)}, f32[80,512]{1,0:T(8,128)S(1)}, u32[]{:S(2)}, u32[]{:S(2)}) collective-permute-start(f32[80,512]{1,0:T(8,128)S(1)} %merge_with_fixed.1.own_ref), channel_id=1, source_target_pairs={{0,2},{2,0},{4,6},{6,4},{1,3},{3,1},{5,7},{7,5},{8,10},{10,8},{12,... | collective-permute-start | bytes 491528 | tf_op jit(solution)/shard_map/ppermute | solution.py:323
  20.9 2.7 %copy-start.1 = (s32[2,1,16,512]{3,2,1,0:T(8,128)S(1)}, s32[2,1,16,512]{3,2,1,0:T(8,128)}, u32[]{:S(2)}) copy-start(s32[2,1,16,512]{3,2,1,0:T(8,128)} %fwd_bracket_ref.1) | copy-start | bytes 196612
  20.9 2.7 %copy-start.2 = (f32[2,1,16,512]{3,2,1,0:T(8,128)S(1)}, f32[2,1,16,512]{3,2,1,0:T(8,128)}, u32[]{:S(2)}) copy-start(f32[2,1,16,512]{3,2,1,0:T(8,128)} %fwd_weight_ref.1) | copy-start | bytes 196612
  20.9 2.7 %copy-start.3 = (s32[2,1,16,512]{3,2,1,0:T(8,128)S(1)}, s32[2,1,16,512]{3,2,1,0:T(8,128)}, u32[]{:S(2)}) copy-start(s32[2,1,16,512]{3,2,1,0:T(8,128)} %step_ref.3) | copy-start | bytes 196612
  20.9 2.7 %copy-start.4 = (f32[2,1,16,512]{3,2,1,0:T(8,128)S(1)}, f32[2,1,16,512]{3,2,1,0:T(8,128)}, u32[]{:S(2)}) copy-start(f32[2,1,16,512]{3,2,1,0:T(8,128)} %omega_ref.3) | copy-start | bytes 196612
  21.2 2.4 %collective-permute-start.5 = (f32[32,512]{1,0:T(8,128)S(1)}, f32[32,512]{1,0:T(8,128)S(1)}, u32[]{:S(2)}, u32[]{:S(2)}) collective-permute-start(f32[32,512]{1,0:T(8,128)S(1)} %get-tuple-element.28), channel_id=1, source_target_pairs={{0,1},{1,0},{2,3},{3,2},{4,5},{5,4},{6,7},{7,6},{8,9},{9,8},{10,11... | collective-permute-start | bytes 196616 | tf_op jit(solution)/shard_map/ppermute | solution.py:326
  24.2 6.5 %collective-permute-start.6 = (f32[32,512]{1,0:T(8,128)S(1)}, f32[32,512]{1,0:T(8,128)S(1)}, u32[]{:S(2)}, u32[]{:S(2)}) collective-permute-start(f32[32,512]{1,0:T(8,128)S(1)} %get-tuple-element.32), channel_id=1, source_target_pairs={{8,16},{16,8},{24,32},{32,24},{40,48},{48,40},{56,64},{64,56},{72,... | collective-permute-start | bytes 196616 | tf_op jit(solution)/shard_map/ppermute | solution.py:329
  24.9 7.5 %collective-permute-start.7 = (f32[32,512]{1,0:T(8,128)S(1)}, f32[32,512]{1,0:T(8,128)S(1)}, u32[]{:S(2)}, u32[]{:S(2)}) collective-permute-start(f32[32,512]{1,0:T(8,128)S(1)} %get-tuple-element.33), channel_id=1, source_target_pairs={{0,8},{8,0},{16,24},{24,16},{32,40},{40,32},{48,56},{56,48},{64,72... | collective-permute-start | bytes 196616 | tf_op jit(solution)/shard_map/ppermute | solution.py:330
  32.4 4.9 %collective-permute-start.10 = (f32[40,512]{1,0:T(8,128)S(1)}, f32[40,512]{1,0:T(8,128)S(1)}, u32[]{:S(2)}, u32[]{:S(2)}) collective-permute-start(f32[40,512]{1,0:T(8,128)S(1)} %merge_with_demand.1.own_ref), channel_id=1, source_target_pairs={{0,4},{2,6},{4,0},{6,2},{1,5},{3,7},{5,1},{7,3},{8,12},{10,14},{12... | collective-permute-start | bytes 245768 | tf_op jit(solution)/shard_map/ppermute | solution.py:323
  33.8 4.5 %collective-permute-start.9 = (f32[40,512]{1,0:T(8,128)S(1)}, f32[40,512]{1,0:T(8,128)S(1)}, u32[]{:S(2)}, u32[]{:S(2)}) collective-permute-start(f32[40,512]{1,0:T(8,128)S(1)} %merge_with_demand.1.own_ref), channel_id=1, source_target_pairs={{0,6},{2,4},{4,2},{6,0},{1,7},{3,5},{5,3},{7,1},{8,14},{10,12},{12... | collective-permute-start | bytes 245768 | tf_op jit(solution)/shard_map/ppermute | solution.py:323
  35.6 4.4 %collective-permute-start.8 = (f32[40,512]{1,0:T(8,128)S(1)}, f32[40,512]{1,0:T(8,128)S(1)}, u32[]{:S(2)}, u32[]{:S(2)}) collective-permute-start(f32[40,512]{1,0:T(8,128)S(1)} %merge_with_demand.1.own_ref), channel_id=1, source_target_pairs={{0,2},{2,0},{4,6},{6,4},{1,3},{3,1},{5,7},{7,5},{8,10},{10,8},{12,... | collective-permute-start | bytes 245768 | tf_op jit(solution)/shard_map/ppermute | solution.py:323
  40.3 3.3 %collective-permute-start.11 = (f32[80,512]{1,0:T(8,128)S(1)}, f32[80,512]{1,0:T(8,128)S(1)}, u32[]{:S(2)}, u32[]{:S(2)}) collective-permute-start(f32[80,512]{1,0:T(8,128)S(1)} %get-tuple-element.36), channel_id=1, source_target_pairs={{0,1},{1,0},{2,3},{3,2},{4,5},{5,4},{6,7},{7,6},{8,9},{9,8},{10,11... | collective-permute-start | bytes 491528 | tf_op jit(solution)/shard_map/ppermute | solution.py:326

commit v6 on v5

--- a/solution.py
+++ b/solution.py
@@ -16,7 +16,6 @@
 F32 = jnp.float32
 BF16 = jnp.bfloat16
 VMEM = pl.BlockSpec(memory_space=pltpu.VMEM)
-SMEM = pl.BlockSpec(memory_space=pltpu.SMEM)
 
 
 def in_vmem(*arrays):
@@ -131,8 +130,11 @@
 
 
 def weights_kernel(markov_ref, tax_ref, back_ref, ahead_ref, rates_ref, flip_ref):
+    taxes = tax_ref[...].reshape(1, 2)
     for quarter in range(2):
-        rates_ref[quarter : quarter + 1, :] = jnp.full((1, LANES), tax_ref[quarter], F32)
+        tax = jnp.broadcast_to(taxes[:, quarter : quarter + 1], (1, LANES))
+        rates_ref[quarter : quarter + 1, :] = tax
+        rates_ref[2 + quarter : 3 + quarter, :] = 1.0 / (1.0 + tax)
     chip = lax.axis_index("x")
     states = markov_ref.shape[0]
     wide = ahead_ref.shape[0] // 2
@@ -145,11 +147,10 @@
     ahead_ref[wide:, :] = low
 
 
-def fixed_kernel(scale, energy_ref, mass_ref, bracket_ref, lam_ref, tax_ref, out_ref):
+def fixed_kernel(scale, energy_ref, mass_ref, bracket_ref, out_ref):
     rows = energy_ref.shape[1]
-    out_ref[:rows, :] = scale * mass_ref[0] * energy_ref[0] / (1.0 + tax_ref[0])
-    out_ref[rows : 2 * rows, :] = bracket_ref[0, 0].astype(F32)
-    out_ref[2 * rows :, :] = lam_ref[0, 0]
+    out_ref[:rows, :] = scale * mass_ref[0] * energy_ref[0]
+    out_ref[rows:, :] = bracket_ref[0, 0].astype(F32)
 
 
 def open_kernel(
@@ -161,7 +162,8 @@
     store_halo(pair_ref, other_ref, to_plus, to_minus, value_ref[0])
 
 
-def merge_kernel(self_ref, value_ref, other_ref, pair_ref, rider_ref, out_ref):
+def merge_kernel(self_ref, value_ref, other_ref, pair_ref, *rest):
+    *rider_refs, out_ref = rest
     rows = self_ref.shape[0]
     level = lax.axis_index("dur")
     value = value_ref[...].reshape(self_ref.shape)
@@ -170,7 +172,11 @@
     incoming = pair_ref[:rows, :] + jnp.where(alone, 0.0, other_ref[:rows, :])
     out_ref[:rows, :] = self_ref[...] + incoming
     out_ref[rows : 2 * rows, :] = (1.0 - adjust_share) * value + adjust_share * 0.5 * beside
-    out_ref[2 * rows :, :] = rider_ref[...]
+    top = 2 * rows
+    for ref in rider_refs:
+        rider = ref[0, 0] if len(ref.shape) == 4 else ref[...]
+        out_ref[top : top + rider.shape[0], :] = rider
+        top += rider.shape[0]
 
 
 def place_field(refs, part, rows, field_ref):
@@ -231,7 +237,7 @@
         keep_ref[part, :] = total_ref[pl.ds(pl.multiple_of(k * wide + core * rows, rows), rows), :]
         send_ref[part, :] = total_ref[pl.ds(pl.multiple_of(k * wide + (1 - core) * rows, rows), rows), :]
     for shift, ref in zip(SHIFTS, refs):
-        terms_ref[chip ^ shift] = ref[2 * rows :, :]
+        terms_ref[chip ^ shift] = ref[2 * rows : 2 * rows + demand_ref.shape[0], :]
     demand_ref[...] = (terms_ref[0] + terms_ref[1]) + (terms_ref[2] + terms_ref[3])
 
 
@@ -247,7 +253,7 @@
     share = energy_ref[0]
     spent = density * (share * lax.rsqrt(interp))
     half = demand_ref.shape[0]
-    demand_ref[...] = (scale / (1.0 + tax)) * sum(spent[k : k + half] for k in range(0, rows, half))
+    demand_ref[...] = (scale * rates_ref[3:4, :1]) * sum(spent[k : k + half] for k in range(0, rows, half))
     value = gross_rate * interp * (1.0 + tax * share)
     moved = push_assets(density, fwd_bracket_ref[1, 0], fwd_weight_ref[1, 0], parts_ref, sums_ref)
     to_self, to_plus, to_minus = level_shares(moved, step_ref[1, 0], omega_ref[1, 0])
@@ -264,24 +270,26 @@
     )
 
 
-def close_kernel(keep_ref, got_ref, own_ref, *rest):
-    (*other_refs, energy_ref, rates_ref, demand_ref, value_ref, mass_ref, terms_ref, out_ref, spent_ref, sems) = rest
+def close_kernel(keep_ref, got_ref, *rest):
+    (*rider_refs, energy_ref, rates_ref, demand_ref, value_ref, mass_ref, terms_ref, out_ref, spent_ref, sems) = rest
     rows = energy_ref.shape[1]
     chip = lax.axis_index("x")
+    tax, shrink = rates_ref[:1, :1], rates_ref[2:3, :1]
     out_ref[1, 0] = keep_ref[:rows, :] + got_ref[:rows, :]
     mass_copy = pltpu.make_async_copy(out_ref.at[1], mass_ref, sems.at[1])
     mass_copy.start()
     value_copy = pltpu.make_async_copy(out_ref.at[0], value_ref, sems.at[0])
-    for shift, ref in zip(SHIFTS, (own_ref, *other_refs)):
+    for shift, ref, later_ref in zip(SHIFTS, rider_refs[: len(SHIFTS)], rider_refs[len(SHIFTS) :]):
         part = pl.ds(pl.multiple_of(((chip ^ shift) + 1) * rows, rows), rows)
         bracket = ref[3 * rows : 4 * rows, :].astype(jnp.int32)
-        interp = bracket_read(keep_ref[part, :] + got_ref[part, :], bracket, ref[4 * rows :, :])
+        interp = bracket_read(keep_ref[part, :] + got_ref[part, :], bracket, later_ref[later_ref.shape[0] - rows :, :])
         spent = ref[2 * rows : 3 * rows, :] * lax.rsqrt(interp)
         spent_ref[chip ^ shift] = folded(spent)
         if shift == 0:
-            out_ref[0, 0] = gross_rate * interp * (1.0 + rates_ref[:1, :1] * energy_ref[0])
+            out_ref[0, 0] = gross_rate * interp * (1.0 + tax * energy_ref[0])
             value_copy.start()
     first = jnp.sum((spent_ref[0] + spent_ref[1]) + (spent_ref[2] + spent_ref[3]), axis=(0, 1), keepdims=True)
+    first = first * shrink
     second = jnp.sum(folded(demand_ref[...]), axis=(0, 1), keepdims=True)
     lane = lax.broadcasted_iota(jnp.int32, (1, LANES), 1)
     terms_ref[...] = jnp.broadcast_to(jnp.where(lane == 0, first, second)[None], terms_ref.shape)
@@ -336,18 +344,18 @@
             pltpu.VMEM((4 * rows, states), BF16),
             pltpu.VMEM((8, LANES), F32),
         ),
-        in_specs=[VMEM, SMEM],
+        in_specs=[VMEM] * 2,
         out_specs=(VMEM,) * 3,
         scratch_shapes=[pltpu.VMEM((states, states), F32)],
         name="weights",
-    )(*in_vmem(markov), tax)
+    )(*in_vmem(markov, tax))
     fixed = pl.pallas_call(
         functools.partial(fixed_kernel, scale),
-        out_shape=pltpu.VMEM((3 * rows, assets), F32),
-        in_specs=[VMEM] * 4 + [SMEM],
+        out_shape=pair,
+        in_specs=[VMEM] * 3,
         out_specs=VMEM,
         name="fixed",
-    )(*in_vmem(energy_share, mass_start, bwd_bracket, bwd_weight), tax)
+    )(*in_vmem(energy_share, mass_start, bwd_bracket))
     pair_out, other_out, kept = pl.pallas_call(
         open_kernel,
         out_shape=(pair, pair, slab),
@@ -359,7 +367,7 @@
     halo = over_levels(pair_out, other_out)
     mine = pl.pallas_call(
         merge_kernel,
-        out_shape=pltpu.VMEM((5 * rows, assets), F32),
+        out_shape=pltpu.VMEM((4 * rows, assets), F32),
         in_specs=[VMEM] * 5,
         out_specs=VMEM,
         name="merge_with_fixed",
@@ -387,11 +395,12 @@
     halo = over_levels(pair_out, other_out)
     mine = pl.pallas_call(
         merge_kernel,
-        out_shape=pltpu.VMEM((2 * rows + 8, assets), F32),
-        in_specs=[VMEM] * 5,
+        out_shape=pltpu.VMEM((3 * rows + 8, assets), F32),
+        in_specs=[VMEM] * 6,
         out_specs=VMEM,
         name="merge_with_demand",
-    )(*in_vmem(kept, value, *halo, second))
+    )(*in_vmem(kept, value, *halo, second, bwd_weight))
+    every_second = [mine] + over_chips(mine)
     wide = pltpu.VMEM(((1 + chips) * rows, assets), F32)
     keep, send, second = pl.pallas_call(
         markov_wide_kernel,
@@ -404,11 +413,11 @@
             pltpu.VMEM((chips, 8, assets), F32),
         ],
         name="markov_wide",
-    )(*in_vmem(mine, *over_chips(mine), *weights))
+    )(*in_vmem(*every_second, *weights))
     value_start, mass_end, terms = pl.pallas_call(
         close_kernel,
         out_shape=(block, block, pltpu.VMEM((levels * cores, 1, LANES), F32)),
-        in_specs=[VMEM] * 9,
+        in_specs=[VMEM] * 13,
         out_specs=(pl.BlockSpec(memory_space=pl.ANY),) * 2 + (VMEM,),
         scratch_shapes=[
             pltpu.VMEM((2, 1, rows, assets), F32),
@@ -416,7 +425,7 @@
             pltpu.SemaphoreType.DMA((2,)),
         ],
         name="close",
-    )(*in_vmem(keep, over_cores(send), *every_first, energy_share, rates, second))
+    )(*in_vmem(keep, over_cores(send), *every_first, *every_second, energy_share, rates, second))
     every_term = lax.all_to_all(terms, ("dur", "core"), 0, 0)
     demand = pl.pallas_call(
         demand_kernel,

time: 64.7 us -> 63.6 us (0.983)
  Pallas kernels: 5.91 us -> 4.42 us
  waiting for transfers between devices: 15.2 us -> 15.9 us
    ppermute x2, waiting for transfers between devices: 2.6 us -> 3.28 us  [over_levels(): return (other_in, lax.ppermute(pair_out, 'dur', pairs))]
    pallas_call x3, Pallas kernels: 0.72 us -> 0.05 us  [the longest x1 0.02 us: per_device(): pl.pallas_call(merge_kernel, out_shape=pltpu.VMEM((3 * rows + 8, assets),...]
    pallas_call x1, Pallas kernels: 0.76 us -> 0.1 us  [per_device(): pl.pallas_call(weights_kernel, out_shape=(pltpu.VMEM((2 * states, states)...]
  transfers between devices with their start and end apart: 12 -> 12, of which waited for: 9 -> 9; matrix products, arithmetic and copies ran while one was open for 0% -> 0% of each run, Pallas kernels for 2% -> 0%
where the time goes in v6:
time: 63.6 us; the launch traced here: 63.4 us
  starting transfers between devices  22.9 us (36%)
  blocking collectives  19.3 us (30%)
  waiting for transfers between devices  15.9 us (25%)
  Pallas kernels  4.42 us (7%)
  between operations  0.79 us (1%)
    all_to_all x1, blocking collectives, per_device(): every_term = lax.all_to_all(terms, ('dur', 'core'), 0, 0)  19.3 us
    ppermute x2, starting transfers between devices, over_levels(): return (other_in, lax.ppermute(pair_out, 'dur', pairs))  11.2 us
    ppermute x6, waiting for transfers between devices, over_chips(): lax.ppermute(array, 'x', [(i, i ^ k) for i in range(chips)])  10.7 us
    ppermute x6, starting transfers between devices, over_chips(): lax.ppermute(array, 'x', [(i, i ^ k) for i in range(chips)])  6.57 us
    ppermute x2, starting transfers between devices, over_cores(): return lax.ppermute(array, 'core', [(i, i ^ 1) for i in range(cores)])  3.71 us
    ppermute x2, waiting for transfers between devices, over_levels(): return (other_in, lax.ppermute(pair_out, 'dur', pairs))  3.28 us
    ppermute x2, waiting for transfers between devices, over_cores(): return lax.ppermute(array, 'core', [(i, i ^ 1) for i in range(cores)])  1.93 us
    pallas_call x1, Pallas kernels, per_device(): pl.pallas_call(open_kernel, out_shape=(pair, pair, slab), in_specs=[VMEM]...  1.57 us
  transfers between devices with their start and end apart: 12, of which 9 were waited for; matrix products, arithmetic and copies ran while one was open for 0% of the time, Pallas kernels for 0%

profile of v6, /device:TPU:1, one launch (start us, length us, event | category | flops | bytes accessed | tf_op | source)
XLA Modules:
  0.0 63.4 jit_solution(2081723633666039481)
XLA Ops:
  0.7 1.6 %open.1 = (f32[32,512]{1,0:T(8,128)S(1)}, f32[32,512]{1,0:T(8,128)S(1)}, f32[16,512]{1,0:T(8,128)S(1)}) custom-call(f32[1,16,512]{2,1,0:T(8,128)} %value_ref.3, f32[1,16,512]{2,1,0:T(8,128)} %mass_ref.3, s32[2,1,16,512]{3,2,1,0:T(8,128)} %fwd_bracket_ref.1, f32[2,1,16,512]{3,2,1,0:T(8,128)} %fwd_weight_ref.1, s32[2,1,16,512]{3,2,1,0:T(8,128)} %step_ref.3, ...), custom_call_target="tpu_custom_call" | custom-call | tf_op jit(solution)/shard_map/open/pallas_call | solution.py:359
  2.2 0.7 %collective-permute-start = (f32[32,512]{1,0:T(8,128)S(1)}, f32[32,512]{1,0:T(8,128)S(1)}, u32[]{:S(2)}, u32[]{:S(2)}) collective-permute-start(f32[32,512]{1,0:T(8,128)S(1)} %get-tuple-element.23), channel_id=1, source_target_pairs={{8,16},{16,8},{24,32},{32,24},{40,48},{48,40},{56,64},{64,56},{72,... | collective-permute-start | bytes 196616 | tf_op jit(solution)/shard_map/ppermute | solution.py:337
  2.9 0.0 copy-start.7
  2.9 5.4 %collective-permute-start.1 = (f32[32,512]{1,0:T(8,128)S(1)}, f32[32,512]{1,0:T(8,128)S(1)}, u32[]{:S(2)}, u32[]{:S(2)}) collective-permute-start(f32[32,512]{1,0:T(8,128)S(1)} %get-tuple-element.24), channel_id=1, source_target_pairs={{0,8},{8,0},{16,24},{24,16},{32,40},{40,32},{48,56},{56,48},{64,72... | collective-permute-start | bytes 196616 | tf_op jit(solution)/shard_map/ppermute | solution.py:338
  8.4 0.0 collective-permute-done.other_ref
  8.4 1.6 %collective-permute-done.1.pair_ref = f32[32,512]{1,0:T(8,128)S(1)} collective-permute-done((f32[32,512]{1,0:T(8,128)S(1)}, f32[32,512]{1,0:T(8,128)S(1)}, u32[]{:S(2)}, u32[]{:S(2)}) %collective-permute-start.1) | collective-permute-done | bytes 65568 | tf_op jit(solution)/shard_map/ppermute | solution.py:338
  10.0 2.8 %collective-permute-start.4 = (f32[64,512]{1,0:T(8,128)S(1)}, f32[64,512]{1,0:T(8,128)S(1)}, u32[]{:S(2)}, u32[]{:S(2)}) collective-permute-start(f32[64,512]{1,0:T(8,128)S(1)} %merge_with_fixed.1.own_ref.rest_0_), channel_id=1, source_target_pairs={{0,4},{2,6},{4,0},{6,2},{1,5},{3,7},{5,1},{7,3},{8,12},{10,14},{12... | collective-permute-start | bytes 393224 | tf_op jit(solution)/shard_map/ppermute | solution.py:331
  12.9 0.9 %collective-permute-start.3 = (f32[64,512]{1,0:T(8,128)S(1)}, f32[64,512]{1,0:T(8,128)S(1)}, u32[]{:S(2)}, u32[]{:S(2)}) collective-permute-start(f32[64,512]{1,0:T(8,128)S(1)} %merge_with_fixed.1.own_ref.rest_0_), channel_id=1, source_target_pairs={{0,6},{2,4},{4,2},{6,0},{1,7},{3,5},{5,3},{7,1},{8,14},{10,12},{12... | collective-permute-start | bytes 393224 | tf_op jit(solution)/shard_map/ppermute | solution.py:331
  13.7 0.1 weights.1
  13.9 1.6 %collective-permute-done.4.three_ref.rest_3_ = f32[64,512]{1,0:T(8,128)S(1)} collective-permute-done((f32[64,512]{1,0:T(8,128)S(1)}, f32[64,512]{1,0:T(8,128)S(1)}, u32[]{:S(2)}, u32[]{:S(2)}) %collective-permute-start.4) | collective-permute-done | bytes 131104 | tf_op jit(solution)/shard_map/ppermute | solution.py:331
  15.5 4.0 %collective-permute-done.3.two_ref.rest_2_ = f32[64,512]{1,0:T(8,128)S(1)} collective-permute-done((f32[64,512]{1,0:T(8,128)S(1)}, f32[64,512]{1,0:T(8,128)S(1)}, u32[]{:S(2)}, u32[]{:S(2)}) %collective-permute-start.3) | collective-permute-done | bytes 131104 | tf_op jit(solution)/shard_map/ppermute | solution.py:331
  19.5 0.0 collective-permute-done.2.one_ref.rest_1_
  19.5 0.0 copy-start.4
  19.5 0.0 copy-start.6
  19.5 0.3 markov.1
  19.8 1.9 %collective-permute-start.5 = (f32[32,512]{1,0:T(8,128)S(1)}, f32[32,512]{1,0:T(8,128)S(1)}, u32[]{:S(2)}, u32[]{:S(2)}) collective-permute-start(f32[32,512]{1,0:T(8,128)S(1)} %get-tuple-element.28), channel_id=1, source_target_pairs={{0,1},{1,0},{2,3},{3,2},{4,5},{5,4},{6,7},{7,6},{8,9},{9,8},{10,11... | collective-permute-start | bytes 196616 | tf_op jit(solution)/shard_map/ppermute | solution.py:334
  21.6 0.9 %collective-permute-done.5.got_ref = f32[32,512]{1,0:T(8,128)S(1)} collective-permute-done((f32[32,512]{1,0:T(8,128)S(1)}, f32[32,512]{1,0:T(8,128)S(1)}, u32[]{:S(2)}, u32[]{:S(2)}) %collective-permute-start.5) | collective-permute-done | bytes 65568 | tf_op jit(solution)/shard_map/ppermute | solution.py:334
  22.6 0.6 turn.1
  23.1 0.7 %collective-permute-start.6 = (f32[32,512]{1,0:T(8,128)S(1)}, f32[32,512]{1,0:T(8,128)S(1)}, u32[]{:S(2)}, u32[]{:S(2)}) collective-permute-start(f32[32,512]{1,0:T(8,128)S(1)} %get-tuple-element.32), channel_id=1, source_target_pairs={{8,16},{16,8},{24,32},{32,24},{40,48},{48,40},{56,64},{64,56},{72,... | collective-permute-start | bytes 196616 | tf_op jit(solution)/shard_map/ppermute | solution.py:337
  23.8 5.8 %collective-permute-start.7 = (f32[32,512]{1,0:T(8,128)S(1)}, f32[32,512]{1,0:T(8,128)S(1)}, u32[]{:S(2)}, u32[]{:S(2)}) collective-permute-start(f32[32,512]{1,0:T(8,128)S(1)} %get-tuple-element.33), channel_id=1, source_target_pairs={{0,8},{8,0},{16,24},{24,16},{32,40},{40,32},{48,56},{56,48},{64,72... | collective-permute-start | bytes 196616 | tf_op jit(solution)/shard_map/ppermute | solution.py:338
  29.6 1.7 %collective-permute-done.7.pair_ref = f32[32,512]{1,0:T(8,128)S(1)} collective-permute-done((f32[32,512]{1,0:T(8,128)S(1)}, f32[32,512]{1,0:T(8,128)S(1)}, u32[]{:S(2)}, u32[]{:S(2)}) %collective-permute-start.7) | collective-permute-done | bytes 65568 | tf_op jit(solution)/shard_map/ppermute | solution.py:338
  31.3 1.4 %collective-permute-start.10 = (f32[56,512]{1,0:T(8,128)S(1)}, f32[56,512]{1,0:T(8,128)S(1)}, u32[]{:S(2)}, u32[]{:S(2)}) collective-permute-start(f32[56,512]{1,0:T(8,128)S(1)} %merge_with_demand.1.own_ref.rest_4_), channel_id=1, source_target_pairs={{0,4},{2,6},{4,0},{6,2},{1,5},{3,7},{5,1},{7,3},{8,12},{10,14},{12... | collective-permute-start | bytes 344072 | tf_op jit(solution)/shard_map/ppermute | solution.py:331
  32.7 1.4 %collective-permute-start.9 = (f32[56,512]{1,0:T(8,128)S(1)}, f32[56,512]{1,0:T(8,128)S(1)}, u32[]{:S(2)}, u32[]{:S(2)}) collective-permute-start(f32[56,512]{1,0:T(8,128)S(1)} %merge_with_demand.1.own_ref.rest_4_), channel_id=1, source_target_pairs={{0,6},{2,4},{4,2},{6,0},{1,7},{3,5},{5,3},{7,1},{8,14},{10,12},{12... | collective-permute-start | bytes 344072 | tf_op jit(solution)/shard_map/ppermute | solution.py:331
  34.2 2.4 %collective-permute-done.10.three_ref.rest_7_ = f32[56,512]{1,0:T(8,128)S(1)} collective-permute-done((f32[56,512]{1,0:T(8,128)S(1)}, f32[56,512]{1,0:T(8,128)S(1)}, u32[]{:S(2)}, u32[]{:S(2)}) %collective-permute-start.10) | collective-permute-done | bytes 114720 | tf_op jit(solution)/shard_map/ppermute | solution.py:331
  36.6 2.3 %collective-permute-done.9.two_ref.rest_6_ = f32[56,512]{1,0:T(8,128)S(1)} collective-permute-done((f32[56,512]{1,0:T(8,128)S(1)}, f32[56,512]{1,0:T(8,128)S(1)}, u32[]{:S(2)}, u32[]{:S(2)}) %collective-permute-start.9) | collective-permute-done | bytes 114720 | tf_op jit(solution)/shard_map/ppermute | solution.py:331
  38.8 0.5 collective-permute-done.8.one_ref.rest_5_
  39.3 0.4 markov_wide.1
  39.7 1.8 %collective-permute-start.11 = (f32[80,512]{1,0:T(8,128)S(1)}, f32[80,512]{1,0:T(8,128)S(1)}, u32[]{:S(2)}, u32[]{:S(2)}) collective-permute-start(f32[80,512]{1,0:T(8,128)S(1)} %get-tuple-element.36), channel_id=1, source_target_pairs={{0,1},{1,0},{2,3},{3,2},{4,5},{5,4},{6,7},{7,6},{8,9},{9,8},{10,11... | collective-permute-start | bytes 491528 | tf_op jit(solution)/shard_map/ppermute | solution.py:334
  41.5 1.0 %collective-permute-done.11.got_ref = f32[80,512]{1,0:T(8,128)S(1)} collective-permute-done((f32[80,512]{1,0:T(8,128)S(1)}, f32[80,512]{1,0:T(8,128)S(1)}, u32[]{:S(2)}, u32[]{:S(2)}) %collective-permute-start.11) | collective-permute-done | bytes 163872 | tf_op jit(solution)/shard_map/ppermute | solution.py:334
  42.6 0.9 %close.1 = (f32[1,16,512]{2,1,0:T(8,128)}, f32[1,16,512]{2,1,0:T(8,128)}, f32[64,1,128]{2,1,0:T(1,128)S(1)}) custom-call(f32[80,512]{1,0:T(8,128)S(1)} %get-tuple-element.35.keep_ref, f32[80,512]{1,0:T(8,128)S(1)} %collective-permute-done.11.got_ref, f32[64,512]{1,0:T(8,128)S(1)} %merge_with_fixed.1.own_ref.rest_0_, ...), custom_call_target="tpu_custom_call" | custom-call | tf_op jit(solution)/shard_map/close/pallas_call | solution.py:417
  43.5 19.3 %all_to_all.5.terms_ref = f32[64,1,128]{2,1,0:T(1,128)S(1)} all-to-all(f32[64,1,128]{2,1,0:T(1,128)S(1)} %get-tuple-element.40), channel_id=1, replica_groups=mesh['dur'=32,'x'=4,'core'=2] {'dur','core'}, dimensions={0} | all-to-all | bytes 65536 | tf_op jit(solution)/shard_map/all_to_all | solution.py:429
  62.8 0.6 demand.1
  (25 shorter events, 0.1 us)
Async XLA Ops:
  0.6 7.7 %copy-start.8 = (f32[1,16,512]{2,1,0:T(8,128)S(1)}, f32[1,16,512]{2,1,0:T(8,128)}, u32[]{:S(2)}) copy-start(f32[1,16,512]{2,1,0:T(8,128)} %mass_ref.3) | copy-start | bytes 98308
  0.6 7.7 %copy-start = (f32[1,16,512]{2,1,0:T(8,128)S(1)}, f32[1,16,512]{2,1,0:T(8,128)}, u32[]{:S(2)}) copy-start(f32[1,16,512]{2,1,0:T(8,128)} %rest_8_.1) | copy-start | bytes 98308
  0.7 7.7 %copy-start.5 = (s32[2,1,16,512]{3,2,1,0:T(8,128)S(1)}, s32[2,1,16,512]{3,2,1,0:T(8,128)}, u32[]{:S(2)}) copy-start(s32[2,1,16,512]{3,2,1,0:T(8,128)} %bracket_ref.5) | copy-start | bytes 196612
  2.2 6.1 %collective-permute-start = (f32[32,512]{1,0:T(8,128)S(1)}, f32[32,512]{1,0:T(8,128)S(1)}, u32[]{:S(2)}, u32[]{:S(2)}) collective-permute-start(f32[32,512]{1,0:T(8,128)S(1)} %get-tuple-element.23), channel_id=1, source_target_pairs={{8,16},{16,8},{24,32},{32,24},{40,48},{48,40},{56,64},{64,56},{72,... | collective-permute-start | bytes 196616 | tf_op jit(solution)/shard_map/ppermute | solution.py:337
  2.9 7.1 %copy-start.7 = (f32[1,16,512]{2,1,0:T(8,128)S(1)}, f32[1,16,512]{2,1,0:T(8,128)}, u32[]{:S(2)}) copy-start(f32[1,16,512]{2,1,0:T(8,128)} %value_ref.3) | copy-start | bytes 98308
  2.9 7.1 %collective-permute-start.1 = (f32[32,512]{1,0:T(8,128)S(1)}, f32[32,512]{1,0:T(8,128)S(1)}, u32[]{:S(2)}, u32[]{:S(2)}) collective-permute-start(f32[32,512]{1,0:T(8,128)S(1)} %get-tuple-element.24), channel_id=1, source_target_pairs={{0,8},{8,0},{16,24},{24,16},{32,40},{40,32},{48,56},{56,48},{64,72... | collective-permute-start | bytes 196616 | tf_op jit(solution)/shard_map/ppermute | solution.py:338
  10.0 3.7 %copy-start.9 = (f32[128,128]{1,0:T(8,128)S(1)}, f32[128,128]{1,0:T(8,128)}, u32[]{:S(2)}) copy-start(f32[128,128]{1,0:T(8,128)} %markov_ref.1) | copy-start | bytes 196612
  10.0 3.7 %copy-start.10 = (f32[2]{0:T(128)S(1)}, f32[2]{0:T(128)}, u32[]{:S(2)}) copy-start(f32[2]{0:T(128)} %tax_ref.1) | copy-start | bytes 28
  10.0 5.4 %collective-permute-start.4 = (f32[64,512]{1,0:T(8,128)S(1)}, f32[64,512]{1,0:T(8,128)S(1)}, u32[]{:S(2)}, u32[]{:S(2)}) collective-permute-start(f32[64,512]{1,0:T(8,128)S(1)} %merge_with_fixed.1.own_ref.rest_0_), channel_id=1, source_target_pairs={{0,4},{2,6},{4,0},{6,2},{1,5},{3,7},{5,1},{7,3},{8,12},{10,14},{12... | collective-permute-start | bytes 393224 | tf_op jit(solution)/shard_map/ppermute | solution.py:331
  12.9 6.6 %collective-permute-start.3 = (f32[64,512]{1,0:T(8,128)S(1)}, f32[64,512]{1,0:T(8,128)S(1)}, u32[]{:S(2)}, u32[]{:S(2)}) collective-permute-start(f32[64,512]{1,0:T(8,128)S(1)} %merge_with_fixed.1.own_ref.rest_0_), channel_id=1, source_target_pairs={{0,6},{2,4},{4,2},{6,0},{1,7},{3,5},{5,3},{7,1},{8,14},{10,12},{12... | collective-permute-start | bytes 393224 | tf_op jit(solution)/shard_map/ppermute | solution.py:331
  13.7 5.7 %collective-permute-start.2 = (f32[64,512]{1,0:T(8,128)S(1)}, f32[64,512]{1,0:T(8,128)S(1)}, u32[]{:S(2)}, u32[]{:S(2)}) collective-permute-start(f32[64,512]{1,0:T(8,128)S(1)} %merge_with_fixed.1.own_ref.rest_0_), channel_id=1, source_target_pairs={{0,2},{2,0},{4,6},{6,4},{1,3},{3,1},{5,7},{7,5},{8,10},{10,8},{12,... | collective-permute-start | bytes 393224 | tf_op jit(solution)/shard_map/ppermute | solution.py:331
  19.5 3.1 %copy-start.1 = (s32[2,1,16,512]{3,2,1,0:T(8,128)S(1)}, s32[2,1,16,512]{3,2,1,0:T(8,128)}, u32[]{:S(2)}) copy-start(s32[2,1,16,512]{3,2,1,0:T(8,128)} %fwd_bracket_ref.1) | copy-start | bytes 196612
  19.5 3.1 %copy-start.2 = (f32[2,1,16,512]{3,2,1,0:T(8,128)S(1)}, f32[2,1,16,512]{3,2,1,0:T(8,128)}, u32[]{:S(2)}) copy-start(f32[2,1,16,512]{3,2,1,0:T(8,128)} %fwd_weight_ref.1) | copy-start | bytes 196612
  19.5 3.1 %copy-start.3 = (s32[2,1,16,512]{3,2,1,0:T(8,128)S(1)}, s32[2,1,16,512]{3,2,1,0:T(8,128)}, u32[]{:S(2)}) copy-start(s32[2,1,16,512]{3,2,1,0:T(8,128)} %step_ref.3) | copy-start | bytes 196612
  19.5 3.1 %copy-start.4 = (f32[2,1,16,512]{3,2,1,0:T(8,128)S(1)}, f32[2,1,16,512]{3,2,1,0:T(8,128)}, u32[]{:S(2)}) copy-start(f32[2,1,16,512]{3,2,1,0:T(8,128)} %omega_ref.3) | copy-start | bytes 196612
  19.5 3.1 %copy-start.6 = (f32[2,1,16,512]{3,2,1,0:T(8,128)S(1)}, f32[2,1,16,512]{3,2,1,0:T(8,128)}, u32[]{:S(2)}) copy-start(f32[2,1,16,512]{3,2,1,0:T(8,128)} %rest_1_.1) | copy-start | bytes 196612
  19.8 2.8 %collective-permute-start.5 = (f32[32,512]{1,0:T(8,128)S(1)}, f32[32,512]{1,0:T(8,128)S(1)}, u32[]{:S(2)}, u32[]{:S(2)}) collective-permute-start(f32[32,512]{1,0:T(8,128)S(1)} %get-tuple-element.28), channel_id=1, source_target_pairs={{0,1},{1,0},{2,3},{3,2},{4,5},{5,4},{6,7},{7,6},{8,9},{9,8},{10,11... | collective-permute-start | bytes 196616 | tf_op jit(solution)/shard_map/ppermute | solution.py:334
  23.1 6.5 %collective-permute-start.6 = (f32[32,512]{1,0:T(8,128)S(1)}, f32[32,512]{1,0:T(8,128)S(1)}, u32[]{:S(2)}, u32[]{:S(2)}) collective-permute-start(f32[32,512]{1,0:T(8,128)S(1)} %get-tuple-element.32), channel_id=1, source_target_pairs={{8,16},{16,8},{24,32},{32,24},{40,48},{48,40},{56,64},{64,56},{72,... | collective-permute-start | bytes 196616 | tf_op jit(solution)/shard_map/ppermute | solution.py:337
  23.8 7.5 %collective-permute-start.7 = (f32[32,512]{1,0:T(8,128)S(1)}, f32[32,512]{1,0:T(8,128)S(1)}, u32[]{:S(2)}, u32[]{:S(2)}) collective-permute-start(f32[32,512]{1,0:T(8,128)S(1)} %get-tuple-element.33), channel_id=1, source_target_pairs={{0,8},{8,0},{16,24},{24,16},{32,40},{40,32},{48,56},{56,48},{64,72... | collective-permute-start | bytes 196616 | tf_op jit(solution)/shard_map/ppermute | solution.py:338
  31.3 5.3 %collective-permute-start.10 = (f32[56,512]{1,0:T(8,128)S(1)}, f32[56,512]{1,0:T(8,128)S(1)}, u32[]{:S(2)}, u32[]{:S(2)}) collective-permute-start(f32[56,512]{1,0:T(8,128)S(1)} %merge_with_demand.1.own_ref.rest_4_), channel_id=1, source_target_pairs={{0,4},{2,6},{4,0},{6,2},{1,5},{3,7},{5,1},{7,3},{8,12},{10,14},{12... | collective-permute-start | bytes 344072 | tf_op jit(solution)/shard_map/ppermute | solution.py:331
  32.7 6.1 %collective-permute-start.9 = (f32[56,512]{1,0:T(8,128)S(1)}, f32[56,512]{1,0:T(8,128)S(1)}, u32[]{:S(2)}, u32[]{:S(2)}) collective-permute-start(f32[56,512]{1,0:T(8,128)S(1)} %merge_with_demand.1.own_ref.rest_4_), channel_id=1, source_target_pairs={{0,6},{2,4},{4,2},{6,0},{1,7},{3,5},{5,3},{7,1},{8,14},{10,12},{12... | collective-permute-start | bytes 344072 | tf_op jit(solution)/shard_map/ppermute | solution.py:331
  34.2 5.1 %collective-permute-start.8 = (f32[56,512]{1,0:T(8,128)S(1)}, f32[56,512]{1,0:T(8,128)S(1)}, u32[]{:S(2)}, u32[]{:S(2)}) collective-permute-start(f32[56,512]{1,0:T(8,128)S(1)} %merge_with_demand.1.own_ref.rest_4_), channel_id=1, source_target_pairs={{0,2},{2,0},{4,6},{6,4},{1,3},{3,1},{5,7},{7,5},{8,10},{10,8},{12,... | collective-permute-start | bytes 344072 | tf_op jit(solution)/shard_map/ppermute | solution.py:331
  39.7 2.9 %collective-permute-start.11 = (f32[80,512]{1,0:T(8,128)S(1)}, f32[80,512]{1,0:T(8,128)S(1)}, u32[]{:S(2)}, u32[]{:S(2)}) collective-permute-start(f32[80,512]{1,0:T(8,128)S(1)} %get-tuple-element.36), channel_id=1, source_target_pairs={{0,1},{1,0},{2,3},{3,2},{4,5},{5,4},{6,7},{7,6},{8,9},{9,8},{10,11... | collective-permute-start | bytes 491528 | tf_op jit(solution)/shard_map/ppermute | solution.py:334

commit v7 on v6

--- a/solution.py
+++ b/solution.py
@@ -154,12 +154,32 @@
 
 
 def open_kernel(
-    value_ref, mass_ref, bracket_ref, weight_ref, step_ref, omega_ref, pair_ref, other_ref, self_ref, parts_ref, sums_ref
+    mass_ref, bracket_ref, weight_ref, step_ref, omega_ref, value_ref, pair_ref, other_ref, self_ref, floats_ref, ints_ref,
+    sems, parts_ref, sums_ref,
 ):
-    moved = push_assets(mass_ref[0], bracket_ref[0, 0], weight_ref[0, 0], parts_ref, sums_ref)
-    to_self, to_plus, to_minus = level_shares(moved, step_ref[0, 0], omega_ref[0, 0])
+    copies = [
+        pltpu.make_async_copy(source, target, sems.at[k])
+        for k, (source, target) in enumerate(
+            (
+                (mass_ref.at[0], floats_ref.at[0]),
+                (bracket_ref.at[0, 0], ints_ref.at[0]),
+                (weight_ref.at[0, 0], floats_ref.at[1]),
+                (step_ref.at[0, 0], ints_ref.at[1]),
+                (omega_ref.at[0, 0], floats_ref.at[2]),
+                (value_ref.at[0], floats_ref.at[3]),
+            )
+        )
+    ]
+    for copy in copies:
+        copy.start()
+    for copy in copies[:3]:
+        copy.wait()
+    moved = push_assets(floats_ref[0], ints_ref[0], floats_ref[1], parts_ref, sums_ref)
+    for copy in copies[3:]:
+        copy.wait()
+    to_self, to_plus, to_minus = level_shares(moved, ints_ref[1], floats_ref[2])
     self_ref[...] = to_self
-    store_halo(pair_ref, other_ref, to_plus, to_minus, value_ref[0])
+    store_halo(pair_ref, other_ref, to_plus, to_minus, floats_ref[3])
 
 
 def merge_kernel(self_ref, value_ref, other_ref, pair_ref, *rest):
@@ -359,11 +379,16 @@
     pair_out, other_out, kept = pl.pallas_call(
         open_kernel,
         out_shape=(pair, pair, slab),
-        in_specs=[VMEM] * 6,
+        in_specs=[pl.BlockSpec(memory_space=pl.ANY)] * 6,
         out_specs=(VMEM,) * 3,
-        scratch_shapes=push_scratch,
+        scratch_shapes=[
+            pltpu.VMEM((4, rows, assets), F32),
+            pltpu.VMEM((2, rows, assets), jnp.int32),
+            pltpu.SemaphoreType.DMA((6,)),
+            *push_scratch,
+        ],
         name="open",
-    )(value_next, mass_start, fwd_bracket, fwd_weight, dur_step, dur_weight)
+    )(mass_start, fwd_bracket, fwd_weight, dur_step, dur_weight, value_next)
     halo = over_levels(pair_out, other_out)
     mine = pl.pallas_call(
         merge_kernel,

time: 63.6 us -> 63.5 us (level)
  no operation moved by 1% of the time
where the time goes in v7:
time: 63.5 us; the launch traced here: 63.3 us
  starting transfers between devices  22.9 us (36%)
  blocking collectives  19.3 us (30%)
  waiting for transfers between devices  15.9 us (25%)
  Pallas kernels  4.31 us (7%)
  between operations  0.79 us (1%)
    all_to_all x1, blocking collectives, per_device(): every_term = lax.all_to_all(terms, ('dur', 'core'), 0, 0)  19.3 us
    ppermute x2, starting transfers between devices, over_levels(): return (other_in, lax.ppermute(pair_out, 'dur', pairs))  11.3 us
    ppermute x6, waiting for transfers between devices, over_chips(): lax.ppermute(array, 'x', [(i, i ^ k) for i in range(chips)])  10.7 us
    ppermute x6, starting transfers between devices, over_chips(): lax.ppermute(array, 'x', [(i, i ^ k) for i in range(chips)])  6.57 us
    ppermute x2, starting transfers between devices, over_cores(): return lax.ppermute(array, 'core', [(i, i ^ 1) for i in range(cores)])  3.71 us
    ppermute x2, waiting for transfers between devices, over_levels(): return (other_in, lax.ppermute(pair_out, 'dur', pairs))  3.28 us
    ppermute x2, waiting for transfers between devices, over_cores(): return lax.ppermute(array, 'core', [(i, i ^ 1) for i in range(cores)])  1.93 us
    pallas_call x1, Pallas kernels, per_device(): pl.pallas_call(open_kernel, out_shape=(pair, pair, slab), in_specs=[pl.Bl...  1.46 us
  transfers between devices with their start and end apart: 12, of which 9 were waited for; matrix products, arithmetic and copies ran while one was open for 0% of the time, Pallas kernels for 0%

profile of v7, /device:TPU:1, one launch (start us, length us, event | category | flops | bytes accessed | tf_op | source)
XLA Modules:
  0.0 63.3 jit_solution(16423539934416558029)
XLA Ops:
  0.7 1.5 %open.1 = (f32[32,512]{1,0:T(8,128)S(1)}, f32[32,512]{1,0:T(8,128)S(1)}, f32[16,512]{1,0:T(8,128)S(1)}) custom-call(f32[1,16,512]{2,1,0:T(8,128)} %mass_ref.3, s32[2,1,16,512]{3,2,1,0:T(8,128)} %fwd_bracket_ref.1, f32[2,1,16,512]{3,2,1,0:T(8,128)} %fwd_weight_ref.1, s32[2,1,16,512]{3,2,1,0:T(8,128)} %step_ref.3, f32[2,1,16,512]{3,2,1,0:T(8,128)} %omega_ref.3, ...), custom_call_target="tpu_custom_call" | custom-call | tf_op jit(solution)/shard_map/open/pallas_call | solution.py:379
  2.1 0.7 %collective-permute-start = (f32[32,512]{1,0:T(8,128)S(1)}, f32[32,512]{1,0:T(8,128)S(1)}, u32[]{:S(2)}, u32[]{:S(2)}) collective-permute-start(f32[32,512]{1,0:T(8,128)S(1)} %get-tuple-element.23), channel_id=1, source_target_pairs={{8,16},{16,8},{24,32},{32,24},{40,48},{48,40},{56,64},{64,56},{72,... | collective-permute-start | bytes 196616 | tf_op jit(solution)/shard_map/ppermute | solution.py:357
  2.8 0.0 copy-start.7
  2.8 5.4 %collective-permute-start.1 = (f32[32,512]{1,0:T(8,128)S(1)}, f32[32,512]{1,0:T(8,128)S(1)}, u32[]{:S(2)}, u32[]{:S(2)}) collective-permute-start(f32[32,512]{1,0:T(8,128)S(1)} %get-tuple-element.24), channel_id=1, source_target_pairs={{0,8},{8,0},{16,24},{24,16},{32,40},{40,32},{48,56},{56,48},{64,72... | collective-permute-start | bytes 196616 | tf_op jit(solution)/shard_map/ppermute | solution.py:358
  8.3 0.0 collective-permute-done.other_ref
  8.3 1.6 %collective-permute-done.1.pair_ref = f32[32,512]{1,0:T(8,128)S(1)} collective-permute-done((f32[32,512]{1,0:T(8,128)S(1)}, f32[32,512]{1,0:T(8,128)S(1)}, u32[]{:S(2)}, u32[]{:S(2)}) %collective-permute-start.1) | collective-permute-done | bytes 65568 | tf_op jit(solution)/shard_map/ppermute | solution.py:358
  9.9 2.8 %collective-permute-start.4 = (f32[64,512]{1,0:T(8,128)S(1)}, f32[64,512]{1,0:T(8,128)S(1)}, u32[]{:S(2)}, u32[]{:S(2)}) collective-permute-start(f32[64,512]{1,0:T(8,128)S(1)} %merge_with_fixed.1.own_ref.rest_0_), channel_id=1, source_target_pairs={{0,4},{2,6},{4,0},{6,2},{1,5},{3,7},{5,1},{7,3},{8,12},{10,14},{12... | collective-permute-start | bytes 393224 | tf_op jit(solution)/shard_map/ppermute | solution.py:351
  12.8 0.9 %collective-permute-start.3 = (f32[64,512]{1,0:T(8,128)S(1)}, f32[64,512]{1,0:T(8,128)S(1)}, u32[]{:S(2)}, u32[]{:S(2)}) collective-permute-start(f32[64,512]{1,0:T(8,128)S(1)} %merge_with_fixed.1.own_ref.rest_0_), channel_id=1, source_target_pairs={{0,6},{2,4},{4,2},{6,0},{1,7},{3,5},{5,3},{7,1},{8,14},{10,12},{12... | collective-permute-start | bytes 393224 | tf_op jit(solution)/shard_map/ppermute | solution.py:351
  13.6 0.0 collective-permute-start.2
  13.6 0.1 weights.1
  13.8 1.6 %collective-permute-done.4.three_ref.rest_3_ = f32[64,512]{1,0:T(8,128)S(1)} collective-permute-done((f32[64,512]{1,0:T(8,128)S(1)}, f32[64,512]{1,0:T(8,128)S(1)}, u32[]{:S(2)}, u32[]{:S(2)}) %collective-permute-start.4) | collective-permute-done | bytes 131104 | tf_op jit(solution)/shard_map/ppermute | solution.py:351
  15.4 4.0 %collective-permute-done.3.two_ref.rest_2_ = f32[64,512]{1,0:T(8,128)S(1)} collective-permute-done((f32[64,512]{1,0:T(8,128)S(1)}, f32[64,512]{1,0:T(8,128)S(1)}, u32[]{:S(2)}, u32[]{:S(2)}) %collective-permute-start.3) | collective-permute-done | bytes 131104 | tf_op jit(solution)/shard_map/ppermute | solution.py:351
  19.4 0.0 copy-start.4
  19.4 0.0 copy-start.6
  19.4 0.3 markov.1
  19.7 1.9 %collective-permute-start.5 = (f32[32,512]{1,0:T(8,128)S(1)}, f32[32,512]{1,0:T(8,128)S(1)}, u32[]{:S(2)}, u32[]{:S(2)}) collective-permute-start(f32[32,512]{1,0:T(8,128)S(1)} %get-tuple-element.28), channel_id=1, source_target_pairs={{0,1},{1,0},{2,3},{3,2},{4,5},{5,4},{6,7},{7,6},{8,9},{9,8},{10,11... | collective-permute-start | bytes 196616 | tf_op jit(solution)/shard_map/ppermute | solution.py:354
  21.5 0.9 %collective-permute-done.5.got_ref = f32[32,512]{1,0:T(8,128)S(1)} collective-permute-done((f32[32,512]{1,0:T(8,128)S(1)}, f32[32,512]{1,0:T(8,128)S(1)}, u32[]{:S(2)}, u32[]{:S(2)}) %collective-permute-start.5) | collective-permute-done | bytes 65568 | tf_op jit(solution)/shard_map/ppermute | solution.py:354
  22.5 0.6 turn.1
  23.0 0.7 %collective-permute-start.6 = (f32[32,512]{1,0:T(8,128)S(1)}, f32[32,512]{1,0:T(8,128)S(1)}, u32[]{:S(2)}, u32[]{:S(2)}) collective-permute-start(f32[32,512]{1,0:T(8,128)S(1)} %get-tuple-element.32), channel_id=1, source_target_pairs={{8,16},{16,8},{24,32},{32,24},{40,48},{48,40},{56,64},{64,56},{72,... | collective-permute-start | bytes 196616 | tf_op jit(solution)/shard_map/ppermute | solution.py:357
  23.7 5.8 %collective-permute-start.7 = (f32[32,512]{1,0:T(8,128)S(1)}, f32[32,512]{1,0:T(8,128)S(1)}, u32[]{:S(2)}, u32[]{:S(2)}) collective-permute-start(f32[32,512]{1,0:T(8,128)S(1)} %get-tuple-element.33), channel_id=1, source_target_pairs={{0,8},{8,0},{16,24},{24,16},{32,40},{40,32},{48,56},{56,48},{64,72... | collective-permute-start | bytes 196616 | tf_op jit(solution)/shard_map/ppermute | solution.py:358
  29.5 1.7 %collective-permute-done.7.pair_ref = f32[32,512]{1,0:T(8,128)S(1)} collective-permute-done((f32[32,512]{1,0:T(8,128)S(1)}, f32[32,512]{1,0:T(8,128)S(1)}, u32[]{:S(2)}, u32[]{:S(2)}) %collective-permute-start.7) | collective-permute-done | bytes 65568 | tf_op jit(solution)/shard_map/ppermute | solution.py:358
  31.2 1.4 %collective-permute-start.10 = (f32[56,512]{1,0:T(8,128)S(1)}, f32[56,512]{1,0:T(8,128)S(1)}, u32[]{:S(2)}, u32[]{:S(2)}) collective-permute-start(f32[56,512]{1,0:T(8,128)S(1)} %merge_with_demand.1.own_ref.rest_4_), channel_id=1, source_target_pairs={{0,4},{2,6},{4,0},{6,2},{1,5},{3,7},{5,1},{7,3},{8,12},{10,14},{12... | collective-permute-start | bytes 344072 | tf_op jit(solution)/shard_map/ppermute | solution.py:351
  32.6 1.4 %collective-permute-start.9 = (f32[56,512]{1,0:T(8,128)S(1)}, f32[56,512]{1,0:T(8,128)S(1)}, u32[]{:S(2)}, u32[]{:S(2)}) collective-permute-start(f32[56,512]{1,0:T(8,128)S(1)} %merge_with_demand.1.own_ref.rest_4_), channel_id=1, source_target_pairs={{0,6},{2,4},{4,2},{6,0},{1,7},{3,5},{5,3},{7,1},{8,14},{10,12},{12... | collective-permute-start | bytes 344072 | tf_op jit(solution)/shard_map/ppermute | solution.py:351
  34.1 2.4 %collective-permute-done.10.three_ref.rest_7_ = f32[56,512]{1,0:T(8,128)S(1)} collective-permute-done((f32[56,512]{1,0:T(8,128)S(1)}, f32[56,512]{1,0:T(8,128)S(1)}, u32[]{:S(2)}, u32[]{:S(2)}) %collective-permute-start.10) | collective-permute-done | bytes 114720 | tf_op jit(solution)/shard_map/ppermute | solution.py:351
  36.5 2.3 %collective-permute-done.9.two_ref.rest_6_ = f32[56,512]{1,0:T(8,128)S(1)} collective-permute-done((f32[56,512]{1,0:T(8,128)S(1)}, f32[56,512]{1,0:T(8,128)S(1)}, u32[]{:S(2)}, u32[]{:S(2)}) %collective-permute-start.9) | collective-permute-done | bytes 114720 | tf_op jit(solution)/shard_map/ppermute | solution.py:351
  38.7 0.5 collective-permute-done.8.one_ref.rest_5_
  39.2 0.4 markov_wide.1
  39.6 1.8 %collective-permute-start.11 = (f32[80,512]{1,0:T(8,128)S(1)}, f32[80,512]{1,0:T(8,128)S(1)}, u32[]{:S(2)}, u32[]{:S(2)}) collective-permute-start(f32[80,512]{1,0:T(8,128)S(1)} %get-tuple-element.36), channel_id=1, source_target_pairs={{0,1},{1,0},{2,3},{3,2},{4,5},{5,4},{6,7},{7,6},{8,9},{9,8},{10,11... | collective-permute-start | bytes 491528 | tf_op jit(solution)/shard_map/ppermute | solution.py:354
  41.4 1.0 %collective-permute-done.11.got_ref = f32[80,512]{1,0:T(8,128)S(1)} collective-permute-done((f32[80,512]{1,0:T(8,128)S(1)}, f32[80,512]{1,0:T(8,128)S(1)}, u32[]{:S(2)}, u32[]{:S(2)}) %collective-permute-start.11) | collective-permute-done | bytes 163872 | tf_op jit(solution)/shard_map/ppermute | solution.py:354
  42.4 0.9 %close.1 = (f32[1,16,512]{2,1,0:T(8,128)}, f32[1,16,512]{2,1,0:T(8,128)}, f32[64,1,128]{2,1,0:T(1,128)S(1)}) custom-call(f32[80,512]{1,0:T(8,128)S(1)} %get-tuple-element.35.keep_ref, f32[80,512]{1,0:T(8,128)S(1)} %collective-permute-done.11.got_ref, f32[64,512]{1,0:T(8,128)S(1)} %merge_with_fixed.1.own_ref.rest_0_, ...), custom_call_target="tpu_custom_call" | custom-call | tf_op jit(solution)/shard_map/close/pallas_call | solution.py:442
  43.4 19.3 %all_to_all.5.terms_ref = f32[64,1,128]{2,1,0:T(1,128)S(1)} all-to-all(f32[64,1,128]{2,1,0:T(1,128)S(1)} %get-tuple-element.40), channel_id=1, replica_groups=mesh['dur'=32,'x'=4,'core'=2] {'dur','core'}, dimensions={0} | all-to-all | bytes 65536 | tf_op jit(solution)/shard_map/all_to_all | solution.py:454
  62.7 0.6 demand.1
  (25 shorter events, 0.1 us)
Async XLA Ops:
  0.6 7.6 %copy-start.8 = (f32[1,16,512]{2,1,0:T(8,128)S(1)}, f32[1,16,512]{2,1,0:T(8,128)}, u32[]{:S(2)}) copy-start(f32[1,16,512]{2,1,0:T(8,128)} %mass_ref.3) | copy-start | bytes 98308
  0.6 7.6 %copy-start = (f32[1,16,512]{2,1,0:T(8,128)S(1)}, f32[1,16,512]{2,1,0:T(8,128)}, u32[]{:S(2)}) copy-start(f32[1,16,512]{2,1,0:T(8,128)} %rest_8_.1) | copy-start | bytes 98308
  0.7 7.6 %copy-start.5 = (s32[2,1,16,512]{3,2,1,0:T(8,128)S(1)}, s32[2,1,16,512]{3,2,1,0:T(8,128)}, u32[]{:S(2)}) copy-start(s32[2,1,16,512]{3,2,1,0:T(8,128)} %bracket_ref.5) | copy-start | bytes 196612
  2.1 6.1 %collective-permute-start = (f32[32,512]{1,0:T(8,128)S(1)}, f32[32,512]{1,0:T(8,128)S(1)}, u32[]{:S(2)}, u32[]{:S(2)}) collective-permute-start(f32[32,512]{1,0:T(8,128)S(1)} %get-tuple-element.23), channel_id=1, source_target_pairs={{8,16},{16,8},{24,32},{32,24},{40,48},{48,40},{56,64},{64,56},{72,... | collective-permute-start | bytes 196616 | tf_op jit(solution)/shard_map/ppermute | solution.py:357
  2.8 7.1 %copy-start.7 = (f32[1,16,512]{2,1,0:T(8,128)S(1)}, f32[1,16,512]{2,1,0:T(8,128)}, u32[]{:S(2)}) copy-start(f32[1,16,512]{2,1,0:T(8,128)} %value_ref.3) | copy-start | bytes 98308
  2.8 7.1 %collective-permute-start.1 = (f32[32,512]{1,0:T(8,128)S(1)}, f32[32,512]{1,0:T(8,128)S(1)}, u32[]{:S(2)}, u32[]{:S(2)}) collective-permute-start(f32[32,512]{1,0:T(8,128)S(1)} %get-tuple-element.24), channel_id=1, source_target_pairs={{0,8},{8,0},{16,24},{24,16},{32,40},{40,32},{48,56},{56,48},{64,72... | collective-permute-start | bytes 196616 | tf_op jit(solution)/shard_map/ppermute | solution.py:358
  9.9 3.7 %copy-start.9 = (f32[128,128]{1,0:T(8,128)S(1)}, f32[128,128]{1,0:T(8,128)}, u32[]{:S(2)}) copy-start(f32[128,128]{1,0:T(8,128)} %markov_ref.1) | copy-start | bytes 196612
  9.9 3.7 %copy-start.10 = (f32[2]{0:T(128)S(1)}, f32[2]{0:T(128)}, u32[]{:S(2)}) copy-start(f32[2]{0:T(128)} %tax_ref.1) | copy-start | bytes 28
  9.9 5.4 %collective-permute-start.4 = (f32[64,512]{1,0:T(8,128)S(1)}, f32[64,512]{1,0:T(8,128)S(1)}, u32[]{:S(2)}, u32[]{:S(2)}) collective-permute-start(f32[64,512]{1,0:T(8,128)S(1)} %merge_with_fixed.1.own_ref.rest_0_), channel_id=1, source_target_pairs={{0,4},{2,6},{4,0},{6,2},{1,5},{3,7},{5,1},{7,3},{8,12},{10,14},{12... | collective-permute-start | bytes 393224 | tf_op jit(solution)/shard_map/ppermute | solution.py:351
  12.8 6.6 %collective-permute-start.3 = (f32[64,512]{1,0:T(8,128)S(1)}, f32[64,512]{1,0:T(8,128)S(1)}, u32[]{:S(2)}, u32[]{:S(2)}) collective-permute-start(f32[64,512]{1,0:T(8,128)S(1)} %merge_with_fixed.1.own_ref.rest_0_), channel_id=1, source_target_pairs={{0,6},{2,4},{4,2},{6,0},{1,7},{3,5},{5,3},{7,1},{8,14},{10,12},{12... | collective-permute-start | bytes 393224 | tf_op jit(solution)/shard_map/ppermute | solution.py:351
  13.6 5.7 %collective-permute-start.2 = (f32[64,512]{1,0:T(8,128)S(1)}, f32[64,512]{1,0:T(8,128)S(1)}, u32[]{:S(2)}, u32[]{:S(2)}) collective-permute-start(f32[64,512]{1,0:T(8,128)S(1)} %merge_with_fixed.1.own_ref.rest_0_), channel_id=1, source_target_pairs={{0,2},{2,0},{4,6},{6,4},{1,3},{3,1},{5,7},{7,5},{8,10},{10,8},{12,... | collective-permute-start | bytes 393224 | tf_op jit(solution)/shard_map/ppermute | solution.py:351
  19.4 3.1 %copy-start.1 = (s32[2,1,16,512]{3,2,1,0:T(8,128)S(1)}, s32[2,1,16,512]{3,2,1,0:T(8,128)}, u32[]{:S(2)}) copy-start(s32[2,1,16,512]{3,2,1,0:T(8,128)} %fwd_bracket_ref.1) | copy-start | bytes 196612
  19.4 3.1 %copy-start.2 = (f32[2,1,16,512]{3,2,1,0:T(8,128)S(1)}, f32[2,1,16,512]{3,2,1,0:T(8,128)}, u32[]{:S(2)}) copy-start(f32[2,1,16,512]{3,2,1,0:T(8,128)} %fwd_weight_ref.1) | copy-start | bytes 196612
  19.4 3.1 %copy-start.3 = (s32[2,1,16,512]{3,2,1,0:T(8,128)S(1)}, s32[2,1,16,512]{3,2,1,0:T(8,128)}, u32[]{:S(2)}) copy-start(s32[2,1,16,512]{3,2,1,0:T(8,128)} %step_ref.3) | copy-start | bytes 196612
  19.4 3.1 %copy-start.4 = (f32[2,1,16,512]{3,2,1,0:T(8,128)S(1)}, f32[2,1,16,512]{3,2,1,0:T(8,128)}, u32[]{:S(2)}) copy-start(f32[2,1,16,512]{3,2,1,0:T(8,128)} %omega_ref.3) | copy-start | bytes 196612
  19.4 3.1 %copy-start.6 = (f32[2,1,16,512]{3,2,1,0:T(8,128)S(1)}, f32[2,1,16,512]{3,2,1,0:T(8,128)}, u32[]{:S(2)}) copy-start(f32[2,1,16,512]{3,2,1,0:T(8,128)} %rest_1_.1) | copy-start | bytes 196612
  19.7 2.8 %collective-permute-start.5 = (f32[32,512]{1,0:T(8,128)S(1)}, f32[32,512]{1,0:T(8,128)S(1)}, u32[]{:S(2)}, u32[]{:S(2)}) collective-permute-start(f32[32,512]{1,0:T(8,128)S(1)} %get-tuple-element.28), channel_id=1, source_target_pairs={{0,1},{1,0},{2,3},{3,2},{4,5},{5,4},{6,7},{7,6},{8,9},{9,8},{10,11... | collective-permute-start | bytes 196616 | tf_op jit(solution)/shard_map/ppermute | solution.py:354
  23.0 6.5 %collective-permute-start.6 = (f32[32,512]{1,0:T(8,128)S(1)}, f32[32,512]{1,0:T(8,128)S(1)}, u32[]{:S(2)}, u32[]{:S(2)}) collective-permute-start(f32[32,512]{1,0:T(8,128)S(1)} %get-tuple-element.32), channel_id=1, source_target_pairs={{8,16},{16,8},{24,32},{32,24},{40,48},{48,40},{56,64},{64,56},{72,... | collective-permute-start | bytes 196616 | tf_op jit(solution)/shard_map/ppermute | solution.py:357
  23.7 7.5 %collective-permute-start.7 = (f32[32,512]{1,0:T(8,128)S(1)}, f32[32,512]{1,0:T(8,128)S(1)}, u32[]{:S(2)}, u32[]{:S(2)}) collective-permute-start(f32[32,512]{1,0:T(8,128)S(1)} %get-tuple-element.33), channel_id=1, source_target_pairs={{0,8},{8,0},{16,24},{24,16},{32,40},{40,32},{48,56},{56,48},{64,72... | collective-permute-start | bytes 196616 | tf_op jit(solution)/shard_map/ppermute | solution.py:358
  31.2 5.3 %collective-permute-start.10 = (f32[56,512]{1,0:T(8,128)S(1)}, f32[56,512]{1,0:T(8,128)S(1)}, u32[]{:S(2)}, u32[]{:S(2)}) collective-permute-start(f32[56,512]{1,0:T(8,128)S(1)} %merge_with_demand.1.own_ref.rest_4_), channel_id=1, source_target_pairs={{0,4},{2,6},{4,0},{6,2},{1,5},{3,7},{5,1},{7,3},{8,12},{10,14},{12... | collective-permute-start | bytes 344072 | tf_op jit(solution)/shard_map/ppermute | solution.py:351
  32.6 6.1 %collective-permute-start.9 = (f32[56,512]{1,0:T(8,128)S(1)}, f32[56,512]{1,0:T(8,128)S(1)}, u32[]{:S(2)}, u32[]{:S(2)}) collective-permute-start(f32[56,512]{1,0:T(8,128)S(1)} %merge_with_demand.1.own_ref.rest_4_), channel_id=1, source_target_pairs={{0,6},{2,4},{4,2},{6,0},{1,7},{3,5},{5,3},{7,1},{8,14},{10,12},{12... | collective-permute-start | bytes 344072 | tf_op jit(solution)/shard_map/ppermute | solution.py:351
  34.1 5.1 %collective-permute-start.8 = (f32[56,512]{1,0:T(8,128)S(1)}, f32[56,512]{1,0:T(8,128)S(1)}, u32[]{:S(2)}, u32[]{:S(2)}) collective-permute-start(f32[56,512]{1,0:T(8,128)S(1)} %merge_with_demand.1.own_ref.rest_4_), channel_id=1, source_target_pairs={{0,2},{2,0},{4,6},{6,4},{1,3},{3,1},{5,7},{7,5},{8,10},{10,8},{12,... | collective-permute-start | bytes 344072 | tf_op jit(solution)/shard_map/ppermute | solution.py:351
  39.6 2.9 %collective-permute-start.11 = (f32[80,512]{1,0:T(8,128)S(1)}, f32[80,512]{1,0:T(8,128)S(1)}, u32[]{:S(2)}, u32[]{:S(2)}) collective-permute-start(f32[80,512]{1,0:T(8,128)S(1)} %get-tuple-element.36), channel_id=1, source_target_pairs={{0,1},{1,0},{2,3},{3,2},{4,5},{5,4},{6,7},{7,6},{8,9},{9,8},{10,11... | collective-permute-start | bytes 491528 | tf_op jit(solution)/shard_map/ppermute | solution.py:354

commit v8 on v7

--- a/solution.py
+++ b/solution.py
@@ -201,7 +201,8 @@
 
 def place_field(refs, part, rows, field_ref):
     chip, core = lax.axis_index("x"), lax.axis_index("core")
-    field_ref[...] = jnp.zeros_like(field_ref)
+    if part == 0:
+        field_ref[...] = jnp.zeros_like(field_ref)
     for shift, ref in zip(SHIFTS, refs):
         at = pl.ds(pl.multiple_of((chip ^ shift) * 2 * rows + core * rows, rows), rows)
         field_ref[at, :] = ref[part * rows : (part + 1) * rows, :]

time: 63.5 us -> 63.4 us (level)
  no operation moved by 1% of the time
where the time goes in v8:
time: 63.4 us; the launch traced here: 63.2 us
  starting transfers between devices  22.9 us (36%)
  blocking collectives  19.3 us (30%)
  waiting for transfers between devices  15.9 us (25%)
  Pallas kernels  4.29 us (7%)
  between operations  0.79 us (1%)
    all_to_all x1, blocking collectives, per_device(): every_term = lax.all_to_all(terms, ('dur', 'core'), 0, 0)  19.3 us
    ppermute x2, starting transfers between devices, over_levels(): return (other_in, lax.ppermute(pair_out, 'dur', pairs))  11.3 us
    ppermute x6, waiting for transfers between devices, over_chips(): lax.ppermute(array, 'x', [(i, i ^ k) for i in range(chips)])  10.7 us
    ppermute x6, starting transfers between devices, over_chips(): lax.ppermute(array, 'x', [(i, i ^ k) for i in range(chips)])  6.57 us
    ppermute x2, starting transfers between devices, over_cores(): return lax.ppermute(array, 'core', [(i, i ^ 1) for i in range(cores)])  3.7 us
    ppermute x2, waiting for transfers between devices, over_levels(): return (other_in, lax.ppermute(pair_out, 'dur', pairs))  3.28 us
    ppermute x2, waiting for transfers between devices, over_cores(): return lax.ppermute(array, 'core', [(i, i ^ 1) for i in range(cores)])  1.93 us
    pallas_call x1, Pallas kernels, per_device(): pl.pallas_call(open_kernel, out_shape=(pair, pair, slab), in_specs=[pl.Bl...  1.46 us
  transfers between devices with their start and end apart: 12, of which 9 were waited for; matrix products, arithmetic and copies ran while one was open for 0% of the time, Pallas kernels for 0%

profile of v8, /device:TPU:1, one launch (start us, length us, event | category | flops | bytes accessed | tf_op | source)
XLA Modules:
  0.0 63.2 jit_solution(1944316855109271684)
XLA Ops:
  0.7 1.5 %open.1 = (f32[32,512]{1,0:T(8,128)S(1)}, f32[32,512]{1,0:T(8,128)S(1)}, f32[16,512]{1,0:T(8,128)S(1)}) custom-call(f32[1,16,512]{2,1,0:T(8,128)} %mass_ref.3, s32[2,1,16,512]{3,2,1,0:T(8,128)} %fwd_bracket_ref.1, f32[2,1,16,512]{3,2,1,0:T(8,128)} %fwd_weight_ref.1, s32[2,1,16,512]{3,2,1,0:T(8,128)} %step_ref.3, f32[2,1,16,512]{3,2,1,0:T(8,128)} %omega_ref.3, ...), custom_call_target="tpu_custom_call" | custom-call | tf_op jit(solution)/shard_map/open/pallas_call | solution.py:380
  2.1 0.7 %collective-permute-start = (f32[32,512]{1,0:T(8,128)S(1)}, f32[32,512]{1,0:T(8,128)S(1)}, u32[]{:S(2)}, u32[]{:S(2)}) collective-permute-start(f32[32,512]{1,0:T(8,128)S(1)} %get-tuple-element.23), channel_id=1, source_target_pairs={{8,16},{16,8},{24,32},{32,24},{40,48},{48,40},{56,64},{64,56},{72,... | collective-permute-start | bytes 196616 | tf_op jit(solution)/shard_map/ppermute | solution.py:358
  2.8 0.0 copy-start.7
  2.8 5.4 %collective-permute-start.1 = (f32[32,512]{1,0:T(8,128)S(1)}, f32[32,512]{1,0:T(8,128)S(1)}, u32[]{:S(2)}, u32[]{:S(2)}) collective-permute-start(f32[32,512]{1,0:T(8,128)S(1)} %get-tuple-element.24), channel_id=1, source_target_pairs={{0,8},{8,0},{16,24},{24,16},{32,40},{40,32},{48,56},{56,48},{64,72... | collective-permute-start | bytes 196616 | tf_op jit(solution)/shard_map/ppermute | solution.py:359
  8.3 0.0 collective-permute-done.other_ref
  8.3 1.6 %collective-permute-done.1.pair_ref = f32[32,512]{1,0:T(8,128)S(1)} collective-permute-done((f32[32,512]{1,0:T(8,128)S(1)}, f32[32,512]{1,0:T(8,128)S(1)}, u32[]{:S(2)}, u32[]{:S(2)}) %collective-permute-start.1) | collective-permute-done | bytes 65568 | tf_op jit(solution)/shard_map/ppermute | solution.py:359
  9.9 2.8 %collective-permute-start.4 = (f32[64,512]{1,0:T(8,128)S(1)}, f32[64,512]{1,0:T(8,128)S(1)}, u32[]{:S(2)}, u32[]{:S(2)}) collective-permute-start(f32[64,512]{1,0:T(8,128)S(1)} %merge_with_fixed.1.own_ref.rest_0_), channel_id=1, source_target_pairs={{0,4},{2,6},{4,0},{6,2},{1,5},{3,7},{5,1},{7,3},{8,12},{10,14},{12... | collective-permute-start | bytes 393224 | tf_op jit(solution)/shard_map/ppermute | solution.py:352
  12.8 0.9 %collective-permute-start.3 = (f32[64,512]{1,0:T(8,128)S(1)}, f32[64,512]{1,0:T(8,128)S(1)}, u32[]{:S(2)}, u32[]{:S(2)}) collective-permute-start(f32[64,512]{1,0:T(8,128)S(1)} %merge_with_fixed.1.own_ref.rest_0_), channel_id=1, source_target_pairs={{0,6},{2,4},{4,2},{6,0},{1,7},{3,5},{5,3},{7,1},{8,14},{10,12},{12... | collective-permute-start | bytes 393224 | tf_op jit(solution)/shard_map/ppermute | solution.py:352
  13.6 0.0 collective-permute-start.2
  13.6 0.1 weights.1
  13.8 1.6 %collective-permute-done.4.three_ref.rest_3_ = f32[64,512]{1,0:T(8,128)S(1)} collective-permute-done((f32[64,512]{1,0:T(8,128)S(1)}, f32[64,512]{1,0:T(8,128)S(1)}, u32[]{:S(2)}, u32[]{:S(2)}) %collective-permute-start.4) | collective-permute-done | bytes 131104 | tf_op jit(solution)/shard_map/ppermute | solution.py:352
  15.4 4.0 %collective-permute-done.3.two_ref.rest_2_ = f32[64,512]{1,0:T(8,128)S(1)} collective-permute-done((f32[64,512]{1,0:T(8,128)S(1)}, f32[64,512]{1,0:T(8,128)S(1)}, u32[]{:S(2)}, u32[]{:S(2)}) %collective-permute-start.3) | collective-permute-done | bytes 131104 | tf_op jit(solution)/shard_map/ppermute | solution.py:352
  19.4 0.0 copy-start.4
  19.4 0.0 copy-start.6
  19.4 0.3 markov.1
  19.6 1.9 %collective-permute-start.5 = (f32[32,512]{1,0:T(8,128)S(1)}, f32[32,512]{1,0:T(8,128)S(1)}, u32[]{:S(2)}, u32[]{:S(2)}) collective-permute-start(f32[32,512]{1,0:T(8,128)S(1)} %get-tuple-element.28), channel_id=1, source_target_pairs={{0,1},{1,0},{2,3},{3,2},{4,5},{5,4},{6,7},{7,6},{8,9},{9,8},{10,11... | collective-permute-start | bytes 196616 | tf_op jit(solution)/shard_map/ppermute | solution.py:355
  21.5 0.9 %collective-permute-done.5.got_ref = f32[32,512]{1,0:T(8,128)S(1)} collective-permute-done((f32[32,512]{1,0:T(8,128)S(1)}, f32[32,512]{1,0:T(8,128)S(1)}, u32[]{:S(2)}, u32[]{:S(2)}) %collective-permute-start.5) | collective-permute-done | bytes 65568 | tf_op jit(solution)/shard_map/ppermute | solution.py:355
  22.4 0.6 turn.1
  23.0 0.7 %collective-permute-start.6 = (f32[32,512]{1,0:T(8,128)S(1)}, f32[32,512]{1,0:T(8,128)S(1)}, u32[]{:S(2)}, u32[]{:S(2)}) collective-permute-start(f32[32,512]{1,0:T(8,128)S(1)} %get-tuple-element.32), channel_id=1, source_target_pairs={{8,16},{16,8},{24,32},{32,24},{40,48},{48,40},{56,64},{64,56},{72,... | collective-permute-start | bytes 196616 | tf_op jit(solution)/shard_map/ppermute | solution.py:358
  23.7 5.8 %collective-permute-start.7 = (f32[32,512]{1,0:T(8,128)S(1)}, f32[32,512]{1,0:T(8,128)S(1)}, u32[]{:S(2)}, u32[]{:S(2)}) collective-permute-start(f32[32,512]{1,0:T(8,128)S(1)} %get-tuple-element.33), channel_id=1, source_target_pairs={{0,8},{8,0},{16,24},{24,16},{32,40},{40,32},{48,56},{56,48},{64,72... | collective-permute-start | bytes 196616 | tf_op jit(solution)/shard_map/ppermute | solution.py:359
  29.5 1.7 %collective-permute-done.7.pair_ref = f32[32,512]{1,0:T(8,128)S(1)} collective-permute-done((f32[32,512]{1,0:T(8,128)S(1)}, f32[32,512]{1,0:T(8,128)S(1)}, u32[]{:S(2)}, u32[]{:S(2)}) %collective-permute-start.7) | collective-permute-done | bytes 65568 | tf_op jit(solution)/shard_map/ppermute | solution.py:359
  31.2 1.4 %collective-permute-start.10 = (f32[56,512]{1,0:T(8,128)S(1)}, f32[56,512]{1,0:T(8,128)S(1)}, u32[]{:S(2)}, u32[]{:S(2)}) collective-permute-start(f32[56,512]{1,0:T(8,128)S(1)} %merge_with_demand.1.own_ref.rest_4_), channel_id=1, source_target_pairs={{0,4},{2,6},{4,0},{6,2},{1,5},{3,7},{5,1},{7,3},{8,12},{10,14},{12... | collective-permute-start | bytes 344072 | tf_op jit(solution)/shard_map/ppermute | solution.py:352
  32.6 1.4 %collective-permute-start.9 = (f32[56,512]{1,0:T(8,128)S(1)}, f32[56,512]{1,0:T(8,128)S(1)}, u32[]{:S(2)}, u32[]{:S(2)}) collective-permute-start(f32[56,512]{1,0:T(8,128)S(1)} %merge_with_demand.1.own_ref.rest_4_), channel_id=1, source_target_pairs={{0,6},{2,4},{4,2},{6,0},{1,7},{3,5},{5,3},{7,1},{8,14},{10,12},{12... | collective-permute-start | bytes 344072 | tf_op jit(solution)/shard_map/ppermute | solution.py:352
  34.1 2.4 %collective-permute-done.10.three_ref.rest_7_ = f32[56,512]{1,0:T(8,128)S(1)} collective-permute-done((f32[56,512]{1,0:T(8,128)S(1)}, f32[56,512]{1,0:T(8,128)S(1)}, u32[]{:S(2)}, u32[]{:S(2)}) %collective-permute-start.10) | collective-permute-done | bytes 114720 | tf_op jit(solution)/shard_map/ppermute | solution.py:352
  36.5 2.3 %collective-permute-done.9.two_ref.rest_6_ = f32[56,512]{1,0:T(8,128)S(1)} collective-permute-done((f32[56,512]{1,0:T(8,128)S(1)}, f32[56,512]{1,0:T(8,128)S(1)}, u32[]{:S(2)}, u32[]{:S(2)}) %collective-permute-start.9) | collective-permute-done | bytes 114720 | tf_op jit(solution)/shard_map/ppermute | solution.py:352
  38.7 0.5 collective-permute-done.8.one_ref.rest_5_
  39.2 0.4 markov_wide.1
  39.6 1.8 %collective-permute-start.11 = (f32[80,512]{1,0:T(8,128)S(1)}, f32[80,512]{1,0:T(8,128)S(1)}, u32[]{:S(2)}, u32[]{:S(2)}) collective-permute-start(f32[80,512]{1,0:T(8,128)S(1)} %get-tuple-element.36), channel_id=1, source_target_pairs={{0,1},{1,0},{2,3},{3,2},{4,5},{5,4},{6,7},{7,6},{8,9},{9,8},{10,11... | collective-permute-start | bytes 491528 | tf_op jit(solution)/shard_map/ppermute | solution.py:355
  41.4 1.0 %collective-permute-done.11.got_ref = f32[80,512]{1,0:T(8,128)S(1)} collective-permute-done((f32[80,512]{1,0:T(8,128)S(1)}, f32[80,512]{1,0:T(8,128)S(1)}, u32[]{:S(2)}, u32[]{:S(2)}) %collective-permute-start.11) | collective-permute-done | bytes 163872 | tf_op jit(solution)/shard_map/ppermute | solution.py:355
  42.4 0.9 %close.1 = (f32[1,16,512]{2,1,0:T(8,128)}, f32[1,16,512]{2,1,0:T(8,128)}, f32[64,1,128]{2,1,0:T(1,128)S(1)}) custom-call(f32[80,512]{1,0:T(8,128)S(1)} %get-tuple-element.35.keep_ref, f32[80,512]{1,0:T(8,128)S(1)} %collective-permute-done.11.got_ref, f32[64,512]{1,0:T(8,128)S(1)} %merge_with_fixed.1.own_ref.rest_0_, ...), custom_call_target="tpu_custom_call" | custom-call | tf_op jit(solution)/shard_map/close/pallas_call | solution.py:443
  43.3 19.3 %all_to_all.5.terms_ref = f32[64,1,128]{2,1,0:T(1,128)S(1)} all-to-all(f32[64,1,128]{2,1,0:T(1,128)S(1)} %get-tuple-element.40), channel_id=1, replica_groups=mesh['dur'=32,'x'=4,'core'=2] {'dur','core'}, dimensions={0} | all-to-all | bytes 65536 | tf_op jit(solution)/shard_map/all_to_all | solution.py:455
  62.7 0.6 demand.1
  (25 shorter events, 0.1 us)
Async XLA Ops:
  0.6 7.6 %copy-start.8 = (f32[1,16,512]{2,1,0:T(8,128)S(1)}, f32[1,16,512]{2,1,0:T(8,128)}, u32[]{:S(2)}) copy-start(f32[1,16,512]{2,1,0:T(8,128)} %mass_ref.3) | copy-start | bytes 98308
  0.6 7.6 %copy-start = (f32[1,16,512]{2,1,0:T(8,128)S(1)}, f32[1,16,512]{2,1,0:T(8,128)}, u32[]{:S(2)}) copy-start(f32[1,16,512]{2,1,0:T(8,128)} %rest_8_.1) | copy-start | bytes 98308
  0.7 7.6 %copy-start.5 = (s32[2,1,16,512]{3,2,1,0:T(8,128)S(1)}, s32[2,1,16,512]{3,2,1,0:T(8,128)}, u32[]{:S(2)}) copy-start(s32[2,1,16,512]{3,2,1,0:T(8,128)} %bracket_ref.5) | copy-start | bytes 196612
  2.1 6.1 %collective-permute-start = (f32[32,512]{1,0:T(8,128)S(1)}, f32[32,512]{1,0:T(8,128)S(1)}, u32[]{:S(2)}, u32[]{:S(2)}) collective-permute-start(f32[32,512]{1,0:T(8,128)S(1)} %get-tuple-element.23), channel_id=1, source_target_pairs={{8,16},{16,8},{24,32},{32,24},{40,48},{48,40},{56,64},{64,56},{72,... | collective-permute-start | bytes 196616 | tf_op jit(solution)/shard_map/ppermute | solution.py:358
  2.8 7.1 %copy-start.7 = (f32[1,16,512]{2,1,0:T(8,128)S(1)}, f32[1,16,512]{2,1,0:T(8,128)}, u32[]{:S(2)}) copy-start(f32[1,16,512]{2,1,0:T(8,128)} %value_ref.3) | copy-start | bytes 98308
  2.8 7.1 %collective-permute-start.1 = (f32[32,512]{1,0:T(8,128)S(1)}, f32[32,512]{1,0:T(8,128)S(1)}, u32[]{:S(2)}, u32[]{:S(2)}) collective-permute-start(f32[32,512]{1,0:T(8,128)S(1)} %get-tuple-element.24), channel_id=1, source_target_pairs={{0,8},{8,0},{16,24},{24,16},{32,40},{40,32},{48,56},{56,48},{64,72... | collective-permute-start | bytes 196616 | tf_op jit(solution)/shard_map/ppermute | solution.py:359
  9.9 3.7 %copy-start.9 = (f32[128,128]{1,0:T(8,128)S(1)}, f32[128,128]{1,0:T(8,128)}, u32[]{:S(2)}) copy-start(f32[128,128]{1,0:T(8,128)} %markov_ref.1) | copy-start | bytes 196612
  9.9 3.7 %copy-start.10 = (f32[2]{0:T(128)S(1)}, f32[2]{0:T(128)}, u32[]{:S(2)}) copy-start(f32[2]{0:T(128)} %tax_ref.1) | copy-start | bytes 28
  9.9 5.4 %collective-permute-start.4 = (f32[64,512]{1,0:T(8,128)S(1)}, f32[64,512]{1,0:T(8,128)S(1)}, u32[]{:S(2)}, u32[]{:S(2)}) collective-permute-start(f32[64,512]{1,0:T(8,128)S(1)} %merge_with_fixed.1.own_ref.rest_0_), channel_id=1, source_target_pairs={{0,4},{2,6},{4,0},{6,2},{1,5},{3,7},{5,1},{7,3},{8,12},{10,14},{12... | collective-permute-start | bytes 393224 | tf_op jit(solution)/shard_map/ppermute | solution.py:352
  12.8 6.6 %collective-permute-start.3 = (f32[64,512]{1,0:T(8,128)S(1)}, f32[64,512]{1,0:T(8,128)S(1)}, u32[]{:S(2)}, u32[]{:S(2)}) collective-permute-start(f32[64,512]{1,0:T(8,128)S(1)} %merge_with_fixed.1.own_ref.rest_0_), channel_id=1, source_target_pairs={{0,6},{2,4},{4,2},{6,0},{1,7},{3,5},{5,3},{7,1},{8,14},{10,12},{12... | collective-permute-start | bytes 393224 | tf_op jit(solution)/shard_map/ppermute | solution.py:352
  13.6 5.7 %collective-permute-start.2 = (f32[64,512]{1,0:T(8,128)S(1)}, f32[64,512]{1,0:T(8,128)S(1)}, u32[]{:S(2)}, u32[]{:S(2)}) collective-permute-start(f32[64,512]{1,0:T(8,128)S(1)} %merge_with_fixed.1.own_ref.rest_0_), channel_id=1, source_target_pairs={{0,2},{2,0},{4,6},{6,4},{1,3},{3,1},{5,7},{7,5},{8,10},{10,8},{12,... | collective-permute-start | bytes 393224 | tf_op jit(solution)/shard_map/ppermute | solution.py:352
  19.4 3.1 %copy-start.1 = (s32[2,1,16,512]{3,2,1,0:T(8,128)S(1)}, s32[2,1,16,512]{3,2,1,0:T(8,128)}, u32[]{:S(2)}) copy-start(s32[2,1,16,512]{3,2,1,0:T(8,128)} %fwd_bracket_ref.1) | copy-start | bytes 196612
  19.4 3.1 %copy-start.2 = (f32[2,1,16,512]{3,2,1,0:T(8,128)S(1)}, f32[2,1,16,512]{3,2,1,0:T(8,128)}, u32[]{:S(2)}) copy-start(f32[2,1,16,512]{3,2,1,0:T(8,128)} %fwd_weight_ref.1) | copy-start | bytes 196612
  19.4 3.1 %copy-start.3 = (s32[2,1,16,512]{3,2,1,0:T(8,128)S(1)}, s32[2,1,16,512]{3,2,1,0:T(8,128)}, u32[]{:S(2)}) copy-start(s32[2,1,16,512]{3,2,1,0:T(8,128)} %step_ref.3) | copy-start | bytes 196612
  19.4 3.1 %copy-start.4 = (f32[2,1,16,512]{3,2,1,0:T(8,128)S(1)}, f32[2,1,16,512]{3,2,1,0:T(8,128)}, u32[]{:S(2)}) copy-start(f32[2,1,16,512]{3,2,1,0:T(8,128)} %omega_ref.3) | copy-start | bytes 196612
  19.4 3.1 %copy-start.6 = (f32[2,1,16,512]{3,2,1,0:T(8,128)S(1)}, f32[2,1,16,512]{3,2,1,0:T(8,128)}, u32[]{:S(2)}) copy-start(f32[2,1,16,512]{3,2,1,0:T(8,128)} %rest_1_.1) | copy-start | bytes 196612
  19.6 2.8 %collective-permute-start.5 = (f32[32,512]{1,0:T(8,128)S(1)}, f32[32,512]{1,0:T(8,128)S(1)}, u32[]{:S(2)}, u32[]{:S(2)}) collective-permute-start(f32[32,512]{1,0:T(8,128)S(1)} %get-tuple-element.28), channel_id=1, source_target_pairs={{0,1},{1,0},{2,3},{3,2},{4,5},{5,4},{6,7},{7,6},{8,9},{9,8},{10,11... | collective-permute-start | bytes 196616 | tf_op jit(solution)/shard_map/ppermute | solution.py:355
  23.0 6.5 %collective-permute-start.6 = (f32[32,512]{1,0:T(8,128)S(1)}, f32[32,512]{1,0:T(8,128)S(1)}, u32[]{:S(2)}, u32[]{:S(2)}) collective-permute-start(f32[32,512]{1,0:T(8,128)S(1)} %get-tuple-element.32), channel_id=1, source_target_pairs={{8,16},{16,8},{24,32},{32,24},{40,48},{48,40},{56,64},{64,56},{72,... | collective-permute-start | bytes 196616 | tf_op jit(solution)/shard_map/ppermute | solution.py:358
  23.7 7.5 %collective-permute-start.7 = (f32[32,512]{1,0:T(8,128)S(1)}, f32[32,512]{1,0:T(8,128)S(1)}, u32[]{:S(2)}, u32[]{:S(2)}) collective-permute-start(f32[32,512]{1,0:T(8,128)S(1)} %get-tuple-element.33), channel_id=1, source_target_pairs={{0,8},{8,0},{16,24},{24,16},{32,40},{40,32},{48,56},{56,48},{64,72... | collective-permute-start | bytes 196616 | tf_op jit(solution)/shard_map/ppermute | solution.py:359
  31.2 5.3 %collective-permute-start.10 = (f32[56,512]{1,0:T(8,128)S(1)}, f32[56,512]{1,0:T(8,128)S(1)}, u32[]{:S(2)}, u32[]{:S(2)}) collective-permute-start(f32[56,512]{1,0:T(8,128)S(1)} %merge_with_demand.1.own_ref.rest_4_), channel_id=1, source_target_pairs={{0,4},{2,6},{4,0},{6,2},{1,5},{3,7},{5,1},{7,3},{8,12},{10,14},{12... | collective-permute-start | bytes 344072 | tf_op jit(solution)/shard_map/ppermute | solution.py:352
  32.6 6.1 %collective-permute-start.9 = (f32[56,512]{1,0:T(8,128)S(1)}, f32[56,512]{1,0:T(8,128)S(1)}, u32[]{:S(2)}, u32[]{:S(2)}) collective-permute-start(f32[56,512]{1,0:T(8,128)S(1)} %merge_with_demand.1.own_ref.rest_4_), channel_id=1, source_target_pairs={{0,6},{2,4},{4,2},{6,0},{1,7},{3,5},{5,3},{7,1},{8,14},{10,12},{12... | collective-permute-start | bytes 344072 | tf_op jit(solution)/shard_map/ppermute | solution.py:352
  34.1 5.1 %collective-permute-start.8 = (f32[56,512]{1,0:T(8,128)S(1)}, f32[56,512]{1,0:T(8,128)S(1)}, u32[]{:S(2)}, u32[]{:S(2)}) collective-permute-start(f32[56,512]{1,0:T(8,128)S(1)} %merge_with_demand.1.own_ref.rest_4_), channel_id=1, source_target_pairs={{0,2},{2,0},{4,6},{6,4},{1,3},{3,1},{5,7},{7,5},{8,10},{10,8},{12,... | collective-permute-start | bytes 344072 | tf_op jit(solution)/shard_map/ppermute | solution.py:352
  39.6 2.9 %collective-permute-start.11 = (f32[80,512]{1,0:T(8,128)S(1)}, f32[80,512]{1,0:T(8,128)S(1)}, u32[]{:S(2)}, u32[]{:S(2)}) collective-permute-start(f32[80,512]{1,0:T(8,128)S(1)} %get-tuple-element.36), channel_id=1, source_target_pairs={{0,1},{1,0},{2,3},{3,2},{4,5},{5,4},{6,7},{7,6},{8,9},{9,8},{10,11... | collective-permute-start | bytes 491528 | tf_op jit(solution)/shard_map/ppermute | solution.py:355
